TPU v7x, 32 devices: a whole 2x2x4 slice. The times are simulated.
32 devices in a mesh: groups: 2 (over x), row: 16 (over z, y, core).
Axes of the slice: x: 2, y: 2, z: 4, core: 2. Of those that a mesh axis runs over, the one named last changes fastest.
Arguments:
- pair_rep: bfloat16 [64, 32, 128], P(('groups', 'row')), parts along dimension 0, may hold values from -6 to 6
- pair_mask: int32 [64, 32], P(('groups', 'row')), parts along dimension 0, may hold values from 0 to 1, as said below
- gain_in: float32 [2, 128], replicated, may hold values from 0.25 to 1.75
- shift_in: float32 [2, 128], replicated, may hold values from -3 to 3
- proj_weight: bfloat16 [2, 128, 512], replicated, may hold values from -0.5 to 0.5
- gate_weight: bfloat16 [2, 128, 128], replicated, may hold values from -0.5 to 0.5
- gain_out: float32 [2, 128], replicated, may hold values from 0.25 to 1.75
- shift_out: float32 [2, 128], replicated, may hold values from -3 to 3
- out_weight: bfloat16 [2, 128, 128], replicated, may hold values from -0.5 to 0.5
Outputs:
- pair_out: bfloat16 [64, 32, 128], P(('groups', 'row')), parts along dimension 0
There are 2 independent parts, one for each index of `groups`. A program takes and returns all parts, laid end to end along the dimension named above; an argument that names none is the same for every part. Nothing has to cross between parts.
Inputs may be any that keep to these rules, and one draw needn't show every extreme that they name: Each token is real or padding on its own, padding with probability one in four; pair_mask[i, j] = 1 exactly when tokens i and j are both real.
All inputs are finite; a program needn't handle non-finite values.
Results may differ from a plain program's by a relative error of at most 0.0095.
Values may be sent and summed in bfloat16 or wider, within the bound.
No kernel may reach another device: no remote copies, remote signals or barrier semaphores. Data moves between devices by JAX's collectives and lax.ppermute only.
A program may use at most 64 MiB of HBM per device.

v0:
```python
import jax
import jax.numpy as jnp
from jax import lax
from jax.sharding import PartitionSpec as P

H = 128


def layer_norm(values, gain, offset, axis):
    mean = jnp.mean(values, axis=axis, keepdims=True)
    centered = values - mean
    variance = jnp.mean(centered * centered, axis=axis, keepdims=True)
    return centered * lax.rsqrt(variance + 1e-05) * gain + offset


def triangle(
    pair_now,
    pair_mask,
    layer_index,
    gain_in,
    shift_in,
    proj_weight,
    gate_weight,
    gain_out,
    shift_out,
    out_weight,
):
    normed = layer_norm(
        pair_now.astype(jnp.float32), gain_in[layer_index], shift_in[layer_index], -1
    ).astype(jnp.bfloat16)
    packed = jnp.einsum(
        "rnc,ch->hrn", normed, proj_weight[layer_index], preferred_element_type=jnp.float32
    )
    masked = pair_mask.astype(jnp.float32)[None, :, :]
    left = (masked * jax.nn.sigmoid(packed[0:H]) * packed[H : 2 * H]).astype(jnp.bfloat16)
    right = (masked * jax.nn.sigmoid(packed[2 * H : 3 * H]) * packed[3 * H :]).astype(jnp.bfloat16)
    gating = jax.nn.sigmoid(
        jnp.einsum(
            "rnc,cd->rnd", normed, gate_weight[layer_index], preferred_element_type=jnp.float32
        )
    )
    lifted_left, lifted_right = (
        lax.all_to_all(left, "row", split_axis=0, concat_axis=1, tiled=True),
        lax.all_to_all(right, "row", split_axis=0, concat_axis=1, tiled=True),
    )
    if layer_index == 0:
        product = jnp.einsum(
            "hik,hjk->hij", lifted_left, lifted_right, preferred_element_type=jnp.float32
        )
    else:
        product = jnp.einsum(
            "hki,hkj->hij", lifted_left, lifted_right, preferred_element_type=jnp.float32
        )
    product = product.astype(jnp.bfloat16)
    out_gain = gain_out[layer_index][:, None, None]
    out_shift = shift_out[layer_index][:, None, None]
    out_proj = out_weight[layer_index]
    returned = lax.all_to_all(product, "row", split_axis=1, concat_axis=0, tiled=True)
    scaled = layer_norm(returned.astype(jnp.float32), out_gain, out_shift, 0).astype(jnp.bfloat16)
    update = jnp.einsum("hrn,hc->rnc", scaled, out_proj, preferred_element_type=jnp.float32)
    return (pair_now.astype(jnp.float32) + gating * update).astype(jnp.bfloat16)


def shards(
    pair_rep,
    pair_mask,
    gain_in,
    shift_in,
    proj_weight,
    gate_weight,
    gain_out,
    shift_out,
    out_weight,
):
    current = pair_rep
    for layer_index in range(2):
        current = triangle(
            current,
            pair_mask,
            layer_index,
            gain_in,
            shift_in,
            proj_weight,
            gate_weight,
            gain_out,
            shift_out,
            out_weight,
        )
    return current


def solution(mesh):
    in_specs = (
        P(("groups", "row"), None, None),
        P(("groups", "row"), None),
        P(),
        P(),
        P(),
        P(),
        P(),
        P(),
        P(),
    )
    out_specs = P(("groups", "row"), None, None)
    return jax.shard_map(shards, mesh=mesh, in_specs=in_specs, out_specs=out_specs, check_vma=False)
```

profile of v0, /device:TPU:0, one launch (start us, length us, event | category | flops | bytes accessed | tf_op | source)
XLA Modules:
  0.0 74.3 jit_solution(13424063652281926590)
XLA Ops:
  0.0 0.9 %convert_reduce_fusion = f32[2,32]{1,0:T(2,128)S(1)} fusion(bf16[2,32,128]{2,1,0:T(8,128)(2,1)} %param.9), kind=kLoop, calls=%fused_computation.47 | loop fusion | flops 16320 | bytes 16640 | tf_op jit(solution)/shard_map/reduce_sum | solution.py:10
  0.9 0.2 fusion.30
  1.1 0.7 copy-done.2
  1.7 0.7 copy-done.3
  2.4 1.1 %convolution_bitcast_fusion.1 = f32[512,2,32]{0,2,1:T(8,128)S(1)} fusion(bf16[2,128,512]{2,1,0:T(8,128)(2,1)} %param.13, bf16[2,32,128]{2,1,0:T(8,128)(2,1)S(1)} %copy-done.1, f32[128]{0:T(128)S(1)} %get-tuple-element.16, f32[128]{0:T(128)S(1)} %get-tuple-element.19, f32[2,32]{1,0:T(2,128)S(1)} %add_rsqrt_fusion.3, f32[2,32]{1,0:T(2,128)S(1)} %broadcast_multiply_fusion.3), kind=kOutput, calls=%fused_computation.1 | convolution fusion | flops 8437760 | bytes 280064 | tf_op jit(solution)/shard_map/rnc,ch->hrn/dot_general | solution.py:31
  3.5 0.1 fusion.44
  3.6 0.1 copy.36
  3.8 0.7 reshape.103
  4.5 7.4 %all-to-all-start.1 = ((bf16[16,2,256]{2,1,0:T(2,128)(2,1)}), bf16[16,2,256]{2,1,0:T(2,128)(2,1)S(1)}, u32[]{:S(2)}, u32[]{:S(2)}) async-start(bf16[16,2,256]{2,1,0:T(2,128)(2,1)} %reshape.103), calls=%async_computation.1 | async-start | bytes 32768 | tf_op jit(solution)/shard_map/all_to_all | solution.py:44
  11.9 0.1 copy.33
  12.0 0.7 reshape.101
  12.7 5.6 %all-to-all-done.1 = bf16[16,2,256]{2,1,0:T(2,128)(2,1)S(1)} async-done(((bf16[16,2,256]{2,1,0:T(2,128)(2,1)}), bf16[16,2,256]{2,1,0:T(2,128)(2,1)S(1)}, u32[]{:S(2)}, u32[]{:S(2)}) %all-to-all-start.1) | async-done | bytes 16416 | tf_op jit(solution)/shard_map/all_to_all | solution.py:44
  18.4 3.5 %all-to-all-start = ((bf16[16,2,256]{2,1,0:T(2,128)(2,1)}), bf16[16,2,256]{2,1,0:T(2,128)(2,1)S(1)}, u32[]{:S(2)}, u32[]{:S(2)}) async-start(bf16[16,2,256]{2,1,0:T(2,128)(2,1)} %reshape.101), calls=%async_computation | async-start | bytes 32768 | tf_op jit(solution)/shard_map/all_to_all | solution.py:43
  21.9 0.2 fusion.7
  22.1 0.1 reshape.104
  22.3 6.0 %all-to-all-done = bf16[16,2,256]{2,1,0:T(2,128)(2,1)S(1)} async-done(((bf16[16,2,256]{2,1,0:T(2,128)(2,1)}), bf16[16,2,256]{2,1,0:T(2,128)(2,1)S(1)}, u32[]{:S(2)}, u32[]{:S(2)}) %all-to-all-start) | async-done | bytes 16416 | tf_op jit(solution)/shard_map/all_to_all | solution.py:43
  28.3 0.1 reshape.102
  28.5 0.2 convolution_convert_fusion.1
  28.7 0.7 reshape.105
  29.4 3.6 %all-to-all-start.2 = ((bf16[16,2,256]{2,1,0:T(2,128)(2,1)}), bf16[16,2,256]{2,1,0:T(2,128)(2,1)S(1)}, u32[]{:S(2)}, u32[]{:S(2)}) async-start(bf16[16,2,256]{2,1,0:T(2,128)(2,1)} %reshape.105), calls=%async_computation.2 | async-start | bytes 32768 | tf_op jit(solution)/shard_map/all_to_all | solution.py:58
  33.1 0.1 add.106
  33.2 0.1 mul.148
  33.3 6.3 %all-to-all-done.2 = bf16[16,2,256]{2,1,0:T(2,128)(2,1)S(1)} async-done(((bf16[16,2,256]{2,1,0:T(2,128)(2,1)}), bf16[16,2,256]{2,1,0:T(2,128)(2,1)S(1)}, u32[]{:S(2)}, u32[]{:S(2)}) %all-to-all-start.2) | async-done | bytes 16416 | tf_op jit(solution)/shard_map/all_to_all | solution.py:58
  39.5 0.1 reshape.106
  39.8 0.7 copy-done.8
  40.5 0.3 fusion.64
  40.8 0.2 multiply_reduce_fusion.2
  41.0 0.2 convolution_bitcast_fusion
  41.2 0.1 fusion.39
  41.3 0.1 copy.42
  41.5 0.7 reshape.109
  42.2 3.5 %all-to-all-start.3 = ((bf16[16,2,256]{2,1,0:T(2,128)(2,1)}), bf16[16,2,256]{2,1,0:T(2,128)(2,1)S(1)}, u32[]{:S(2)}, u32[]{:S(2)}) async-start(bf16[16,2,256]{2,1,0:T(2,128)(2,1)} %reshape.109), calls=%async_computation.3 | async-start | bytes 32768 | tf_op jit(solution)/shard_map/all_to_all | solution.py:43
  45.7 0.1 copy.45
  45.8 0.7 reshape.107
  46.5 5.6 %all-to-all-done.3 = bf16[16,2,256]{2,1,0:T(2,128)(2,1)S(1)} async-done(((bf16[16,2,256]{2,1,0:T(2,128)(2,1)}), bf16[16,2,256]{2,1,0:T(2,128)(2,1)S(1)}, u32[]{:S(2)}, u32[]{:S(2)}) %all-to-all-start.3) | async-done | bytes 16416 | tf_op jit(solution)/shard_map/all_to_all | solution.py:43
  52.1 3.5 %all-to-all-start.4 = ((bf16[16,2,256]{2,1,0:T(2,128)(2,1)}), bf16[16,2,256]{2,1,0:T(2,128)(2,1)S(1)}, u32[]{:S(2)}, u32[]{:S(2)}) async-start(bf16[16,2,256]{2,1,0:T(2,128)(2,1)} %reshape.107), calls=%async_computation.4 | async-start | bytes 32768 | tf_op jit(solution)/shard_map/all_to_all | solution.py:44
  55.6 0.1 add.118
  55.7 0.1 mul.165
  55.8 0.1 reshape.110
  56.0 6.1 %all-to-all-done.4 = bf16[16,2,256]{2,1,0:T(2,128)(2,1)S(1)} async-done(((bf16[16,2,256]{2,1,0:T(2,128)(2,1)}), bf16[16,2,256]{2,1,0:T(2,128)(2,1)S(1)}, u32[]{:S(2)}, u32[]{:S(2)}) %all-to-all-start.4) | async-done | bytes 16416 | tf_op jit(solution)/shard_map/all_to_all | solution.py:44
  62.1 0.1 reshape.108
  62.3 0.2 convolution_convert_fusion
  62.5 0.7 reshape.111
  63.3 3.5 %all-to-all-start.5 = ((bf16[16,2,256]{2,1,0:T(2,128)(2,1)}), bf16[16,2,256]{2,1,0:T(2,128)(2,1)S(1)}, u32[]{:S(2)}, u32[]{:S(2)}) async-start(bf16[16,2,256]{2,1,0:T(2,128)(2,1)} %reshape.111), calls=%async_computation.5 | async-start | bytes 32768 | tf_op jit(solution)/shard_map/all_to_all | solution.py:58
  66.8 0.2 fusion.3
  67.0 6.2 %all-to-all-done.5 = bf16[16,2,256]{2,1,0:T(2,128)(2,1)S(1)} async-done(((bf16[16,2,256]{2,1,0:T(2,128)(2,1)}), bf16[16,2,256]{2,1,0:T(2,128)(2,1)S(1)}, u32[]{:S(2)}, u32[]{:S(2)}) %all-to-all-start.5) | async-done | bytes 16416 | tf_op jit(solution)/shard_map/all_to_all | solution.py:58
  73.2 0.1 reshape.112
  73.4 0.9 %fusion.10 = bf16[2,32,128]{2,1,0:T(8,128)(2,1)} fusion(f32[2,32,128]{2,1,0:T(8,128)S(1)} %get-tuple-element.18, f32[2,32,128]{2,1,0:T(8,128)S(1)} %fusion.3, f32[16,8]{1,0:T(8,128)S(1)} %add.118, f32[16,8]{1,0:T(8,128)S(1)} %mul.165, f32[2,32]{1,0:T(2,128)S(1)} %add_rsqrt_fusion, f32[2,32]{1,0:T(2,128)S(1)} %broadcast_multiply_fusion, ...), kind=kOutput, calls=%fused_computation.18 | convolution fusion | flops 2170880 | bytes 198656 | tf_op jit(solution)/shard_map/hrn,hc->rnc/dot_general | solution.py:60
  (42 shorter events, 0.6 us)
Async XLA Ops:
  0.0 0.9 %copy-start.1 = (bf16[2,32,128]{2,1,0:T(8,128)(2,1)S(1)}, bf16[2,32,128]{2,1,0:T(8,128)(2,1)}, u32[]{:S(2)}) copy-start(bf16[2,32,128]{2,1,0:T(8,128)(2,1)} %param.9) | copy-start | bytes 49156
  1.0 0.7 copy-start.2
  1.7 0.7 copy-start.3
  1.7 0.7 copy-start.4
  4.5 13.9 %all-to-all-start.1 = ((bf16[16,2,256]{2,1,0:T(2,128)(2,1)}), bf16[16,2,256]{2,1,0:T(2,128)(2,1)S(1)}, u32[]{:S(2)}, u32[]{:S(2)}) async-start(bf16[16,2,256]{2,1,0:T(2,128)(2,1)} %reshape.103), calls=%async_computation.1 | async-start | bytes 32768 | tf_op jit(solution)/shard_map/all_to_all | solution.py:44
  12.0 9.9 %copy-start.7 = (bf16[2,128,128]{2,1,0:T(8,128)(2,1)S(1)}, bf16[2,128,128]{2,1,0:T(8,128)(2,1)}, u32[]{:S(2)}) copy-start(bf16[2,128,128]{2,1,0:T(8,128)(2,1)} %param.14) | copy-start | bytes 196612
  18.4 10.0 %all-to-all-start = ((bf16[16,2,256]{2,1,0:T(2,128)(2,1)}), bf16[16,2,256]{2,1,0:T(2,128)(2,1)S(1)}, u32[]{:S(2)}, u32[]{:S(2)}) async-start(bf16[16,2,256]{2,1,0:T(2,128)(2,1)} %reshape.101), calls=%async_computation | async-start | bytes 32768 | tf_op jit(solution)/shard_map/all_to_all | solution.py:43
  29.4 3.6 %copy-start.5 = (f32[2,128]{1,0:T(2,128)S(1)}, f32[2,128]{1,0:T(2,128)}, u32[]{:S(2)}) copy-start(f32[2,128]{1,0:T(2,128)} %param.16) | copy-start | bytes 3076
  29.4 3.6 %copy-start.6 = (f32[2,128]{1,0:T(2,128)S(1)}, f32[2,128]{1,0:T(2,128)}, u32[]{:S(2)}) copy-start(f32[2,128]{1,0:T(2,128)} %param.15) | copy-start | bytes 3076
  29.4 10.1 %all-to-all-start.2 = ((bf16[16,2,256]{2,1,0:T(2,128)(2,1)}), bf16[16,2,256]{2,1,0:T(2,128)(2,1)S(1)}, u32[]{:S(2)}, u32[]{:S(2)}) async-start(bf16[16,2,256]{2,1,0:T(2,128)(2,1)} %reshape.105), calls=%async_computation.2 | async-start | bytes 32768 | tf_op jit(solution)/shard_map/all_to_all | solution.py:58
  39.6 0.8 %copy-start.8 = (bf16[2,128,128]{2,1,0:T(8,128)(2,1)S(1)}, bf16[2,128,128]{2,1,0:T(8,128)(2,1)}, u32[]{:S(2)}) copy-start(bf16[2,128,128]{2,1,0:T(8,128)(2,1)} %param.17) | copy-start | bytes 196612
  39.7 1.3 %copy-start = (bf16[2,128,512]{2,1,0:T(8,128)(2,1)S(1)}, bf16[2,128,512]{2,1,0:T(8,128)(2,1)}, u32[]{:S(2)}) copy-start(bf16[2,128,512]{2,1,0:T(8,128)(2,1)} %param.13) | copy-start | bytes 786436
  42.2 10.0 %all-to-all-start.3 = ((bf16[16,2,256]{2,1,0:T(2,128)(2,1)}), bf16[16,2,256]{2,1,0:T(2,128)(2,1)S(1)}, u32[]{:S(2)}, u32[]{:S(2)}) async-start(bf16[16,2,256]{2,1,0:T(2,128)(2,1)} %reshape.109), calls=%async_computation.3 | async-start | bytes 32768 | tf_op jit(solution)/shard_map/all_to_all | solution.py:43
  52.1 10.0 %all-to-all-start.4 = ((bf16[16,2,256]{2,1,0:T(2,128)(2,1)}), bf16[16,2,256]{2,1,0:T(2,128)(2,1)S(1)}, u32[]{:S(2)}, u32[]{:S(2)}) async-start(bf16[16,2,256]{2,1,0:T(2,128)(2,1)} %reshape.107), calls=%async_computation.4 | async-start | bytes 32768 | tf_op jit(solution)/shard_map/all_to_all | solution.py:44
  63.3 10.0 %all-to-all-start.5 = ((bf16[16,2,256]{2,1,0:T(2,128)(2,1)}), bf16[16,2,256]{2,1,0:T(2,128)(2,1)S(1)}, u32[]{:S(2)}, u32[]{:S(2)}) async-start(bf16[16,2,256]{2,1,0:T(2,128)(2,1)} %reshape.111), calls=%async_computation.5 | async-start | bytes 32768 | tf_op jit(solution)/shard_map/all_to_all | solution.py:58
where the time goes:
time: 74.9 us; the launch traced here: 74.3 us
  waiting for transfers between devices  35.9 us (48%)
  starting transfers between devices  25 us (33%)
  local copies, waits for them, and re-layouts  8.18 us (11%)
  matrix products  3.3 us (4%)
  other arithmetic  1.58 us (2%)
    all_to_all x2, waiting for transfers between devices, triangle(): lax.all_to_all(product, 'row', split_axis=1, concat_axis=0, tiled=True)  12.5 us
    all_to_all x2, waiting for transfers between devices, triangle(): lax.all_to_all(right, 'row', split_axis=0, concat_axis=1, tiled=True)  11.8 us
    all_to_all x2, waiting for transfers between devices, triangle(): lax.all_to_all(left, 'row', split_axis=0, concat_axis=1, tiled=True)  11.6 us
    all_to_all x2, starting transfers between devices, triangle(): lax.all_to_all(right, 'row', split_axis=0, concat_axis=1, tiled=True)  10.9 us
    all_to_all x2, starting transfers between devices, triangle(): lax.all_to_all(product, 'row', split_axis=1, concat_axis=0, tiled=True)  7.12 us
    unnamed x30, local copies, waits for them, and re-layouts  7.01 us
    all_to_all x2, starting transfers between devices, triangle(): lax.all_to_all(left, 'row', split_axis=0, concat_axis=1, tiled=True)  6.99 us
  transfers between devices with their start and end apart: 6, of which 6 were waited for; matrix products, arithmetic and copies ran while one was open for 4% of the time, Pallas kernels for 0%

commit v1 on v0

--- a/solution.py
+++ b/solution.py
@@ -1,7 +1,176 @@
+import functools
+
 import jax
 import jax.numpy as jnp
 from jax import lax
+from jax.experimental import pallas as pl
+from jax.experimental.pallas import tpu as pltpu
 from jax.sharding import PartitionSpec as P
+
+EPS = 1e-05
+MARK_ROWS = 16
+GATHER_LIMIT = 4 << 20
+
+
+def sigmoid(values):
+    return 0.5 * jnp.tanh(0.5 * values) + 0.5
+
+
+def norm_rows(values, gain, offset):
+    mean = jnp.mean(values, axis=-1, keepdims=True)
+    centered = values - mean
+    variance = jnp.mean(centered * centered, axis=-1, keepdims=True)
+    return (centered * lax.rsqrt(variance + EPS) * gain + offset).astype(jnp.bfloat16)
+
+
+def matmul(left, right):
+    return jnp.dot(left, right, preferred_element_type=jnp.float32)
+
+
+def gated(mask, packed, width):
+    value = mask * sigmoid(packed[:, :width]) * packed[:, width:]
+    return value.astype(jnp.bfloat16).astype(jnp.float32)
+
+
+def updates_kernel(
+    n_row,
+    order,
+    me_ref,
+    own_ref,
+    other_ref,
+    gain_in,
+    shift_in,
+    proj_weight,
+    gate_weight,
+    gain_out,
+    shift_out,
+    out_weight,
+    out_ref,
+    pair,
+    valid,
+    left0,
+    right0,
+    gate0,
+    middle,
+    right1,
+):
+    me = me_ref[0]
+    half, block_rows, width = own_ref.shape
+    tokens = valid.shape[0]
+    per = tokens // n_row
+    rows = per * tokens
+
+    for half_index, ref in enumerate((own_ref, other_ref)):
+        for slot, step in enumerate(order):
+            at = me ^ (step ^ half_index)
+            pair[pl.ds(pl.multiple_of(at * rows, rows), rows), :] = ref[slot, 0:rows, :]
+            marks = ref[slot, rows:block_rows, :].astype(jnp.float32)
+            valid[pl.ds(at * per, per), :] = marks[0:per]
+
+    step_i = 8
+    chunk = step_i * tokens
+
+    def project(i, _):
+        at = pl.ds(pl.multiple_of(i * chunk, chunk), chunk)
+        normed = norm_rows(pair[at, :].astype(jnp.float32), gain_in[0:1, :], shift_in[0:1, :])
+        rowmask = valid[pl.ds(i * step_i, step_i), :]
+        mask = (rowmask[:, None, :] * valid[...][None, :, :]).reshape(chunk, width)
+        packed = matmul(normed, proj_weight[0])
+        left0[at, :] = gated(mask, packed[:, 0 : 2 * width], width)
+        right0[at, :] = gated(mask, packed[:, 2 * width :], width)
+        gate0[at, :] = sigmoid(matmul(normed, gate_weight[0]))
+        return 0
+
+    lax.fori_loop(0, tokens // step_i, project, 0)
+
+    for k in range(tokens):
+        right1[k * tokens : (k + 1) * tokens, :] = right0[pl.ds(k, tokens, stride=tokens), :]
+
+    def update(i, _):
+        base = pl.multiple_of(i * chunk, chunk)
+        at = pl.ds(base, chunk)
+        totals = [jnp.zeros((tokens, width), jnp.float32)] * step_i
+        for k in range(tokens):
+            row = right1[k * tokens : (k + 1) * tokens, :]
+            for r in range(step_i):
+                totals[r] = totals[r] + left0[pl.ds(base + (r * tokens + k), 1), :] * row
+        product = jnp.concatenate(totals, axis=0).astype(jnp.bfloat16).astype(jnp.float32)
+        scaled = norm_rows(product, gain_out[0:1, :], shift_out[0:1, :])
+        moved = pair[at, :].astype(jnp.float32) + gate0[at, :] * matmul(scaled, out_weight[0])
+        middle[at, :] = moved.astype(jnp.bfloat16).astype(jnp.float32)
+        return 0
+
+    lax.fori_loop(0, tokens // step_i, update, 0)
+
+    def project_last(i, _):
+        at = pl.ds(pl.multiple_of(i * chunk, chunk), chunk)
+        normed = norm_rows(middle[at, :], gain_in[1:2, :], shift_in[1:2, :])
+        rowmask = valid[pl.ds(i * step_i, step_i), :]
+        mask = (rowmask[:, None, :] * valid[...][None, :, :]).reshape(chunk, width)
+        right0[at, :] = gated(mask, matmul(normed, proj_weight[1, :, 2 * width :]), width)
+        return 0
+
+    lax.fori_loop(0, tokens // step_i, project_last, 0)
+
+    first = me * per
+    columns = jnp.concatenate([middle[pl.ds(first + r, tokens, stride=tokens), :] for r in range(per)], axis=0)
+    normed = norm_rows(columns, gain_in[1:2, :], shift_in[1:2, :])
+    mask = jnp.concatenate([valid[...] * valid[pl.ds(first + r, 1), :] for r in range(per)], axis=0)
+    left0[0:rows, :] = gated(mask, matmul(normed, proj_weight[1, :, 0 : 2 * width]), width)
+    totals = [jnp.zeros((tokens, width), jnp.float32)] * per
+    for k in range(tokens):
+        row = right0[k * tokens : (k + 1) * tokens, :]
+        for r in range(per):
+            totals[r] = totals[r] + left0[r * tokens + k : r * tokens + k + 1, :] * row
+    product = jnp.concatenate(totals, axis=0).astype(jnp.bfloat16).astype(jnp.float32)
+    scaled = norm_rows(product, gain_out[1:2, :], shift_out[1:2, :])
+    held = middle[pl.ds(pl.multiple_of(first * tokens, rows), rows), :]
+    gate = sigmoid(matmul(norm_rows(held, gain_in[1:2, :], shift_in[1:2, :]), gate_weight[1]))
+    out_ref[...] = (held + gate * matmul(scaled, out_weight[1])).astype(jnp.bfloat16)
+
+
+def updates(n_row, order, tokens, me, own, other, params):
+    width = own.shape[-1]
+    rows = tokens * tokens // n_row
+    pairs = tokens * tokens
+    vmem = pl.BlockSpec(memory_space=pltpu.VMEM)
+    return pl.pallas_call(
+        functools.partial(updates_kernel, n_row, order),
+        out_shape=jax.ShapeDtypeStruct((rows, width), jnp.bfloat16),
+        in_specs=[pl.BlockSpec(memory_space=pltpu.SMEM)] + [vmem] * 9,
+        out_specs=vmem,
+        scratch_shapes=[
+            pltpu.VMEM((pairs, width), jnp.bfloat16),
+            pltpu.VMEM((tokens, width), jnp.float32),
+        ]
+        + [pltpu.VMEM((pairs, width), jnp.float32)] * 5,
+        compiler_params=pltpu.CompilerParams(vmem_limit_bytes=24 << 20),
+    )(me, own, other, *params)
+
+
+def swap(values, step, n_row):
+    return lax.ppermute(values, "row", [(i, i ^ step) for i in range(n_row)])
+
+
+def gathered(n_row, pair_rep, pair_mask, *params):
+    per, tokens, width = pair_rep.shape
+    rows = per * tokens
+    me = lax.axis_index("row")
+    first = me * per
+    diagonal = [lax.dynamic_slice(pair_mask, (r, first + r), (1, 1)) for r in range(per)]
+    marks = jnp.concatenate(diagonal, axis=0).astype(jnp.bfloat16)
+    marks = jnp.pad(jnp.broadcast_to(marks, (per, width)), ((0, MARK_ROWS - per), (0, 0)))
+    held = jnp.concatenate([pair_rep.reshape(rows, width), marks], axis=0)[None]
+    order = [0]
+    step = n_row // 2
+    while step > 1:
+        held = jnp.concatenate([held, swap(held, step, n_row)], axis=0)
+        order = order + [s ^ step for s in order]
+        step //= 2
+    other = swap(held, 1, n_row)
+    out = updates(n_row, tuple(order), tokens, me.astype(jnp.int32).reshape(1), held, other, params)
+    return out.reshape(per, tokens, width)
+
 
 H = 128
 
@@ -61,7 +230,7 @@
     return (pair_now.astype(jnp.float32) + gating * update).astype(jnp.bfloat16)
 
 
-def shards(
+def exchanged(
     pair_rep,
     pair_mask,
     gain_in,
@@ -90,6 +259,16 @@
 
 
 def solution(mesh):
+    n_row = mesh.shape["row"]
+
+    def shards(pair_rep, *rest):
+        per, tokens, _ = pair_rep.shape
+        small = pair_rep.size * n_row * 2 <= GATHER_LIMIT
+        fits = n_row & (n_row - 1) == 0 and n_row > 1 and tokens % 8 == 0 and per <= MARK_ROWS
+        if small and fits:
+            return gathered(n_row, pair_rep, *rest)
+        return exchanged(pair_rep, *rest)
+
     in_specs = (
         P(("groups", "row"), None, None),
         P(("groups", "row"), None),

time: 74.9 us -> 26 us (0.35)
  waiting for transfers between devices: 35.9 us -> 7.77 us
  starting transfers between devices: 25 us -> 8.09 us
  Pallas kernels: 0 us -> 6.94 us
  local copies, waits for them, and re-layouts: 8.18 us -> 1.44 us
  matrix products: 3.3 us -> 0 us
  other arithmetic: 1.58 us -> 0.19 us
  between operations: 0.34 us -> 1.37 us
    all_to_all x6 -> x0, waiting for transfers between devices: 35.9 us -> none  [the longest x2 12.5 us: triangle(): lax.all_to_all(product, 'row', split_axis=1, concat_axis=0, tiled=True)]
    all_to_all x6 -> x0, starting transfers between devices: 25 us -> none  [the longest x2 10.9 us: triangle(): lax.all_to_all(right, 'row', split_axis=0, concat_axis=1, tiled=True)]
    ppermute x0 -> x4, starting transfers between devices: none -> 8.09 us  [swap(): return lax.ppermute(values, 'row', [(i, i ^ step) for i in range(n_row)])]
    ppermute x0 -> x4, waiting for transfers between devices: none -> 7.77 us  [swap(): return lax.ppermute(values, 'row', [(i, i ^ step) for i in range(n_row)])]
    pallas_call x0 -> x1, Pallas kernels: none -> 6.94 us  [updates(): pl.pallas_call(functools.partial(updates_kernel, n_row, order), out_shape...]
    unnamed x30 -> x18, local copies, waits for them, and re-layouts: 7.01 us -> 0.71 us
    dot_general x8 -> x0, matrix products: 3.3 us -> none  [the longest x2 1.31 us: triangle(): jnp.einsum('rnc,ch->hrn', normed, proj_weight[layer_index], preferred_ele...]
    reduce_sum x7 -> x0, other arithmetic: 1.33 us -> none  [the longest x3 0.94 us: layer_norm(): mean = jnp.mean(values, axis=axis, keepdims=True)]
  transfers between devices with their start and end apart: 6 -> 4, of which waited for: 6 -> 4; matrix products, arithmetic and copies ran while one was open for 4% -> 0% of each run, Pallas kernels for 0% -> 0%
where the time goes in v1:
time: 26 us; the launch traced here: 25.8 us
  starting transfers between devices  8.09 us (31%)
  waiting for transfers between devices  7.77 us (30%)
  Pallas kernels  6.94 us (27%)
  local copies, waits for them, and re-layouts  1.44 us (6%)
  between operations  1.37 us (5%)
    ppermute x4, starting transfers between devices, swap(): return lax.ppermute(values, 'row', [(i, i ^ step) for i in range(n_row)])  8.09 us
    ppermute x4, waiting for transfers between devices, swap(): return lax.ppermute(values, 'row', [(i, i ^ step) for i in range(n_row)])  7.77 us
    pallas_call x1, Pallas kernels, updates(): pl.pallas_call(functools.partial(updates_kernel, n_row, order), out_shape...  6.94 us
    unnamed x18, local copies, waits for them, and re-layouts  0.71 us
    dynamic_slice x1, local copies, waits for them, and re-layouts, gathered(): lax.dynamic_slice(pair_mask, (r, first + r), (1, 1))  0.65 us
  transfers between devices with their start and end apart: 4, of which 4 were waited for; matrix products, arithmetic and copies ran while one was open for 0% of the time, Pallas kernels for 0%

profile of v1, /device:TPU:0, one launch (start us, length us, event | category | flops | bytes accessed | tf_op | source)
XLA Modules:
  0.0 25.8 jit_solution(1919870249023641646)
XLA Ops:
  0.0 0.0 copy-start.8
  0.0 0.0 copy-start.7
  0.0 0.7 %copy-done.8 = s32[2,32]{1,0:T(2,128)S(1)} copy-done((s32[2,32]{1,0:T(2,128)S(1)}, s32[2,32]{1,0:T(2,128)}, u32[]{:S(2)}) %copy-start.8) | copy-done | bytes 280
  0.7 0.6 %constant_dynamic-slice_fusion.1 = (s32[1,1]{1,0:T(1,128)}, s32[1,1]{1,0:T(1,128)}) fusion(s32[2,32]{1,0:T(2,128)S(1)} %copy-done.8, s32[]{:T(128)S(6)} %select_n.6, s32[]{:T(128)S(6)} %select_n.7), kind=kLoop, calls=%fused_computation.8 | loop fusion | bytes 24 | tf_op jit(solution)/shard_map/dynamic_slice | solution.py:160
  2.6 0.1 fusion
  2.7 0.1 pad.18.clone
  2.8 0.0 copy-done.7
  2.8 0.1 maximum_bitcast_fusion
  2.8 4.1 %collective-permute-start = (bf16[1,80,128]{2,1,0:T(8,128)(2,1)S(1)}, bf16[1,80,128]{2,1,0:T(8,128)(2,1)S(1)}, u32[]{:S(2)}, u32[]{:S(2)}) collective-permute-start(bf16[1,80,128]{2,1,0:T(8,128)(2,1)S(1)} %maximum_bitcast_fusion), channel_id=1, source_target_pairs={{0,8},{1,9},{2,10},{3,11},{4,12},{5,13},{6,14},{7,15},{8,0},{9,1},... | collective-permute-start | bytes 61448 | tf_op jit(solution)/shard_map/ppermute | solution.py:152
  6.9 1.8 %collective-permute-done = bf16[1,80,128]{2,1,0:T(8,128)(2,1)S(1)} collective-permute-done((bf16[1,80,128]{2,1,0:T(8,128)(2,1)S(1)}, bf16[1,80,128]{2,1,0:T(8,128)(2,1)S(1)}, u32[]{:S(2)}, u32[]{:S(2)}) %collective-permute-start) | collective-permute-done | bytes 20512 | tf_op jit(solution)/shard_map/ppermute | solution.py:152
  8.7 0.0 copy-start
  8.7 2.0 %collective-permute-start.1 = (bf16[2,80,128]{2,1,0:T(8,128)(2,1)S(1)}, bf16[2,80,128]{2,1,0:T(8,128)(2,1)S(1)}, u32[]{:S(2)}, u32[]{:S(2)}) collective-permute-start(bf16[2,80,128]{2,1,0:T(8,128)(2,1)S(1)} %pad_maximum_fusion.2), channel_id=1, source_target_pairs={{0,4},{1,5},{2,6},{3,7},{4,0},{5,1},{6,2},{7,3},{8,12},{9,13},{10,... | collective-permute-start | bytes 122888 | tf_op jit(solution)/shard_map/ppermute | solution.py:152
  10.6 2.1 %collective-permute-done.1 = bf16[2,80,128]{2,1,0:T(8,128)(2,1)S(1)} collective-permute-done((bf16[2,80,128]{2,1,0:T(8,128)(2,1)S(1)}, bf16[2,80,128]{2,1,0:T(8,128)(2,1)S(1)}, u32[]{:S(2)}, u32[]{:S(2)}) %collective-permute-start.1) | collective-permute-done | bytes 40992 | tf_op jit(solution)/shard_map/ppermute | solution.py:152
  12.8 0.0 copy-start.1
  12.8 0.0 copy-start.2
  12.8 2.0 %collective-permute-start.2 = (bf16[4,80,128]{2,1,0:T(8,128)(2,1)S(1)}, bf16[4,80,128]{2,1,0:T(8,128)(2,1)S(1)}, u32[]{:S(2)}, u32[]{:S(2)}) collective-permute-start(bf16[4,80,128]{2,1,0:T(8,128)(2,1)S(1)} %pad_maximum_fusion.1), channel_id=1, source_target_pairs={{0,2},{1,3},{2,0},{3,1},{4,6},{5,7},{6,4},{7,5},{8,10},{9,11},{10,... | collective-permute-start | bytes 245768 | tf_op jit(solution)/shard_map/ppermute | solution.py:152
  14.8 2.5 %collective-permute-done.2 = bf16[4,80,128]{2,1,0:T(8,128)(2,1)S(1)} collective-permute-done((bf16[4,80,128]{2,1,0:T(8,128)(2,1)S(1)}, bf16[4,80,128]{2,1,0:T(8,128)(2,1)S(1)}, u32[]{:S(2)}, u32[]{:S(2)}) %collective-permute-start.2) | collective-permute-done | bytes 81952 | tf_op jit(solution)/shard_map/ppermute | solution.py:152
  17.3 0.0 copy-start.4
  17.3 0.0 copy-start.5
  17.3 0.0 copy-start.6
  17.3 0.0 copy-start.3
  17.3 0.1 collective-permute-start.3
  17.4 1.4 %collective-permute-done.3.other_ref = bf16[8,80,128]{2,1,0:T(8,128)(2,1)S(1)} collective-permute-done((bf16[8,80,128]{2,1,0:T(8,128)(2,1)S(1)}, bf16[8,80,128]{2,1,0:T(8,128)(2,1)S(1)}, u32[]{:S(2)}, u32[]{:S(2)}) %collective-permute-start.3) | collective-permute-done | bytes 163872 | tf_op jit(solution)/shard_map/ppermute | solution.py:152
  18.8 0.0 copy-done
  18.8 0.0 copy-done.1
  18.8 0.0 copy-done.2
  18.8 0.0 copy-done.4
  18.8 0.0 copy-done.5
  18.8 0.0 copy-done.6
  18.8 0.0 copy-done.3
  18.9 6.9 %shard_map.91 = bf16[64,128]{1,0:T(8,128)(2,1)} custom-call(s32[1]{0:T(128)} %bitcast.me_ref, bf16[8,80,128]{2,1,0:T(8,128)(2,1)S(1)} %pad_maximum_fusion.own_ref, bf16[8,80,128]{2,1,0:T(8,128)(2,1)S(1)} %collective-permute-done.3.other_ref, f32[2,128]{1,0:T(2,128)S(1)} %copy-done.3, f32[2,128]{1,0:T(2,128)S(1)} %copy-done.4, ...), custom_call_target="tpu_custom_call" | custom-call | tf_op jit(solution)/shard_map/pallas_call | solution.py:137
  (3 shorter events, 0.0 us)
Async XLA Ops:
  0.0 0.7 %copy-start.8 = (s32[2,32]{1,0:T(2,128)S(1)}, s32[2,32]{1,0:T(2,128)}, u32[]{:S(2)}) copy-start(s32[2,32]{1,0:T(2,128)} %param.10) | copy-start | bytes 772
  0.0 2.8 %copy-start.7 = (bf16[2,32,128]{2,1,0:T(8,128)(2,1)S(1)}, bf16[2,32,128]{2,1,0:T(8,128)(2,1)}, u32[]{:S(2)}) copy-start(bf16[2,32,128]{2,1,0:T(8,128)(2,1)} %param.9) | copy-start | bytes 49156
  2.8 5.8 %collective-permute-start = (bf16[1,80,128]{2,1,0:T(8,128)(2,1)S(1)}, bf16[1,80,128]{2,1,0:T(8,128)(2,1)S(1)}, u32[]{:S(2)}, u32[]{:S(2)}) collective-permute-start(bf16[1,80,128]{2,1,0:T(8,128)(2,1)S(1)} %maximum_bitcast_fusion), channel_id=1, source_target_pairs={{0,8},{1,9},{2,10},{3,11},{4,12},{5,13},{6,14},{7,15},{8,0},{9,1},... | collective-permute-start | bytes 61448 | tf_op jit(solution)/shard_map/ppermute | solution.py:152
  8.7 10.1 %copy-start = (bf16[2,128,512]{2,1,0:T(8,128)(2,1)S(1)}, bf16[2,128,512]{2,1,0:T(8,128)(2,1)}, u32[]{:S(2)}) copy-start(bf16[2,128,512]{2,1,0:T(8,128)(2,1)} %proj_weight.1) | copy-start | bytes 786436
  8.7 4.1 %collective-permute-start.1 = (bf16[2,80,128]{2,1,0:T(8,128)(2,1)S(1)}, bf16[2,80,128]{2,1,0:T(8,128)(2,1)S(1)}, u32[]{:S(2)}, u32[]{:S(2)}) collective-permute-start(bf16[2,80,128]{2,1,0:T(8,128)(2,1)S(1)} %pad_maximum_fusion.2), channel_id=1, source_target_pairs={{0,4},{1,5},{2,6},{3,7},{4,0},{5,1},{6,2},{7,3},{8,12},{9,13},{10,... | collective-permute-start | bytes 122888 | tf_op jit(solution)/shard_map/ppermute | solution.py:152
  12.8 6.0 %copy-start.1 = (bf16[2,128,128]{2,1,0:T(8,128)(2,1)S(1)}, bf16[2,128,128]{2,1,0:T(8,128)(2,1)}, u32[]{:S(2)}) copy-start(bf16[2,128,128]{2,1,0:T(8,128)(2,1)} %gate_weight.1) | copy-start | bytes 196612
  12.8 6.0 %copy-start.2 = (bf16[2,128,128]{2,1,0:T(8,128)(2,1)S(1)}, bf16[2,128,128]{2,1,0:T(8,128)(2,1)}, u32[]{:S(2)}) copy-start(bf16[2,128,128]{2,1,0:T(8,128)(2,1)} %out_weight.1) | copy-start | bytes 196612
  12.8 4.5 %collective-permute-start.2 = (bf16[4,80,128]{2,1,0:T(8,128)(2,1)S(1)}, bf16[4,80,128]{2,1,0:T(8,128)(2,1)S(1)}, u32[]{:S(2)}, u32[]{:S(2)}) collective-permute-start(bf16[4,80,128]{2,1,0:T(8,128)(2,1)S(1)} %pad_maximum_fusion.1), channel_id=1, source_target_pairs={{0,2},{1,3},{2,0},{3,1},{4,6},{5,7},{6,4},{7,5},{8,10},{9,11},{10,... | collective-permute-start | bytes 245768 | tf_op jit(solution)/shard_map/ppermute | solution.py:152
  17.3 1.5 %copy-start.4 = (f32[2,128]{1,0:T(2,128)S(1)}, f32[2,128]{1,0:T(2,128)}, u32[]{:S(2)}) copy-start(f32[2,128]{1,0:T(2,128)} %shift_in.1) | copy-start | bytes 3076
  17.3 1.5 %copy-start.5 = (f32[2,128]{1,0:T(2,128)S(1)}, f32[2,128]{1,0:T(2,128)}, u32[]{:S(2)}) copy-start(f32[2,128]{1,0:T(2,128)} %gain_out.1) | copy-start | bytes 3076
  17.3 1.5 %copy-start.6 = (f32[2,128]{1,0:T(2,128)S(1)}, f32[2,128]{1,0:T(2,128)}, u32[]{:S(2)}) copy-start(f32[2,128]{1,0:T(2,128)} %shift_out.1) | copy-start | bytes 3076
  17.3 1.5 %copy-start.3 = (f32[2,128]{1,0:T(2,128)S(1)}, f32[2,128]{1,0:T(2,128)}, u32[]{:S(2)}) copy-start(f32[2,128]{1,0:T(2,128)} %gain_in.1) | copy-start | bytes 3076
  17.3 1.5 %collective-permute-start.3 = (bf16[8,80,128]{2,1,0:T(8,128)(2,1)S(1)}, bf16[8,80,128]{2,1,0:T(8,128)(2,1)S(1)}, u32[]{:S(2)}, u32[]{:S(2)}) collective-permute-start(bf16[8,80,128]{2,1,0:T(8,128)(2,1)S(1)} %pad_maximum_fusion.own_ref), channel_id=1, source_target_pairs={{0,1},{1,0},{2,3},{3,2},{4,5},{5,4},{6,7},{7,6},{8,9},{9,8},{10,11... | collective-permute-start | bytes 491528 | tf_op jit(solution)/shard_map/ppermute | solution.py:152

commit v2 on v1

--- a/solution.py
+++ b/solution.py
@@ -68,6 +68,7 @@
             valid[pl.ds(at * per, per), :] = marks[0:per]
 
     step_i = 8
+    pitch = tokens + 8
     chunk = step_i * tokens
 
     def project(i, _):
@@ -77,14 +78,16 @@
         mask = (rowmask[:, None, :] * valid[...][None, :, :]).reshape(chunk, width)
         packed = matmul(normed, proj_weight[0])
         left0[at, :] = gated(mask, packed[:, 0 : 2 * width], width)
-        right0[at, :] = gated(mask, packed[:, 2 * width :], width)
+        right = gated(mask, packed[:, 2 * width :], width)
+        for r in range(step_i):
+            right0[pl.ds((i * step_i + r) * pitch, tokens), :] = right[r * tokens : (r + 1) * tokens, :]
         gate0[at, :] = sigmoid(matmul(normed, gate_weight[0]))
         return 0
 
-    lax.fori_loop(0, tokens // step_i, project, 0)
+    lax.fori_loop(0, tokens // step_i, project, 0, unroll=True)
 
     for k in range(tokens):
-        right1[k * tokens : (k + 1) * tokens, :] = right0[pl.ds(k, tokens, stride=tokens), :]
+        right1[k * tokens : (k + 1) * tokens, :] = right0[pl.ds(k, tokens, stride=pitch), :]
 
     def update(i, _):
         base = pl.multiple_of(i * chunk, chunk)
@@ -100,7 +103,7 @@
         middle[at, :] = moved.astype(jnp.bfloat16).astype(jnp.float32)
         return 0
 
-    lax.fori_loop(0, tokens // step_i, update, 0)
+    lax.fori_loop(0, tokens // step_i, update, 0, unroll=True)
 
     def project_last(i, _):
         at = pl.ds(pl.multiple_of(i * chunk, chunk), chunk)
@@ -110,7 +113,7 @@
         right0[at, :] = gated(mask, matmul(normed, proj_weight[1, :, 2 * width :]), width)
         return 0
 
-    lax.fori_loop(0, tokens // step_i, project_last, 0)
+    lax.fori_loop(0, tokens // step_i, project_last, 0, unroll=True)
 
     first = me * per
     columns = jnp.concatenate([middle[pl.ds(first + r, tokens, stride=tokens), :] for r in range(per)], axis=0)
@@ -143,7 +146,7 @@
             pltpu.VMEM((pairs, width), jnp.bfloat16),
             pltpu.VMEM((tokens, width), jnp.float32),
         ]
-        + [pltpu.VMEM((pairs, width), jnp.float32)] * 5,
+        + [pltpu.VMEM((pairs + 8 * tokens, width), jnp.float32)] * 5,
         compiler_params=pltpu.CompilerParams(vmem_limit_bytes=24 << 20),
     )(me, own, other, *params)
 

time: 26 us -> 23.2 us (0.89)
  Pallas kernels: 6.94 us -> 4.13 us
    pallas_call x1, Pallas kernels: 6.94 us -> 4.13 us  [updates(): pl.pallas_call(functools.partial(updates_kernel, n_row, order), out_shape...]
where the time goes in v2:
time: 23.2 us; the launch traced here: 23 us
  starting transfers between devices  8.09 us (35%)
  waiting for transfers between devices  7.77 us (33%)
  Pallas kernels  4.13 us (18%)
  local copies, waits for them, and re-layouts  1.44 us (6%)
  between operations  1.37 us (6%)
    ppermute x4, starting transfers between devices, swap(): return lax.ppermute(values, 'row', [(i, i ^ step) for i in range(n_row)])  8.09 us
    ppermute x4, waiting for transfers between devices, swap(): return lax.ppermute(values, 'row', [(i, i ^ step) for i in range(n_row)])  7.77 us
    pallas_call x1, Pallas kernels, updates(): pl.pallas_call(functools.partial(updates_kernel, n_row, order), out_shape...  4.13 us
    unnamed x18, local copies, waits for them, and re-layouts  0.71 us
    dynamic_slice x1, local copies, waits for them, and re-layouts, gathered(): lax.dynamic_slice(pair_mask, (r, first + r), (1, 1))  0.65 us
  transfers between devices with their start and end apart: 4, of which 4 were waited for; matrix products, arithmetic and copies ran while one was open for 0% of the time, Pallas kernels for 0%

profile of v2, /device:TPU:0, one launch (start us, length us, event | category | flops | bytes accessed | tf_op | source)
XLA Modules:
  0.0 23.0 jit_solution(1688420031495180441)
XLA Ops:
  0.0 0.0 copy-start.8
  0.0 0.0 copy-start.7
  0.0 0.7 %copy-done.8 = s32[2,32]{1,0:T(2,128)S(1)} copy-done((s32[2,32]{1,0:T(2,128)S(1)}, s32[2,32]{1,0:T(2,128)}, u32[]{:S(2)}) %copy-start.8) | copy-done | bytes 280
  0.7 0.6 %constant_dynamic-slice_fusion.1 = (s32[1,1]{1,0:T(1,128)}, s32[1,1]{1,0:T(1,128)}) fusion(s32[2,32]{1,0:T(2,128)S(1)} %copy-done.8, s32[]{:T(128)S(6)} %select_n.6, s32[]{:T(128)S(6)} %select_n.7), kind=kLoop, calls=%fused_computation.8 | loop fusion | bytes 24 | tf_op jit(solution)/shard_map/dynamic_slice | solution.py:163
  2.6 0.1 fusion
  2.7 0.1 pad.18.clone
  2.8 0.0 copy-done.7
  2.8 0.1 maximum_bitcast_fusion
  2.8 4.1 %collective-permute-start = (bf16[1,80,128]{2,1,0:T(8,128)(2,1)S(1)}, bf16[1,80,128]{2,1,0:T(8,128)(2,1)S(1)}, u32[]{:S(2)}, u32[]{:S(2)}) collective-permute-start(bf16[1,80,128]{2,1,0:T(8,128)(2,1)S(1)} %maximum_bitcast_fusion), channel_id=1, source_target_pairs={{0,8},{1,9},{2,10},{3,11},{4,12},{5,13},{6,14},{7,15},{8,0},{9,1},... | collective-permute-start | bytes 61448 | tf_op jit(solution)/shard_map/ppermute | solution.py:155
  6.9 1.8 %collective-permute-done = bf16[1,80,128]{2,1,0:T(8,128)(2,1)S(1)} collective-permute-done((bf16[1,80,128]{2,1,0:T(8,128)(2,1)S(1)}, bf16[1,80,128]{2,1,0:T(8,128)(2,1)S(1)}, u32[]{:S(2)}, u32[]{:S(2)}) %collective-permute-start) | collective-permute-done | bytes 20512 | tf_op jit(solution)/shard_map/ppermute | solution.py:155
  8.7 0.0 copy-start
  8.7 2.0 %collective-permute-start.1 = (bf16[2,80,128]{2,1,0:T(8,128)(2,1)S(1)}, bf16[2,80,128]{2,1,0:T(8,128)(2,1)S(1)}, u32[]{:S(2)}, u32[]{:S(2)}) collective-permute-start(bf16[2,80,128]{2,1,0:T(8,128)(2,1)S(1)} %pad_maximum_fusion.2), channel_id=1, source_target_pairs={{0,4},{1,5},{2,6},{3,7},{4,0},{5,1},{6,2},{7,3},{8,12},{9,13},{10,... | collective-permute-start | bytes 122888 | tf_op jit(solution)/shard_map/ppermute | solution.py:155
  10.6 2.1 %collective-permute-done.1 = bf16[2,80,128]{2,1,0:T(8,128)(2,1)S(1)} collective-permute-done((bf16[2,80,128]{2,1,0:T(8,128)(2,1)S(1)}, bf16[2,80,128]{2,1,0:T(8,128)(2,1)S(1)}, u32[]{:S(2)}, u32[]{:S(2)}) %collective-permute-start.1) | collective-permute-done | bytes 40992 | tf_op jit(solution)/shard_map/ppermute | solution.py:155
  12.8 0.0 copy-start.1
  12.8 0.0 copy-start.2
  12.8 2.0 %collective-permute-start.2 = (bf16[4,80,128]{2,1,0:T(8,128)(2,1)S(1)}, bf16[4,80,128]{2,1,0:T(8,128)(2,1)S(1)}, u32[]{:S(2)}, u32[]{:S(2)}) collective-permute-start(bf16[4,80,128]{2,1,0:T(8,128)(2,1)S(1)} %pad_maximum_fusion.1), channel_id=1, source_target_pairs={{0,2},{1,3},{2,0},{3,1},{4,6},{5,7},{6,4},{7,5},{8,10},{9,11},{10,... | collective-permute-start | bytes 245768 | tf_op jit(solution)/shard_map/ppermute | solution.py:155
  14.8 2.5 %collective-permute-done.2 = bf16[4,80,128]{2,1,0:T(8,128)(2,1)S(1)} collective-permute-done((bf16[4,80,128]{2,1,0:T(8,128)(2,1)S(1)}, bf16[4,80,128]{2,1,0:T(8,128)(2,1)S(1)}, u32[]{:S(2)}, u32[]{:S(2)}) %collective-permute-start.2) | collective-permute-done | bytes 81952 | tf_op jit(solution)/shard_map/ppermute | solution.py:155
  17.3 0.0 copy-start.4
  17.3 0.0 copy-start.5
  17.3 0.0 copy-start.6
  17.3 0.0 copy-start.3
  17.3 0.1 collective-permute-start.3
  17.4 1.4 %collective-permute-done.3.other_ref = bf16[8,80,128]{2,1,0:T(8,128)(2,1)S(1)} collective-permute-done((bf16[8,80,128]{2,1,0:T(8,128)(2,1)S(1)}, bf16[8,80,128]{2,1,0:T(8,128)(2,1)S(1)}, u32[]{:S(2)}, u32[]{:S(2)}) %collective-permute-start.3) | collective-permute-done | bytes 163872 | tf_op jit(solution)/shard_map/ppermute | solution.py:155
  18.8 0.0 copy-done
  18.8 0.0 copy-done.1
  18.8 0.0 copy-done.2
  18.8 0.0 copy-done.4
  18.8 0.0 copy-done.5
  18.8 0.0 copy-done.6
  18.8 0.0 copy-done.3
  18.9 4.1 %shard_map.91 = bf16[64,128]{1,0:T(8,128)(2,1)} custom-call(s32[1]{0:T(128)} %bitcast.me_ref, bf16[8,80,128]{2,1,0:T(8,128)(2,1)S(1)} %pad_maximum_fusion.own_ref, bf16[8,80,128]{2,1,0:T(8,128)(2,1)S(1)} %collective-permute-done.3.other_ref, f32[2,128]{1,0:T(2,128)S(1)} %copy-done.3, f32[2,128]{1,0:T(2,128)S(1)} %copy-done.4, ...), custom_call_target="tpu_custom_call" | custom-call | tf_op jit(solution)/shard_map/pallas_call | solution.py:140
  (3 shorter events, 0.0 us)
Async XLA Ops:
  0.0 0.7 %copy-start.8 = (s32[2,32]{1,0:T(2,128)S(1)}, s32[2,32]{1,0:T(2,128)}, u32[]{:S(2)}) copy-start(s32[2,32]{1,0:T(2,128)} %param.10) | copy-start | bytes 772
  0.0 2.8 %copy-start.7 = (bf16[2,32,128]{2,1,0:T(8,128)(2,1)S(1)}, bf16[2,32,128]{2,1,0:T(8,128)(2,1)}, u32[]{:S(2)}) copy-start(bf16[2,32,128]{2,1,0:T(8,128)(2,1)} %param.9) | copy-start | bytes 49156
  2.8 5.8 %collective-permute-start = (bf16[1,80,128]{2,1,0:T(8,128)(2,1)S(1)}, bf16[1,80,128]{2,1,0:T(8,128)(2,1)S(1)}, u32[]{:S(2)}, u32[]{:S(2)}) collective-permute-start(bf16[1,80,128]{2,1,0:T(8,128)(2,1)S(1)} %maximum_bitcast_fusion), channel_id=1, source_target_pairs={{0,8},{1,9},{2,10},{3,11},{4,12},{5,13},{6,14},{7,15},{8,0},{9,1},... | collective-permute-start | bytes 61448 | tf_op jit(solution)/shard_map/ppermute | solution.py:155
  8.7 10.1 %copy-start = (bf16[2,128,512]{2,1,0:T(8,128)(2,1)S(1)}, bf16[2,128,512]{2,1,0:T(8,128)(2,1)}, u32[]{:S(2)}) copy-start(bf16[2,128,512]{2,1,0:T(8,128)(2,1)} %proj_weight.1) | copy-start | bytes 786436
  8.7 4.1 %collective-permute-start.1 = (bf16[2,80,128]{2,1,0:T(8,128)(2,1)S(1)}, bf16[2,80,128]{2,1,0:T(8,128)(2,1)S(1)}, u32[]{:S(2)}, u32[]{:S(2)}) collective-permute-start(bf16[2,80,128]{2,1,0:T(8,128)(2,1)S(1)} %pad_maximum_fusion.2), channel_id=1, source_target_pairs={{0,4},{1,5},{2,6},{3,7},{4,0},{5,1},{6,2},{7,3},{8,12},{9,13},{10,... | collective-permute-start | bytes 122888 | tf_op jit(solution)/shard_map/ppermute | solution.py:155
  12.8 6.0 %copy-start.1 = (bf16[2,128,128]{2,1,0:T(8,128)(2,1)S(1)}, bf16[2,128,128]{2,1,0:T(8,128)(2,1)}, u32[]{:S(2)}) copy-start(bf16[2,128,128]{2,1,0:T(8,128)(2,1)} %gate_weight.1) | copy-start | bytes 196612
  12.8 6.0 %copy-start.2 = (bf16[2,128,128]{2,1,0:T(8,128)(2,1)S(1)}, bf16[2,128,128]{2,1,0:T(8,128)(2,1)}, u32[]{:S(2)}) copy-start(bf16[2,128,128]{2,1,0:T(8,128)(2,1)} %out_weight.1) | copy-start | bytes 196612
  12.8 4.5 %collective-permute-start.2 = (bf16[4,80,128]{2,1,0:T(8,128)(2,1)S(1)}, bf16[4,80,128]{2,1,0:T(8,128)(2,1)S(1)}, u32[]{:S(2)}, u32[]{:S(2)}) collective-permute-start(bf16[4,80,128]{2,1,0:T(8,128)(2,1)S(1)} %pad_maximum_fusion.1), channel_id=1, source_target_pairs={{0,2},{1,3},{2,0},{3,1},{4,6},{5,7},{6,4},{7,5},{8,10},{9,11},{10,... | collective-permute-start | bytes 245768 | tf_op jit(solution)/shard_map/ppermute | solution.py:155
  17.3 1.5 %copy-start.4 = (f32[2,128]{1,0:T(2,128)S(1)}, f32[2,128]{1,0:T(2,128)}, u32[]{:S(2)}) copy-start(f32[2,128]{1,0:T(2,128)} %shift_in.1) | copy-start | bytes 3076
  17.3 1.5 %copy-start.5 = (f32[2,128]{1,0:T(2,128)S(1)}, f32[2,128]{1,0:T(2,128)}, u32[]{:S(2)}) copy-start(f32[2,128]{1,0:T(2,128)} %gain_out.1) | copy-start | bytes 3076
  17.3 1.5 %copy-start.6 = (f32[2,128]{1,0:T(2,128)S(1)}, f32[2,128]{1,0:T(2,128)}, u32[]{:S(2)}) copy-start(f32[2,128]{1,0:T(2,128)} %shift_out.1) | copy-start | bytes 3076
  17.3 1.5 %copy-start.3 = (f32[2,128]{1,0:T(2,128)S(1)}, f32[2,128]{1,0:T(2,128)}, u32[]{:S(2)}) copy-start(f32[2,128]{1,0:T(2,128)} %gain_in.1) | copy-start | bytes 3076
  17.3 1.5 %collective-permute-start.3 = (bf16[8,80,128]{2,1,0:T(8,128)(2,1)S(1)}, bf16[8,80,128]{2,1,0:T(8,128)(2,1)S(1)}, u32[]{:S(2)}, u32[]{:S(2)}) collective-permute-start(bf16[8,80,128]{2,1,0:T(8,128)(2,1)S(1)} %pad_maximum_fusion.own_ref), channel_id=1, source_target_pairs={{0,1},{1,0},{2,3},{3,2},{4,5},{5,4},{6,7},{7,6},{8,9},{9,8},{10,11... | collective-permute-start | bytes 491528 | tf_op jit(solution)/shard_map/ppermute | solution.py:155

commit v3 on v0

--- a/solution.py
+++ b/solution.py
@@ -1,7 +1,228 @@
+import functools
+
 import jax
 import jax.numpy as jnp
 from jax import lax
+from jax.experimental import pallas as pl
+from jax.experimental.pallas import tpu as pltpu
 from jax.sharding import PartitionSpec as P
+
+EPS = 1e-05
+MARK_ROWS = 16
+GATHER_LIMIT = 4 << 20
+
+
+def sigmoid(values):
+    return 0.5 * jnp.tanh(0.5 * values) + 0.5
+
+
+def norm_rows(values, gain, offset):
+    mean = jnp.mean(values, axis=-1, keepdims=True)
+    centered = values - mean
+    variance = jnp.mean(centered * centered, axis=-1, keepdims=True)
+    return (centered * lax.rsqrt(variance + EPS) * gain + offset).astype(jnp.bfloat16)
+
+
+def matmul(left, right):
+    return jnp.dot(left, right, preferred_element_type=jnp.float32)
+
+
+def gated(mask, packed, width):
+    value = mask * sigmoid(packed[:, :width]) * packed[:, width:]
+    return value.astype(jnp.bfloat16).astype(jnp.float32)
+
+
+def seat(device, n_row):
+    place = device % 2
+    step, weight = n_row // 2, 2
+    while step > 4:
+        place = place + weight * (device // step % 2)
+        step, weight = step // 2, 2 * weight
+    return place
+
+
+def seats(n_row):
+    return max(2, n_row // 4)
+
+
+def pack_kernel(n_row, pair_ref, mask_ref, out_ref, mask, at, sems):
+    rows = pair_ref.shape[0]
+    per = mask_ref.shape[0]
+    whole = pltpu.make_async_copy(pair_ref, out_ref.at[0:rows], sems.at[0])
+    part = pltpu.make_async_copy(mask_ref, mask, sems.at[1])
+    whole.start()
+    part.start()
+    first = seat(lax.axis_index("row"), n_row) * per
+    at[...] = jnp.zeros_like(at)
+    part.wait()
+    real = jnp.max(mask[...], axis=1, keepdims=True).astype(jnp.float32)
+    at[pl.ds(first, per), :] = jnp.broadcast_to(real, (per, at.shape[1]))
+    out_ref[rows:, :] = at[...].astype(jnp.bfloat16)
+    whole.wait()
+
+
+def hold(values):
+    return pltpu.with_memory_space_constraint(values, pltpu.HBM)
+
+
+def pack(n_row, pair_rep, pair_mask):
+    per, tokens, width = pair_rep.shape
+    rows = per * tokens
+    extra = -(-seats(n_row) * per // MARK_ROWS) * MARK_ROWS
+    hbm = pl.BlockSpec(memory_space=pltpu.HBM)
+    return pl.pallas_call(
+        functools.partial(pack_kernel, n_row),
+        out_shape=jax.ShapeDtypeStruct((rows + extra, width), jnp.bfloat16),
+        in_specs=[hbm, hbm],
+        out_specs=pl.BlockSpec(memory_space=pltpu.VMEM),
+        scratch_shapes=[
+            pltpu.VMEM((per, tokens), jnp.int32),
+            pltpu.VMEM((extra, width), jnp.float32),
+            pltpu.SemaphoreType.DMA((2,)),
+        ],
+        compiler_params=pltpu.CompilerParams(vmem_limit_bytes=1 << 20),
+    )(hold(pair_rep.reshape(rows, width)), hold(pair_mask))
+
+
+def updates_kernel(
+    n_row,
+    order,
+    steps,
+    me_ref,
+    *refs,
+):
+    blocks = refs[: len(steps)]
+    gain_in, shift_in, proj_weight, gate_weight, gain_out, shift_out, out_weight = refs[len(steps) : len(steps) + 7]
+    out_even, out_odd, pair, valid, left0, right0, gate0, middle, right1, marks = refs[len(steps) + 7 :]
+    me = me_ref[0]
+    width = out_even.shape[-1]
+    tokens = valid.shape[0]
+    per = tokens // n_row
+    rows = per * tokens
+    step_i = 8
+    chunk = step_i * tokens
+    pitch = tokens + 8
+
+    def run():
+        for step, ref in zip(steps, blocks, strict=True):
+            marks[...] = ref[len(order) * rows :, :].astype(jnp.float32)
+            for slot, place in enumerate(order):
+                at = me ^ (step ^ place)
+                pair[pl.ds(pl.multiple_of(at * rows, rows), rows), :] = ref[slot * rows : (slot + 1) * rows, :]
+                valid[pl.ds(at * per, per), :] = marks[pl.ds(seat(at, n_row) * per, per), :]
+
+        def mask_of(i):
+            rowmask = valid[i * step_i : (i + 1) * step_i, :]
+            return (rowmask[:, None, :] * valid[...][None, :, :]).reshape(chunk, width)
+
+        for i in range(tokens // step_i):
+            at = pl.ds(i * chunk, chunk)
+            normed = norm_rows(pair[at, :].astype(jnp.float32), gain_in[0:1, :], shift_in[0:1, :])
+            mask = mask_of(i)
+            packed = matmul(normed, proj_weight[0])
+            left0[at, :] = gated(mask, packed[:, 0 : 2 * width], width)
+            right = gated(mask, packed[:, 2 * width :], width)
+            for r in range(step_i):
+                right0[pl.ds((i * step_i + r) * pitch, tokens), :] = right[r * tokens : (r + 1) * tokens, :]
+            gate0[at, :] = sigmoid(matmul(normed, gate_weight[0]))
+
+        for k in range(tokens):
+            right1[k * tokens : (k + 1) * tokens, :] = right0[pl.ds(k, tokens, stride=pitch), :]
+
+        for i in range(tokens // step_i):
+            at = pl.ds(i * chunk, chunk)
+            totals = [jnp.zeros((tokens, width), jnp.float32)] * step_i
+            for k in range(tokens):
+                row = right1[k * tokens : (k + 1) * tokens, :]
+                for r in range(step_i):
+                    totals[r] = totals[r] + left0[pl.ds(i * chunk + r * tokens + k, 1), :] * row
+            product = jnp.concatenate(totals, axis=0).astype(jnp.bfloat16).astype(jnp.float32)
+            scaled = norm_rows(product, gain_out[0:1, :], shift_out[0:1, :])
+            moved = pair[at, :].astype(jnp.float32) + gate0[at, :] * matmul(scaled, out_weight[0])
+            middle[at, :] = moved.astype(jnp.bfloat16).astype(jnp.float32)
+
+        for i in range(tokens // step_i):
+            at = pl.ds(i * chunk, chunk)
+            normed = norm_rows(middle[at, :], gain_in[1:2, :], shift_in[1:2, :])
+            right0[at, :] = gated(mask_of(i), matmul(normed, proj_weight[1, :, 2 * width :]), width)
+
+        ours = 2 * per
+        first = (me - 1) * per
+        columns = jnp.concatenate([middle[pl.ds(first + r, tokens, stride=tokens), :] for r in range(ours)], axis=0)
+        normed = norm_rows(columns, gain_in[1:2, :], shift_in[1:2, :])
+        mask = jnp.concatenate([valid[...] * valid[pl.ds(first + r, 1), :] for r in range(ours)], axis=0)
+        left0[0 : 2 * rows, :] = gated(mask, matmul(normed, proj_weight[1, :, 0 : 2 * width]), width)
+        totals = [jnp.zeros((tokens, width), jnp.float32)] * ours
+        for k in range(tokens):
+            row = right0[k * tokens : (k + 1) * tokens, :]
+            for r in range(ours):
+                totals[r] = totals[r] + left0[r * tokens + k : r * tokens + k + 1, :] * row
+        product = jnp.concatenate(totals, axis=0).astype(jnp.bfloat16).astype(jnp.float32)
+        scaled = norm_rows(product, gain_out[1:2, :], shift_out[1:2, :])
+        held = middle[pl.ds(pl.multiple_of(first * tokens, 2 * rows), 2 * rows), :]
+        gate = sigmoid(matmul(norm_rows(held, gain_in[1:2, :], shift_in[1:2, :]), gate_weight[1]))
+        result = (held + gate * matmul(scaled, out_weight[1])).astype(jnp.bfloat16)
+        out_even[...] = result[0:rows]
+        out_odd[...] = result[rows:]
+
+    pl.when(me % 2 == 1)(run)
+
+
+def updates(n_row, order, steps, tokens, me, blocks, params):
+    width = blocks[0].shape[-1]
+    rows = tokens * tokens // n_row
+    pairs = tokens * tokens
+    vmem = pl.BlockSpec(memory_space=pltpu.VMEM)
+    return pl.pallas_call(
+        functools.partial(updates_kernel, n_row, order, steps),
+        out_shape=[jax.ShapeDtypeStruct((rows, width), jnp.bfloat16)] * 2,
+        in_specs=[pl.BlockSpec(memory_space=pltpu.SMEM)] + [vmem] * (len(blocks) + 7),
+        out_specs=[vmem] * 2,
+        scratch_shapes=[
+            pltpu.VMEM((pairs, width), jnp.bfloat16),
+            pltpu.VMEM((tokens, width), jnp.float32),
+        ]
+        + [pltpu.VMEM((pairs + 8 * tokens, width), jnp.float32)] * 5
+        + [pltpu.VMEM((blocks[0].shape[0] - len(order) * rows, width), jnp.float32)],
+        compiler_params=pltpu.CompilerParams(vmem_limit_bytes=8 << 20),
+    )(me, *blocks, *params)
+
+
+def swap(values, step, n_row):
+    return lax.ppermute(values, "row", [(i, i ^ step) for i in range(n_row)])
+
+
+def odd_swap(values, step, n_group, n_row):
+    if n_group % 2:
+        return swap(values, step, n_row)
+    target = [(g, i ^ step) if i % 2 else (g ^ 1, i) for g in range(n_group) for i in range(n_row)]
+    pairs = [(source, g * n_row + i) for source, (g, i) in enumerate(target)]
+    return lax.ppermute(values, ("groups", "row"), pairs)
+
+
+def merge(first, second, rows):
+    return jnp.concatenate([first[:rows], second[:rows], first[rows:] + second[rows:]], axis=0)
+
+
+def gathered(n_group, n_row, pair_rep, pair_mask, *params):
+    per, tokens, width = pair_rep.shape
+    rows = per * tokens
+    me = lax.axis_index("row")
+    held = pack(n_row, pair_rep, pair_mask)
+    held = merge(held, swap(held, 1, n_row), rows)
+    order = [0, 1]
+    step = n_row // 2
+    while step > 4:
+        count = len(order)
+        held = merge(held, odd_swap(held, step, n_group, n_row), count * rows)
+        order = order + [place ^ step for place in order]
+        step //= 2
+    steps = [0] + list(range(2, 2 * step, 2))
+    blocks = [held] + [odd_swap(held, place, n_group, n_row) for place in steps[1:]]
+    even, odd = updates(n_row, tuple(order), tuple(steps), tokens, me.astype(jnp.int32).reshape(1), blocks, params)
+    out = jnp.where(me % 2 == 1, odd, swap(even, 1, n_row))
+    return out.reshape(per, tokens, width)
+
 
 H = 128
 
@@ -61,7 +282,7 @@
     return (pair_now.astype(jnp.float32) + gating * update).astype(jnp.bfloat16)
 
 
-def shards(
+def exchanged(
     pair_rep,
     pair_mask,
     gain_in,
@@ -90,6 +311,16 @@
 
 
 def solution(mesh):
+    n_group, n_row = mesh.shape["groups"], mesh.shape["row"]
+
+    def shards(pair_rep, *rest):
+        per, tokens, _ = pair_rep.shape
+        small = pair_rep.size * n_row * 2 <= GATHER_LIMIT
+        fits = n_row & (n_row - 1) == 0 and n_row > 3 and tokens % MARK_ROWS == 0
+        if small and fits:
+            return gathered(n_group, n_row, pair_rep, *rest)
+        return exchanged(pair_rep, *rest)
+
     in_specs = (
         P(("groups", "row"), None, None),
         P(("groups", "row"), None),

time: 74.9 us -> 19.7 us (0.26)
  waiting for transfers between devices: 35.9 us -> 6.64 us
  starting transfers between devices: 25 us -> 11.2 us
  local copies, waits for them, and re-layouts: 8.18 us -> 0.04 us
  matrix products: 3.3 us -> 0 us
  other arithmetic: 1.58 us -> 0.63 us
  Pallas kernels: 0 us -> 0.94 us
    all_to_all x6 -> x0, waiting for transfers between devices: 35.9 us -> none  [the longest x2 12.5 us: triangle(): lax.all_to_all(product, 'row', split_axis=1, concat_axis=0, tiled=True)]
    all_to_all x6 -> x0, starting transfers between devices: 25 us -> none  [the longest x2 10.9 us: triangle(): lax.all_to_all(right, 'row', split_axis=0, concat_axis=1, tiled=True)]
    ppermute x0 -> x6, starting transfers between devices: none -> 11.2 us  [the longest x4 7.01 us: odd_swap(): return lax.ppermute(values, ('groups', 'row'), pairs)]
    unnamed x30 -> x14, local copies, waits for them, and re-layouts: 7.01 us -> 0.03 us
    ppermute x0 -> x6, waiting for transfers between devices: none -> 6.64 us  [the longest x4 4.95 us: odd_swap(): return lax.ppermute(values, ('groups', 'row'), pairs)]
    dot_general x8 -> x0, matrix products: 3.3 us -> none  [the longest x2 1.31 us: triangle(): jnp.einsum('rnc,ch->hrn', normed, proj_weight[layer_index], preferred_ele...]
    reduce_sum x7 -> x0, other arithmetic: 1.33 us -> none  [the longest x3 0.94 us: layer_norm(): mean = jnp.mean(values, axis=axis, keepdims=True)]
    pallas_call x0 -> x2, Pallas kernels: none -> 0.94 us  [the longest x1 0.92 us: pack(): pl.pallas_call(functools.partial(pack_kernel, n_row), out_shape=jax.Shape...]
  transfers between devices with their start and end apart: 6 -> 6, of which waited for: 6 -> 6; matrix products, arithmetic and copies ran while one was open for 4% -> 0% of each run, Pallas kernels for 0% -> 0%
where the time goes in v3:
time: 19.7 us; the launch traced here: 19.5 us
  starting transfers between devices  11.2 us (57%)
  waiting for transfers between devices  6.64 us (34%)
  Pallas kernels  0.94 us (5%)
  other arithmetic  0.63 us (3%)
    ppermute x4, starting transfers between devices, odd_swap(): return lax.ppermute(values, ('groups', 'row'), pairs)  7.01 us
    ppermute x4, waiting for transfers between devices, odd_swap(): return lax.ppermute(values, ('groups', 'row'), pairs)  4.95 us
    ppermute x2, starting transfers between devices, swap(): return lax.ppermute(values, 'row', [(i, i ^ step) for i in range(n_row)])  4.2 us
    ppermute x2, waiting for transfers between devices, swap(): return lax.ppermute(values, 'row', [(i, i ^ step) for i in range(n_row)])  1.68 us
    pallas_call x1, Pallas kernels, pack(): pl.pallas_call(functools.partial(pack_kernel, n_row), out_shape=jax.Shape...  0.92 us
    select_n x1, other arithmetic, gathered(): out = jnp.where(me % 2 == 1, odd, swap(even, 1, n_row))  0.61 us
  transfers between devices with their start and end apart: 6, of which 6 were waited for; matrix products, arithmetic and copies ran while one was open for 0% of the time, Pallas kernels for 0%

profile of v3, /device:TPU:0, one launch (start us, length us, event | category | flops | bytes accessed | tf_op | source)
XLA Modules:
  0.0 19.5 jit_solution(17387088017483688029)
XLA Ops:
  0.0 0.0 copy-start
  0.0 0.9 %shard_map.91 = bf16[80,128]{1,0:T(8,128)(2,1)S(1)} custom-call(bf16[64,128]{1,0:T(8,128)(2,1)} %bitcast.3, s32[2,32]{1,0:T(2,128)} %mask_ref.1), custom_call_target="tpu_custom_call" | custom-call | tf_op jit(solution)/shard_map/pallas_call | solution.py:73
  0.9 0.5 %collective-permute-start = (bf16[80,128]{1,0:T(8,128)(2,1)S(1)}, bf16[80,128]{1,0:T(8,128)(2,1)S(1)}, u32[]{:S(2)}, u32[]{:S(2)}) collective-permute-start(bf16[80,128]{1,0:T(8,128)(2,1)S(1)} %shard_map.91), channel_id=1, source_target_pairs={{0,1},{1,0},{2,3},{3,2},{4,5},{5,4},{6,7},{7,6},{8,9},{9,8},{10,11... | collective-permute-start | bytes 61448 | tf_op jit(solution)/shard_map/ppermute | solution.py:192
  1.5 0.8 %collective-permute-done = bf16[80,128]{1,0:T(8,128)(2,1)S(1)} collective-permute-done((bf16[80,128]{1,0:T(8,128)(2,1)S(1)}, bf16[80,128]{1,0:T(8,128)(2,1)S(1)}, u32[]{:S(2)}, u32[]{:S(2)}) %collective-permute-start) | collective-permute-done | bytes 20512 | tf_op jit(solution)/shard_map/ppermute | solution.py:192
  2.3 2.9 %collective-permute-start.1 = (bf16[144,128]{1,0:T(8,128)(2,1)S(1)}, bf16[144,128]{1,0:T(8,128)(2,1)S(1)}, u32[]{:S(2)}, u32[]{:S(2)}) collective-permute-start(bf16[144,128]{1,0:T(8,128)(2,1)S(1)} %pad_maximum_fusion.1), channel_id=1, source_target_pairs={{0,16},{1,9},{2,18},{3,11},{4,20},{5,13},{6,22},{7,15},{8,24},{9,1... | collective-permute-start | bytes 110600 | tf_op jit(solution)/shard_map/ppermute | solution.py:200
  5.2 1.9 %collective-permute-done.1 = bf16[144,128]{1,0:T(8,128)(2,1)S(1)} collective-permute-done((bf16[144,128]{1,0:T(8,128)(2,1)S(1)}, bf16[144,128]{1,0:T(8,128)(2,1)S(1)}, u32[]{:S(2)}, u32[]{:S(2)}) %collective-permute-start.1) | collective-permute-done | bytes 36896 | tf_op jit(solution)/shard_map/ppermute | solution.py:200
  7.2 0.0 copy-start.1
  7.2 0.0 copy-start.2
  7.2 2.1 %collective-permute-start.2 = (bf16[272,128]{1,0:T(8,128)(2,1)S(1)}, bf16[272,128]{1,0:T(8,128)(2,1)S(1)}, u32[]{:S(2)}, u32[]{:S(2)}) collective-permute-start(bf16[272,128]{1,0:T(8,128)(2,1)S(1)} %pad_maximum_fusion.refs_0_), channel_id=1, source_target_pairs={{0,16},{1,3},{2,18},{3,1},{4,20},{5,7},{6,22},{7,5},{8,24},{9,11},... | collective-permute-start | bytes 208904 | tf_op jit(solution)/shard_map/ppermute | solution.py:200
  9.3 0.1 collective-permute-start.3
  9.3 1.9 %collective-permute-start.4 = (bf16[272,128]{1,0:T(8,128)(2,1)S(1)}, bf16[272,128]{1,0:T(8,128)(2,1)S(1)}, u32[]{:S(2)}, u32[]{:S(2)}) collective-permute-start(bf16[272,128]{1,0:T(8,128)(2,1)S(1)} %pad_maximum_fusion.refs_0_), channel_id=1, source_target_pairs={{0,16},{1,7},{2,18},{3,5},{4,20},{5,3},{6,22},{7,1},{8,24},{9,15},... | collective-permute-start | bytes 208904 | tf_op jit(solution)/shard_map/ppermute | solution.py:200
  11.3 0.0 copy-start.6
  11.3 0.0 copy-start.4
  11.3 0.0 copy-start.5
  11.3 0.0 copy-start.3
  11.3 0.3 %collective-permute-done.2.refs_1_ = bf16[272,128]{1,0:T(8,128)(2,1)S(1)} collective-permute-done((bf16[272,128]{1,0:T(8,128)(2,1)S(1)}, bf16[272,128]{1,0:T(8,128)(2,1)S(1)}, u32[]{:S(2)}, u32[]{:S(2)}) %collective-permute-start.2) | collective-permute-done | bytes 69664 | tf_op jit(solution)/shard_map/ppermute | solution.py:200
  11.6 2.0 %collective-permute-done.3.refs_2_ = bf16[272,128]{1,0:T(8,128)(2,1)S(1)} collective-permute-done((bf16[272,128]{1,0:T(8,128)(2,1)S(1)}, bf16[272,128]{1,0:T(8,128)(2,1)S(1)}, u32[]{:S(2)}, u32[]{:S(2)}) %collective-permute-start.3) | collective-permute-done | bytes 69664 | tf_op jit(solution)/shard_map/ppermute | solution.py:200
  13.6 0.7 %collective-permute-done.4.refs_3_ = bf16[272,128]{1,0:T(8,128)(2,1)S(1)} collective-permute-done((bf16[272,128]{1,0:T(8,128)(2,1)S(1)}, bf16[272,128]{1,0:T(8,128)(2,1)S(1)}, u32[]{:S(2)}, u32[]{:S(2)}) %collective-permute-start.4) | collective-permute-done | bytes 69664 | tf_op jit(solution)/shard_map/ppermute | solution.py:200
  14.3 0.0 copy-done
  14.3 0.0 copy-done.1
  14.3 0.0 copy-done.2
  14.3 0.0 copy-done.6
  14.3 0.0 copy-done.4
  14.4 0.0 copy-done.5
  14.4 0.0 copy-done.3
  14.4 3.7 %collective-permute-start.5 = (bf16[64,128]{1,0:T(8,128)(2,1)S(1)}, bf16[64,128]{1,0:T(8,128)(2,1)S(1)}, u32[]{:S(2)}, u32[]{:S(2)}) collective-permute-start(bf16[64,128]{1,0:T(8,128)(2,1)S(1)} %get-tuple-element.8), channel_id=1, source_target_pairs={{0,1},{1,0},{2,3},{3,2},{4,5},{5,4},{6,7},{7,6},{8,9},{9,8},{10,11... | collective-permute-start | bytes 49160 | tf_op jit(solution)/shard_map/ppermute | solution.py:192
  18.1 0.8 %collective-permute-done.5 = bf16[64,128]{1,0:T(8,128)(2,1)S(1)} collective-permute-done((bf16[64,128]{1,0:T(8,128)(2,1)S(1)}, bf16[64,128]{1,0:T(8,128)(2,1)S(1)}, u32[]{:S(2)}, u32[]{:S(2)}) %collective-permute-start.5) | collective-permute-done | bytes 16416 | tf_op jit(solution)/shard_map/ppermute | solution.py:192
  18.9 0.6 %broadcast_select_fusion = bf16[64,128]{1,0:T(8,128)(2,1)} fusion(bf16[64,128]{1,0:T(8,128)(2,1)S(1)} %get-tuple-element.7, bf16[64,128]{1,0:T(8,128)(2,1)S(1)} %collective-permute-done.5, pred[]{:T(512)S(6)} %eq.5), kind=kLoop, calls=%fused_computation.2 | loop fusion | flops 8192 | bytes 49153 | tf_op jit(solution)/shard_map/jit(_where)/select_n | solution.py:223
  (8 shorter events, 0.0 us)
Async XLA Ops:
  0.0 14.3 %copy-start = (bf16[2,128,512]{2,1,0:T(8,128)(2,1)S(1)}, bf16[2,128,512]{2,1,0:T(8,128)(2,1)}, u32[]{:S(2)}) copy-start(bf16[2,128,512]{2,1,0:T(8,128)(2,1)} %refs_6_.1) | copy-start | bytes 786436
  0.9 1.4 %collective-permute-start = (bf16[80,128]{1,0:T(8,128)(2,1)S(1)}, bf16[80,128]{1,0:T(8,128)(2,1)S(1)}, u32[]{:S(2)}, u32[]{:S(2)}) collective-permute-start(bf16[80,128]{1,0:T(8,128)(2,1)S(1)} %shard_map.91), channel_id=1, source_target_pairs={{0,1},{1,0},{2,3},{3,2},{4,5},{5,4},{6,7},{7,6},{8,9},{9,8},{10,11... | collective-permute-start | bytes 61448 | tf_op jit(solution)/shard_map/ppermute | solution.py:192
  2.3 4.8 %collective-permute-start.1 = (bf16[144,128]{1,0:T(8,128)(2,1)S(1)}, bf16[144,128]{1,0:T(8,128)(2,1)S(1)}, u32[]{:S(2)}, u32[]{:S(2)}) collective-permute-start(bf16[144,128]{1,0:T(8,128)(2,1)S(1)} %pad_maximum_fusion.1), channel_id=1, source_target_pairs={{0,16},{1,9},{2,18},{3,11},{4,20},{5,13},{6,22},{7,15},{8,24},{9,1... | collective-permute-start | bytes 110600 | tf_op jit(solution)/shard_map/ppermute | solution.py:200
  7.2 7.2 %copy-start.1 = (bf16[2,128,128]{2,1,0:T(8,128)(2,1)S(1)}, bf16[2,128,128]{2,1,0:T(8,128)(2,1)}, u32[]{:S(2)}) copy-start(bf16[2,128,128]{2,1,0:T(8,128)(2,1)} %refs_7_.1) | copy-start | bytes 196612
  7.2 7.2 %copy-start.2 = (bf16[2,128,128]{2,1,0:T(8,128)(2,1)S(1)}, bf16[2,128,128]{2,1,0:T(8,128)(2,1)}, u32[]{:S(2)}) copy-start(bf16[2,128,128]{2,1,0:T(8,128)(2,1)} %refs_10_.1) | copy-start | bytes 196612
  7.2 4.4 %collective-permute-start.2 = (bf16[272,128]{1,0:T(8,128)(2,1)S(1)}, bf16[272,128]{1,0:T(8,128)(2,1)S(1)}, u32[]{:S(2)}, u32[]{:S(2)}) collective-permute-start(bf16[272,128]{1,0:T(8,128)(2,1)S(1)} %pad_maximum_fusion.refs_0_), channel_id=1, source_target_pairs={{0,16},{1,3},{2,18},{3,1},{4,20},{5,7},{6,22},{7,5},{8,24},{9,11},... | collective-permute-start | bytes 208904 | tf_op jit(solution)/shard_map/ppermute | solution.py:200
  9.3 4.3 %collective-permute-start.3 = (bf16[272,128]{1,0:T(8,128)(2,1)S(1)}, bf16[272,128]{1,0:T(8,128)(2,1)S(1)}, u32[]{:S(2)}, u32[]{:S(2)}) collective-permute-start(bf16[272,128]{1,0:T(8,128)(2,1)S(1)} %pad_maximum_fusion.refs_0_), channel_id=1, source_target_pairs={{0,16},{1,5},{2,18},{3,7},{4,20},{5,1},{6,22},{7,3},{8,24},{9,13},... | collective-permute-start | bytes 208904 | tf_op jit(solution)/shard_map/ppermute | solution.py:200
  9.3 5.0 %collective-permute-start.4 = (bf16[272,128]{1,0:T(8,128)(2,1)S(1)}, bf16[272,128]{1,0:T(8,128)(2,1)S(1)}, u32[]{:S(2)}, u32[]{:S(2)}) collective-permute-start(bf16[272,128]{1,0:T(8,128)(2,1)S(1)} %pad_maximum_fusion.refs_0_), channel_id=1, source_target_pairs={{0,16},{1,7},{2,18},{3,5},{4,20},{5,3},{6,22},{7,1},{8,24},{9,15},... | collective-permute-start | bytes 208904 | tf_op jit(solution)/shard_map/ppermute | solution.py:200
  11.3 3.0 %copy-start.6 = (f32[2,128]{1,0:T(2,128)S(1)}, f32[2,128]{1,0:T(2,128)}, u32[]{:S(2)}) copy-start(f32[2,128]{1,0:T(2,128)} %refs_9_.1) | copy-start | bytes 3076
  11.3 3.0 %copy-start.4 = (f32[2,128]{1,0:T(2,128)S(1)}, f32[2,128]{1,0:T(2,128)}, u32[]{:S(2)}) copy-start(f32[2,128]{1,0:T(2,128)} %refs_5_.1) | copy-start | bytes 3076
  11.3 3.1 %copy-start.5 = (f32[2,128]{1,0:T(2,128)S(1)}, f32[2,128]{1,0:T(2,128)}, u32[]{:S(2)}) copy-start(f32[2,128]{1,0:T(2,128)} %refs_8_.1) | copy-start | bytes 3076
  11.3 3.1 %copy-start.3 = (f32[2,128]{1,0:T(2,128)S(1)}, f32[2,128]{1,0:T(2,128)}, u32[]{:S(2)}) copy-start(f32[2,128]{1,0:T(2,128)} %refs_4_.1) | copy-start | bytes 3076
  14.4 4.5 %collective-permute-start.5 = (bf16[64,128]{1,0:T(8,128)(2,1)S(1)}, bf16[64,128]{1,0:T(8,128)(2,1)S(1)}, u32[]{:S(2)}, u32[]{:S(2)}) collective-permute-start(bf16[64,128]{1,0:T(8,128)(2,1)S(1)} %get-tuple-element.8), channel_id=1, source_target_pairs={{0,1},{1,0},{2,3},{3,2},{4,5},{5,4},{6,7},{7,6},{8,9},{9,8},{10,11... | collective-permute-start | bytes 49160 | tf_op jit(solution)/shard_map/ppermute | solution.py:192

commit v4 on v3

--- a/solution.py
+++ b/solution.py
@@ -12,10 +12,6 @@
 GATHER_LIMIT = 4 << 20
 
 
-def sigmoid(values):
-    return 0.5 * jnp.tanh(0.5 * values) + 0.5
-
-
 def norm_rows(values, gain, offset):
     mean = jnp.mean(values, axis=-1, keepdims=True)
     centered = values - mean
@@ -27,9 +23,8 @@
     return jnp.dot(left, right, preferred_element_type=jnp.float32)
 
 
-def gated(mask, packed, width):
-    value = mask * sigmoid(packed[:, :width]) * packed[:, width:]
-    return value.astype(jnp.bfloat16).astype(jnp.float32)
+def gated(packed, width):
+    return (jnp.tanh(packed[:, :width]) + 1.0) * packed[:, width:]
 
 
 def seat(device, n_row):
@@ -84,84 +79,138 @@
     )(hold(pair_rep.reshape(rows, width)), hold(pair_mask))
 
 
-def updates_kernel(
-    n_row,
-    order,
-    steps,
-    me_ref,
-    *refs,
-):
-    blocks = refs[: len(steps)]
-    gain_in, shift_in, proj_weight, gate_weight, gain_out, shift_out, out_weight = refs[len(steps) : len(steps) + 7]
-    out_even, out_odd, pair, valid, left0, right0, gate0, middle, right1, marks = refs[len(steps) + 7 :]
+def load_kernel(count, *refs):
+    sources, targets, sems = refs[:count], refs[count : 2 * count], refs[2 * count]
+    copies = [pltpu.make_async_copy(s, t, sems.at[n]) for n, (s, t) in enumerate(zip(sources, targets, strict=True))]
+    for copy in copies:
+        copy.start()
+    for copy in copies:
+        copy.wait()
+
+
+def load(*arrays):
+    count = len(arrays)
+    return pl.pallas_call(
+        functools.partial(load_kernel, count),
+        out_shape=[jax.ShapeDtypeStruct(a.shape, a.dtype) for a in arrays],
+        in_specs=[pl.BlockSpec(memory_space=pltpu.HBM)] * count,
+        out_specs=[pl.BlockSpec(memory_space=pltpu.VMEM)] * count,
+        scratch_shapes=[pltpu.SemaphoreType.DMA((count,))],
+        compiler_params=pltpu.CompilerParams(vmem_limit_bytes=4 << 20),
+    )(*[hold(a) for a in arrays])
+
+
+def project(values, gain_in, shift_in, proj_weight, gate_weight):
+    half = jnp.array(0.5, jnp.bfloat16)
+    width = values.shape[-1]
+    normed = norm_rows(values.astype(jnp.float32), gain_in[0:1, :], shift_in[0:1, :])
+    packed = matmul(normed, proj_weight[0] * half)
+    left, right = gated(packed[:, 0 : 2 * width], width), gated(packed[:, 2 * width :], width)
+    return left, right, jnp.tanh(matmul(normed, gate_weight[0] * half)) + 1.0
+
+
+def project_kernel(block, gain_in, shift_in, proj_weight, gate_weight, left, right, gate):
+    values = block[0 : left.shape[0], :]
+    left[...], right[...], gate[...] = project(values, gain_in, shift_in, proj_weight, gate_weight)
+
+
+def project_block(block, pairs, gain_in, shift_in, proj_weight, gate_weight):
+    width = block.shape[-1]
+    vmem = pl.BlockSpec(memory_space=pltpu.VMEM)
+    return pl.pallas_call(
+        project_kernel,
+        out_shape=[jax.ShapeDtypeStruct((pairs, width), jnp.float32)] * 3,
+        in_specs=[vmem] * 5,
+        out_specs=[vmem] * 3,
+        cost_estimate=pl.CostEstimate(
+            flops=10 * pairs * width * width, bytes_accessed=20 * pairs * width, transcendentals=3 * pairs * width
+        ),
+        compiler_params=pltpu.CompilerParams(vmem_limit_bytes=4 << 20),
+    )(block, gain_in, shift_in, proj_weight, gate_weight)
+
+
+def updates_kernel(n_row, order, steps, me_ref, *refs):
+    count = len(steps)
+    blocks, refs = refs[:count], refs[count:]
+    done, refs = refs[: 3 * (count - 1)], refs[3 * (count - 1) :]
+    gain_in, shift_in, proj_weight, gate_weight, gain_out, shift_out, out_weight = refs[:7]
+    out_even, out_odd, valid, near, marks, last_left, last_gate, right0, right1, middle, left1 = refs[7:]
     me = me_ref[0]
     width = out_even.shape[-1]
     tokens = valid.shape[0]
     per = tokens // n_row
     rows = per * tokens
-    step_i = 8
-    chunk = step_i * tokens
+    held_tokens = len(order) * per
+    chunk = held_tokens * tokens
     pitch = tokens + 8
+    lefts = list(done[0::3]) + [last_left]
+    gates = list(done[2::3]) + [last_gate]
 
     def run():
-        for step, ref in zip(steps, blocks, strict=True):
-            marks[...] = ref[len(order) * rows :, :].astype(jnp.float32)
+        for n, (step, ref) in enumerate(zip(steps, blocks, strict=True)):
+            marks[...] = ref[chunk:, :].astype(jnp.float32)
             for slot, place in enumerate(order):
                 at = me ^ (step ^ place)
-                pair[pl.ds(pl.multiple_of(at * rows, rows), rows), :] = ref[slot * rows : (slot + 1) * rows, :]
-                valid[pl.ds(at * per, per), :] = marks[pl.ds(seat(at, n_row) * per, per), :]
-
-        def mask_of(i):
-            rowmask = valid[i * step_i : (i + 1) * step_i, :]
-            return (rowmask[:, None, :] * valid[...][None, :, :]).reshape(chunk, width)
-
-        for i in range(tokens // step_i):
-            at = pl.ds(i * chunk, chunk)
-            normed = norm_rows(pair[at, :].astype(jnp.float32), gain_in[0:1, :], shift_in[0:1, :])
-            mask = mask_of(i)
-            packed = matmul(normed, proj_weight[0])
-            left0[at, :] = gated(mask, packed[:, 0 : 2 * width], width)
-            right = gated(mask, packed[:, 2 * width :], width)
-            for r in range(step_i):
-                right0[pl.ds((i * step_i + r) * pitch, tokens), :] = right[r * tokens : (r + 1) * tokens, :]
-            gate0[at, :] = sigmoid(matmul(normed, gate_weight[0]))
-
+                real = marks[pl.ds(seat(at, n_row) * per, per), :]
+                valid[pl.ds(at * per, per), :] = real
+                near[n * held_tokens + slot * per : n * held_tokens + (slot + 1) * per, :] = real
+
+        def place_right(n, values):
+            for slot, place in enumerate(order):
+                at = me ^ (steps[n] ^ place)
+                for t in range(per):
+                    row = pl.multiple_of((at * per + t) * pitch, 8)
+                    start = (slot * per + t) * tokens
+                    right0[pl.ds(row, tokens), :] = values[start : start + tokens, :]
+
+        left, right, gate = project(blocks[-1][0:chunk, :], gain_in, shift_in, proj_weight, gate_weight)
+        last_left[...] = left
+        last_gate[...] = gate
+        place_right(count - 1, right)
+        for n in range(count - 1):
+            place_right(n, done[3 * n + 1])
+
+        half = jnp.array(0.5, jnp.bfloat16)
+        real = valid[...]
+        gate_out = out_weight[0] * half
         for k in range(tokens):
-            right1[k * tokens : (k + 1) * tokens, :] = right0[pl.ds(k, tokens, stride=pitch), :]
-
-        for i in range(tokens // step_i):
-            at = pl.ds(i * chunk, chunk)
-            totals = [jnp.zeros((tokens, width), jnp.float32)] * step_i
+            right1[k * tokens : (k + 1) * tokens, :] = right0[pl.ds(k, tokens, stride=pitch), :] * valid[k : k + 1, :]
+
+        for n in range(count):
+            totals = [jnp.zeros((tokens, width), jnp.float32)] * held_tokens
             for k in range(tokens):
                 row = right1[k * tokens : (k + 1) * tokens, :]
-                for r in range(step_i):
-                    totals[r] = totals[r] + left0[pl.ds(i * chunk + r * tokens + k, 1), :] * row
-            product = jnp.concatenate(totals, axis=0).astype(jnp.bfloat16).astype(jnp.float32)
+                for r in range(held_tokens):
+                    totals[r] = totals[r] + lefts[n][r * tokens + k : r * tokens + k + 1, :] * row
+            first = n * held_tokens
+            product = jnp.concatenate(
+                [t * (real * near[first + r : first + r + 1, :]) for r, t in enumerate(totals)], axis=0
+            )
             scaled = norm_rows(product, gain_out[0:1, :], shift_out[0:1, :])
-            moved = pair[at, :].astype(jnp.float32) + gate0[at, :] * matmul(scaled, out_weight[0])
-            middle[at, :] = moved.astype(jnp.bfloat16).astype(jnp.float32)
-
-        for i in range(tokens // step_i):
-            at = pl.ds(i * chunk, chunk)
+            moved = blocks[n][0:chunk, :].astype(jnp.float32) + gates[n][...] * matmul(scaled, gate_out)
+            middle[n * chunk : (n + 1) * chunk, :] = moved
+
+        proj, gate_in, gate_out = proj_weight[1] * half, gate_weight[1] * half, out_weight[1] * half
+        for n in range(count):
+            at = pl.ds(n * chunk, chunk)
             normed = norm_rows(middle[at, :], gain_in[1:2, :], shift_in[1:2, :])
-            right0[at, :] = gated(mask_of(i), matmul(normed, proj_weight[1, :, 2 * width :]), width)
+            right0[at, :] = gated(matmul(normed, proj[:, 2 * width :]), width)
 
         ours = 2 * per
         first = (me - 1) * per
         columns = jnp.concatenate([middle[pl.ds(first + r, tokens, stride=tokens), :] for r in range(ours)], axis=0)
         normed = norm_rows(columns, gain_in[1:2, :], shift_in[1:2, :])
-        mask = jnp.concatenate([valid[...] * valid[pl.ds(first + r, 1), :] for r in range(ours)], axis=0)
-        left0[0 : 2 * rows, :] = gated(mask, matmul(normed, proj_weight[1, :, 0 : 2 * width]), width)
+        left1[...] = gated(matmul(normed, proj[:, 0 : 2 * width]), width) * jnp.concatenate([near[...]] * ours, axis=0)
         totals = [jnp.zeros((tokens, width), jnp.float32)] * ours
         for k in range(tokens):
             row = right0[k * tokens : (k + 1) * tokens, :]
             for r in range(ours):
-                totals[r] = totals[r] + left0[r * tokens + k : r * tokens + k + 1, :] * row
-        product = jnp.concatenate(totals, axis=0).astype(jnp.bfloat16).astype(jnp.float32)
+                totals[r] = totals[r] + left1[r * tokens + k : r * tokens + k + 1, :] * row
+        product = jnp.concatenate([t * (real * valid[pl.ds(first + r, 1), :]) for r, t in enumerate(totals)], axis=0)
         scaled = norm_rows(product, gain_out[1:2, :], shift_out[1:2, :])
-        held = middle[pl.ds(pl.multiple_of(first * tokens, 2 * rows), 2 * rows), :]
-        gate = sigmoid(matmul(norm_rows(held, gain_in[1:2, :], shift_in[1:2, :]), gate_weight[1]))
-        result = (held + gate * matmul(scaled, out_weight[1])).astype(jnp.bfloat16)
+        held = jnp.concatenate([middle[rows : 2 * rows, :], middle[0:rows, :]], axis=0)
+        gate = jnp.tanh(matmul(norm_rows(held, gain_in[1:2, :], shift_in[1:2, :]), gate_in)) + 1.0
+        result = (held + gate * matmul(scaled, gate_out)).astype(jnp.bfloat16)
         out_even[...] = result[0:rows]
         out_odd[...] = result[rows:]
 
@@ -172,20 +221,21 @@
     width = blocks[0].shape[-1]
     rows = tokens * tokens // n_row
     pairs = tokens * tokens
+    chunk = len(order) * rows
+    gain_in, shift_in, proj_weight, gate_weight = params[:4]
+    done = [project_block(block, chunk, gain_in, shift_in, proj_weight, gate_weight) for block in blocks[:-1]]
+    done = [array for arrays in done for array in arrays]
     vmem = pl.BlockSpec(memory_space=pltpu.VMEM)
+    shapes = [(tokens, width)] * 2 + [(blocks[0].shape[0] - chunk, width)]
+    shapes += [(chunk, width)] * 2 + [(pairs + 8 * tokens, width)] + [(pairs, width)] * 2 + [(2 * rows, width)]
     return pl.pallas_call(
         functools.partial(updates_kernel, n_row, order, steps),
         out_shape=[jax.ShapeDtypeStruct((rows, width), jnp.bfloat16)] * 2,
-        in_specs=[pl.BlockSpec(memory_space=pltpu.SMEM)] + [vmem] * (len(blocks) + 7),
+        in_specs=[pl.BlockSpec(memory_space=pltpu.SMEM)] + [vmem] * (len(blocks) + len(done) + 7),
         out_specs=[vmem] * 2,
-        scratch_shapes=[
-            pltpu.VMEM((pairs, width), jnp.bfloat16),
-            pltpu.VMEM((tokens, width), jnp.float32),
-        ]
-        + [pltpu.VMEM((pairs + 8 * tokens, width), jnp.float32)] * 5
-        + [pltpu.VMEM((blocks[0].shape[0] - len(order) * rows, width), jnp.float32)],
+        scratch_shapes=[pltpu.VMEM(shape, jnp.float32) for shape in shapes],
         compiler_params=pltpu.CompilerParams(vmem_limit_bytes=8 << 20),
-    )(me, *blocks, *params)
+    )(me, *blocks, *done, *params)
 
 
 def swap(values, step, n_row):
@@ -217,6 +267,7 @@
         held = merge(held, odd_swap(held, step, n_group, n_row), count * rows)
         order = order + [place ^ step for place in order]
         step //= 2
+    held, *params = lax.optimization_barrier((held, *load(*params)))
     steps = [0] + list(range(2, 2 * step, 2))
     blocks = [held] + [odd_swap(held, place, n_group, n_row) for place in steps[1:]]
     even, odd = updates(n_row, tuple(order), tuple(steps), tokens, me.astype(jnp.int32).reshape(1), blocks, params)

time: 19.7 us -> 19 us (0.964)
  waiting for transfers between devices: 6.64 us -> 4.37 us
  Pallas kernels: 0.94 us -> 3.12 us
  starting transfers between devices: 11.2 us -> 10.7 us
    ppermute x4, waiting for transfers between devices: 4.95 us -> 2.69 us  [odd_swap(): return lax.ppermute(values, ('groups', 'row'), pairs)]
    pallas_call x0 -> x4, Pallas kernels: none -> 2.24 us  [the longest x3 1.17 us: project_block(): pl.pallas_call(project_kernel, out_shape=[jax.ShapeDtypeStruct((pairs, wi...]
    ppermute x2, starting transfers between devices: 4.2 us -> 3.67 us  [swap(): return lax.ppermute(values, 'row', [(i, i ^ step) for i in range(n_row)])]
  transfers between devices with their start and end apart: 6 -> 6, of which waited for: 6 -> 5; matrix products, arithmetic and copies ran while one was open for 0% -> 0% of each run, Pallas kernels for 0% -> 12%
where the time goes in v4:
time: 19 us; the launch traced here: 18.9 us
  starting transfers between devices  10.7 us (56%)
  waiting for transfers between devices  4.37 us (23%)
  Pallas kernels  3.12 us (16%)
  other arithmetic  0.63 us (3%)
    ppermute x4, starting transfers between devices, odd_swap(): return lax.ppermute(values, ('groups', 'row'), pairs)  7.01 us
    ppermute x2, starting transfers between devices, swap(): return lax.ppermute(values, 'row', [(i, i ^ step) for i in range(n_row)])  3.67 us
    ppermute x4, waiting for transfers between devices, odd_swap(): return lax.ppermute(values, ('groups', 'row'), pairs)  2.69 us
    ppermute x2, waiting for transfers between devices, swap(): return lax.ppermute(values, 'row', [(i, i ^ step) for i in range(n_row)])  1.68 us
    pallas_call x3, Pallas kernels, project_block(): pl.pallas_call(project_kernel, out_shape=[jax.ShapeDtypeStruct((pairs, wi...  1.17 us
    pallas_call x1, Pallas kernels, load(): pl.pallas_call(functools.partial(load_kernel, count), out_shape=[jax.Shap...  1.07 us
    pallas_call x1, Pallas kernels, pack(): pl.pallas_call(functools.partial(pack_kernel, n_row), out_shape=jax.Shape...  0.88 us
    select_n x1, other arithmetic, gathered(): out = jnp.where(me % 2 == 1, odd, swap(even, 1, n_row))  0.61 us
  transfers between devices with their start and end apart: 6, of which 5 were waited for; matrix products, arithmetic and copies ran while one was open for 0% of the time, Pallas kernels for 12%

profile of v4, /device:TPU:0, one launch (start us, length us, event | category | flops | bytes accessed | tf_op | source)
XLA Modules:
  0.0 18.9 jit_solution(15020100805353781241)
XLA Ops:
  0.0 0.9 %shard_map.91 = bf16[80,128]{1,0:T(8,128)(2,1)S(1)} custom-call(bf16[64,128]{1,0:T(8,128)(2,1)} %bitcast.3, s32[2,32]{1,0:T(2,128)} %mask_ref.1), custom_call_target="tpu_custom_call" | custom-call | tf_op jit(solution)/shard_map/pallas_call | solution.py:68
  0.9 0.5 %collective-permute-start = (bf16[80,128]{1,0:T(8,128)(2,1)S(1)}, bf16[80,128]{1,0:T(8,128)(2,1)S(1)}, u32[]{:S(2)}, u32[]{:S(2)}) collective-permute-start(bf16[80,128]{1,0:T(8,128)(2,1)S(1)} %shard_map.91), channel_id=1, source_target_pairs={{0,1},{1,0},{2,3},{3,2},{4,5},{5,4},{6,7},{7,6},{8,9},{9,8},{10,11... | collective-permute-start | bytes 61448 | tf_op jit(solution)/shard_map/ppermute | solution.py:242
  1.4 0.8 %collective-permute-done = bf16[80,128]{1,0:T(8,128)(2,1)S(1)} collective-permute-done((bf16[80,128]{1,0:T(8,128)(2,1)S(1)}, bf16[80,128]{1,0:T(8,128)(2,1)S(1)}, u32[]{:S(2)}, u32[]{:S(2)}) %collective-permute-start) | collective-permute-done | bytes 20512 | tf_op jit(solution)/shard_map/ppermute | solution.py:242
  2.3 2.9 %collective-permute-start.1 = (bf16[144,128]{1,0:T(8,128)(2,1)S(1)}, bf16[144,128]{1,0:T(8,128)(2,1)S(1)}, u32[]{:S(2)}, u32[]{:S(2)}) collective-permute-start(bf16[144,128]{1,0:T(8,128)(2,1)S(1)} %pad_maximum_fusion.1), channel_id=1, source_target_pairs={{0,16},{1,9},{2,18},{3,11},{4,20},{5,13},{6,22},{7,15},{8,24},{9,1... | collective-permute-start | bytes 110600 | tf_op jit(solution)/shard_map/ppermute | solution.py:250
  5.2 1.1 %shard_map.92 = (f32[2,128]{1,0:T(2,128)S(1)}, f32[2,128]{1,0:T(2,128)S(1)}, bf16[2,128,512]{2,1,0:T(8,128)(2,1)S(1)}, bf16[2,128,128]{2,1,0:T(8,128)(2,1)S(1)},...) custom-call(f32[2,128]{1,0:T(2,128)} %refs_0_.1, f32[2,128]{1,0:T(2,128)} %refs_1_.1, ...), custom_call_target="tpu_custom_call" | custom-call | tf_op jit(solution)/shard_map/pallas_call | solution.py:93
  6.2 0.9 %collective-permute-done.1 = bf16[144,128]{1,0:T(8,128)(2,1)S(1)} collective-permute-done((bf16[144,128]{1,0:T(8,128)(2,1)S(1)}, bf16[144,128]{1,0:T(8,128)(2,1)S(1)}, u32[]{:S(2)}, u32[]{:S(2)}) %collective-permute-start.1) | collective-permute-done | bytes 36896 | tf_op jit(solution)/shard_map/ppermute | solution.py:250
  7.1 2.1 %collective-permute-start.3 = (bf16[272,128]{1,0:T(8,128)(2,1)S(1)}, bf16[272,128]{1,0:T(8,128)(2,1)S(1)}, u32[]{:S(2)}, u32[]{:S(2)}) collective-permute-start(bf16[272,128]{1,0:T(8,128)(2,1)S(1)} %pad_maximum_fusion.block.refs_0_), channel_id=1, source_target_pairs={{0,16},{1,5},{2,18},{3,7},{4,20},{5,1},{6,22},{7,3},{8,24},{9,13},... | collective-permute-start | bytes 208904 | tf_op jit(solution)/shard_map/ppermute | solution.py:250
  9.2 0.1 collective-permute-start.2
  9.3 1.9 %collective-permute-start.4 = (bf16[272,128]{1,0:T(8,128)(2,1)S(1)}, bf16[272,128]{1,0:T(8,128)(2,1)S(1)}, u32[]{:S(2)}, u32[]{:S(2)}) collective-permute-start(bf16[272,128]{1,0:T(8,128)(2,1)S(1)} %pad_maximum_fusion.block.refs_0_), channel_id=1, source_target_pairs={{0,16},{1,7},{2,18},{3,5},{4,20},{5,3},{6,22},{7,1},{8,24},{9,15},... | collective-permute-start | bytes 208904 | tf_op jit(solution)/shard_map/ppermute | solution.py:250
  11.2 0.4 %shard_map.93 = (f32[256,128]{1,0:T(8,128)S(1)}, f32[256,128]{1,0:T(8,128)S(1)}, f32[256,128]{1,0:T(8,128)S(1)}) custom-call(bf16[272,128]{1,0:T(8,128)(2,1)S(1)} %pad_maximum_fusion.block.refs_0_, f32[2,128]{1,0:T(2,128)S(1)} %get-tuple-element.39.gain_in.refs_13_, f32[2,128]{1,0:T(2,128)S(1)} %get-tuple-element.40.shift_in.refs_14_, ...), custom_call_target="tpu_custom_call" | custom-call | flops 41943040 | bytes 655360 | tf_op jit(solution)/shard_map/pallas_call | solution.py:120
  11.6 0.0 collective-permute-done.3.block.refs_2_
  11.6 0.4 %shard_map.95 = (f32[256,128]{1,0:T(8,128)S(1)}, f32[256,128]{1,0:T(8,128)S(1)}, f32[256,128]{1,0:T(8,128)S(1)}) custom-call(bf16[272,128]{1,0:T(8,128)(2,1)S(1)} %collective-permute-done.3.block.refs_2_, f32[2,128]{1,0:T(2,128)S(1)} %get-tuple-element.39.gain_in.refs_13_, f32[2,128]{1,0:T(2,128)S(1)} %get-tuple-element.40.shift_in.refs_14_, ...), custom_call_target="tpu_custom_call" | custom-call | flops 41943040 | bytes 655360 | tf_op jit(solution)/shard_map/pallas_call | solution.py:120
  12.0 1.5 %collective-permute-done.2.block.refs_1_ = bf16[272,128]{1,0:T(8,128)(2,1)S(1)} collective-permute-done((bf16[272,128]{1,0:T(8,128)(2,1)S(1)}, bf16[272,128]{1,0:T(8,128)(2,1)S(1)}, u32[]{:S(2)}, u32[]{:S(2)}) %collective-permute-start.2) | collective-permute-done | bytes 69664 | tf_op jit(solution)/shard_map/ppermute | solution.py:250
  13.5 0.4 %shard_map.94 = (f32[256,128]{1,0:T(8,128)S(1)}, f32[256,128]{1,0:T(8,128)S(1)}, f32[256,128]{1,0:T(8,128)S(1)}) custom-call(bf16[272,128]{1,0:T(8,128)(2,1)S(1)} %collective-permute-done.2.block.refs_1_, f32[2,128]{1,0:T(2,128)S(1)} %get-tuple-element.39.gain_in.refs_13_, f32[2,128]{1,0:T(2,128)S(1)} %get-tuple-element.40.shift_in.refs_14_, ...), custom_call_target="tpu_custom_call" | custom-call | flops 41943040 | bytes 655360 | tf_op jit(solution)/shard_map/pallas_call | solution.py:120
  13.9 0.3 %collective-permute-done.4.refs_3_ = bf16[272,128]{1,0:T(8,128)(2,1)S(1)} collective-permute-done((bf16[272,128]{1,0:T(8,128)(2,1)S(1)}, bf16[272,128]{1,0:T(8,128)(2,1)S(1)}, u32[]{:S(2)}, u32[]{:S(2)}) %collective-permute-start.4) | collective-permute-done | bytes 69664 | tf_op jit(solution)/shard_map/ppermute | solution.py:250
  14.3 3.1 %collective-permute-start.5 = (bf16[64,128]{1,0:T(8,128)(2,1)S(1)}, bf16[64,128]{1,0:T(8,128)(2,1)S(1)}, u32[]{:S(2)}, u32[]{:S(2)}) collective-permute-start(bf16[64,128]{1,0:T(8,128)(2,1)S(1)} %get-tuple-element.56), channel_id=1, source_target_pairs={{0,1},{1,0},{2,3},{3,2},{4,5},{5,4},{6,7},{7,6},{8,9},{9,8},{10,11... | collective-permute-start | bytes 49160 | tf_op jit(solution)/shard_map/ppermute | solution.py:242
  17.4 0.8 %collective-permute-done.5 = bf16[64,128]{1,0:T(8,128)(2,1)S(1)} collective-permute-done((bf16[64,128]{1,0:T(8,128)(2,1)S(1)}, bf16[64,128]{1,0:T(8,128)(2,1)S(1)}, u32[]{:S(2)}, u32[]{:S(2)}) %collective-permute-start.5) | collective-permute-done | bytes 16416 | tf_op jit(solution)/shard_map/ppermute | solution.py:242
  18.2 0.6 %broadcast_select_fusion = bf16[64,128]{1,0:T(8,128)(2,1)} fusion(bf16[64,128]{1,0:T(8,128)(2,1)S(1)} %get-tuple-element.55, bf16[64,128]{1,0:T(8,128)(2,1)S(1)} %collective-permute-done.5, pred[]{:T(512)S(6)} %eq.5), kind=kLoop, calls=%fused_computation.2 | loop fusion | flops 8192 | bytes 49153 | tf_op jit(solution)/shard_map/jit(_where)/select_n | solution.py:274
  (8 shorter events, 0.0 us)
Async XLA Ops:
  0.9 1.4 %collective-permute-start = (bf16[80,128]{1,0:T(8,128)(2,1)S(1)}, bf16[80,128]{1,0:T(8,128)(2,1)S(1)}, u32[]{:S(2)}, u32[]{:S(2)}) collective-permute-start(bf16[80,128]{1,0:T(8,128)(2,1)S(1)} %shard_map.91), channel_id=1, source_target_pairs={{0,1},{1,0},{2,3},{3,2},{4,5},{5,4},{6,7},{7,6},{8,9},{9,8},{10,11... | collective-permute-start | bytes 61448 | tf_op jit(solution)/shard_map/ppermute | solution.py:242
  2.3 4.8 %collective-permute-start.1 = (bf16[144,128]{1,0:T(8,128)(2,1)S(1)}, bf16[144,128]{1,0:T(8,128)(2,1)S(1)}, u32[]{:S(2)}, u32[]{:S(2)}) collective-permute-start(bf16[144,128]{1,0:T(8,128)(2,1)S(1)} %pad_maximum_fusion.1), channel_id=1, source_target_pairs={{0,16},{1,9},{2,18},{3,11},{4,20},{5,13},{6,22},{7,15},{8,24},{9,1... | collective-permute-start | bytes 110600 | tf_op jit(solution)/shard_map/ppermute | solution.py:250
  7.1 4.5 %collective-permute-start.3 = (bf16[272,128]{1,0:T(8,128)(2,1)S(1)}, bf16[272,128]{1,0:T(8,128)(2,1)S(1)}, u32[]{:S(2)}, u32[]{:S(2)}) collective-permute-start(bf16[272,128]{1,0:T(8,128)(2,1)S(1)} %pad_maximum_fusion.block.refs_0_), channel_id=1, source_target_pairs={{0,16},{1,5},{2,18},{3,7},{4,20},{5,1},{6,22},{7,3},{8,24},{9,13},... | collective-permute-start | bytes 208904 | tf_op jit(solution)/shard_map/ppermute | solution.py:250
  9.2 4.3 %collective-permute-start.2 = (bf16[272,128]{1,0:T(8,128)(2,1)S(1)}, bf16[272,128]{1,0:T(8,128)(2,1)S(1)}, u32[]{:S(2)}, u32[]{:S(2)}) collective-permute-start(bf16[272,128]{1,0:T(8,128)(2,1)S(1)} %pad_maximum_fusion.block.refs_0_), channel_id=1, source_target_pairs={{0,16},{1,3},{2,18},{3,1},{4,20},{5,7},{6,22},{7,5},{8,24},{9,11},... | collective-permute-start | bytes 208904 | tf_op jit(solution)/shard_map/ppermute | solution.py:250
  9.3 5.0 %collective-permute-start.4 = (bf16[272,128]{1,0:T(8,128)(2,1)S(1)}, bf16[272,128]{1,0:T(8,128)(2,1)S(1)}, u32[]{:S(2)}, u32[]{:S(2)}) collective-permute-start(bf16[272,128]{1,0:T(8,128)(2,1)S(1)} %pad_maximum_fusion.block.refs_0_), channel_id=1, source_target_pairs={{0,16},{1,7},{2,18},{3,5},{4,20},{5,3},{6,22},{7,1},{8,24},{9,15},... | collective-permute-start | bytes 208904 | tf_op jit(solution)/shard_map/ppermute | solution.py:250
  14.3 4.0 %collective-permute-start.5 = (bf16[64,128]{1,0:T(8,128)(2,1)S(1)}, bf16[64,128]{1,0:T(8,128)(2,1)S(1)}, u32[]{:S(2)}, u32[]{:S(2)}) collective-permute-start(bf16[64,128]{1,0:T(8,128)(2,1)S(1)} %get-tuple-element.56), channel_id=1, source_target_pairs={{0,1},{1,0},{2,3},{3,2},{4,5},{5,4},{6,7},{7,6},{8,9},{9,8},{10,11... | collective-permute-start | bytes 49160 | tf_op jit(solution)/shard_map/ppermute | solution.py:242

commit v5 on v4

v5 whole, which is shorter than its diff:
```python
import functools

import jax
import jax.numpy as jnp
from jax import lax
from jax.experimental import pallas as pl
from jax.experimental.pallas import tpu as pltpu
from jax.sharding import PartitionSpec as P

EPS = 1e-05
MARK_ROWS = 16
GATHER_LIMIT = 4 << 20


def norm_rows(values, gain, offset):
    mean = jnp.mean(values, axis=-1, keepdims=True)
    centered = values - mean
    variance = jnp.mean(centered * centered, axis=-1, keepdims=True)
    return (centered * lax.rsqrt(variance + EPS) * gain + offset).astype(jnp.bfloat16)


def matmul(left, right):
    return jnp.dot(left, right, preferred_element_type=jnp.float32)


def gated(packed, width):
    return (jnp.tanh(packed[:, :width]) + 1.0) * packed[:, width:]


def seat(device, n_row):
    place = device % 2
    step, weight = n_row // 2, 2
    while step > 4:
        place = place + weight * (device // step % 2)
        step, weight = step // 2, 2 * weight
    return place


def seats(n_row):
    return max(2, n_row // 4)


def pack_kernel(n_row, pair_ref, mask_ref, out_ref, mask, marks, sems):
    rows = pair_ref.shape[0]
    per, tokens = mask_ref.shape
    width = out_ref.shape[1]
    whole = pltpu.make_async_copy(pair_ref, out_ref.at[0:rows], sems.at[0])
    part = pltpu.make_async_copy(mask_ref, mask, sems.at[1])
    part.start()
    whole.start()
    first = seat(lax.axis_index("row"), n_row) * per
    marks[...] = jnp.zeros_like(marks)
    diagonal = lax.broadcasted_iota(jnp.int32, (tokens, tokens), 0)
    diagonal = diagonal == lax.broadcasted_iota(jnp.int32, (tokens, tokens), 1)
    part.wait()
    mine = mask[...].astype(jnp.float32)
    marks[pl.ds(first, per), :] = jnp.broadcast_to(jnp.max(mine, axis=1, keepdims=True), (per, width))
    seen = jnp.where(diagonal, jnp.max(mine, axis=0, keepdims=True), 0.0)
    seen = jnp.broadcast_to(jnp.sum(seen, axis=1, keepdims=True), (tokens, width))
    out_ref[rows:, :] = jnp.concatenate([marks[...], seen], axis=0).astype(jnp.bfloat16)
    whole.wait()


def hold(values):
    return pltpu.with_memory_space_constraint(values, pltpu.HBM)


def mark_rows(n_row, per):
    return -(-seats(n_row) * per // MARK_ROWS) * MARK_ROWS


def pack(n_row, pair_rep, pair_mask):
    per, tokens, width = pair_rep.shape
    rows = per * tokens
    extra = mark_rows(n_row, per)
    hbm = pl.BlockSpec(memory_space=pltpu.HBM)
    return pl.pallas_call(
        functools.partial(pack_kernel, n_row),
        out_shape=jax.ShapeDtypeStruct((rows + extra + tokens, width), jnp.bfloat16),
        in_specs=[hbm, hbm],
        out_specs=pl.BlockSpec(memory_space=pltpu.VMEM),
        scratch_shapes=[
            pltpu.VMEM((per, tokens), jnp.int32),
            pltpu.VMEM((extra, width), jnp.float32),
            pltpu.SemaphoreType.DMA((2,)),
        ],
        compiler_params=pltpu.CompilerParams(vmem_limit_bytes=1 << 20),
    )(hold(pair_rep.reshape(rows, width)), hold(pair_mask))


def load_kernel(count, *refs):
    sources, targets, sems = refs[:count], refs[count : 2 * count], refs[2 * count]
    copies = [pltpu.make_async_copy(s, t, sems.at[n]) for n, (s, t) in enumerate(zip(sources, targets, strict=True))]
    for copy in copies:
        copy.start()
    for copy in copies:
        copy.wait()


def load(*arrays):
    count = len(arrays)
    return pl.pallas_call(
        functools.partial(load_kernel, count),
        out_shape=[jax.ShapeDtypeStruct(a.shape, a.dtype) for a in arrays],
        in_specs=[pl.BlockSpec(memory_space=pltpu.HBM)] * count,
        out_specs=[pl.BlockSpec(memory_space=pltpu.VMEM)] * count,
        scratch_shapes=[pltpu.SemaphoreType.DMA((count,))],
        compiler_params=pltpu.CompilerParams(vmem_limit_bytes=4 << 20),
    )(*[hold(a) for a in arrays])


class Layout:
    def __init__(self, n_row, order, steps, tokens):
        self.n_row, self.order, self.steps, self.tokens = n_row, order, steps, tokens
        self.per = tokens // n_row
        self.group = len(order) * self.per
        self.chunk = self.group * tokens
        self.pitch = tokens + 8
        self.marks = mark_rows(n_row, self.per)

    def places(self):
        me = lax.axis_index("row")
        for n, step in enumerate(self.steps):
            for slot, place in enumerate(self.order):
                yield n * self.group + slot * self.per, me ^ (step ^ place)

    def pairs(self, n):
        return [(n, q) for q in range(n + 1)] + [(p, n) for p in range(n)]


def prepare(lay, n, block, gain_in, shift_in, proj_weight, gate_weight, outs, scratch):
    z, left, right, gate, near = outs
    marks, rough, seen = scratch
    tokens, group, per, chunk, pitch = lay.tokens, lay.group, lay.per, lay.chunk, lay.pitch
    width = z.shape[-1]
    half = jnp.array(0.5, jnp.bfloat16)
    places = list(lay.places())
    marks[...] = block[chunk:, :].astype(jnp.float32)
    for first, at in places:
        seen[first : first + per, :] = jnp.minimum(marks[pl.ds(lay.marks + at * per, per), :], 1.0)
    for first, at in places[n * len(lay.order) : (n + 1) * len(lay.order)]:
        near[first - n * group : first - n * group + per, :] = marks[pl.ds(seat(at, lay.n_row) * per, per), :]
    for t in range(group):
        rough[t * pitch : t * pitch + tokens, :] = block[t * tokens : (t + 1) * tokens, :].astype(jnp.float32)
    for first, at in places:
        for t in range(per):
            z[pl.ds(first + t, group, stride=pitch), :] = rough[pl.ds(at * per + t, group, stride=pitch), :]
    values = jnp.concatenate([z[t * pitch : t * pitch + tokens, :] for t in range(group)], axis=0)
    normed = norm_rows(values, gain_in[0:1, :], shift_in[0:1, :])
    packed = matmul(normed, proj_weight[0] * half)
    rights = gated(packed[:, 2 * width :], width)
    for t in range(group):
        rough[t * pitch : t * pitch + tokens, :] = rights[t * tokens : (t + 1) * tokens, :]
    left[...] = gated(packed[:, 0 : 2 * width], width)
    for k in range(tokens):
        right[k * group : (k + 1) * group, :] = rough[pl.ds(k, group, stride=pitch), :] * seen[k : k + 1, :]
    gate[...] = jnp.tanh(matmul(normed, gate_weight[0] * half)) + 1.0


def block_sums(lay, left, rights):
    tokens, group = lay.tokens, lay.group
    width = left.shape[-1]
    totals = [[jnp.zeros((group, width), jnp.float32)] * group for _ in rights]
    for k in range(tokens):
        rows = [right[k * group : (k + 1) * group, :] for right in rights]
        for i in range(group):
            value = left[i * tokens + k : i * tokens + k + 1, :]
            for q, row in enumerate(rows):
                totals[q][i] = totals[q][i] + value * row
    return totals


def complete(lay, n, lefts, rights, sums):
    size = lay.group * lay.group
    totals = block_sums(lay, lefts[n], rights)
    for p in range(n):
        totals += block_sums(lay, lefts[p], rights[n : n + 1])
    for place, total in enumerate(totals):
        sums[place * size : (place + 1) * size, :] = jnp.concatenate(total, axis=0)


def group_kernel(lay, n, block, *refs):
    lefts, rights, refs = refs[:n], refs[n : 2 * n], refs[2 * n :]
    params, outs, sums, scratch = refs[:4], refs[4:9], refs[9], refs[10:]
    prepare(lay, n, block, *params, outs, scratch)
    complete(lay, n, [*lefts, outs[1]], [*rights, outs[2]], sums)


def group_shapes(lay, n, width):
    count = len(lay.pairs(n)) * lay.group * lay.group
    rows = [lay.group * lay.pitch, lay.chunk, lay.chunk, lay.chunk, lay.group, count]
    return [(r, width) for r in rows]


def scratch_shapes(lay, width):
    rows = [lay.marks + lay.tokens, lay.group * lay.pitch, lay.tokens]
    return [pltpu.VMEM((r, width), jnp.float32) for r in rows]


def complete_group(lay, n, block, lefts, rights, params):
    width = block.shape[-1]
    vmem = pl.BlockSpec(memory_space=pltpu.VMEM)
    shapes = group_shapes(lay, n, width)
    sums = shapes[-1][0] * lay.tokens * width
    return pl.pallas_call(
        functools.partial(group_kernel, lay, n),
        out_shape=[jax.ShapeDtypeStruct(shape, jnp.float32) for shape in shapes],
        in_specs=[vmem] * (5 + 2 * n),
        out_specs=[vmem] * len(shapes),
        scratch_shapes=scratch_shapes(lay, width),
        cost_estimate=pl.CostEstimate(
            flops=10 * lay.chunk * width * width + 2 * sums,
            bytes_accessed=20 * lay.chunk * width,
            transcendentals=3 * lay.chunk * width,
        ),
        compiler_params=pltpu.CompilerParams(vmem_limit_bytes=4 << 20),
    )(block, *lefts, *rights, *params)


def updates_kernel(lay, block, *refs):
    last = len(lay.steps) - 1
    done = [refs[6 * n : 6 * n + 6] for n in range(last)]
    refs = refs[6 * last :]
    gain_in, shift_in, proj_weight, gate_weight, gain_out, shift_out, out_weight = refs[:7]
    out_even, out_odd = refs[7:9]
    own, scratch = refs[9:15], refs[15:18]
    right1, middle, left1, result1 = refs[18:]
    tokens, per, group, chunk, pitch = lay.tokens, lay.per, lay.group, lay.chunk, lay.pitch
    width = out_even.shape[-1]
    rows = per * tokens
    done = done + [own]

    def run():
        prepare(lay, last, block, gain_in, shift_in, proj_weight, gate_weight, own[:5], scratch)
        complete(lay, last, [arrays[1] for arrays in done], [arrays[2] for arrays in done], own[5])

        half = jnp.array(0.5, jnp.bfloat16)
        real = jnp.concatenate([arrays[4][...] for arrays in done], axis=0)
        gate_out = out_weight[0] * half
        for p in range(last + 1):
            z, _, _, gate, near, _ = done[p]
            products = []
            for i in range(group):
                parts = []
                for q in range(last + 1):
                    n = max(p, q)
                    start = (lay.pairs(n).index((p, q)) * group + i) * group
                    parts.append(done[n][5][start : start + group, :])
                products.append(jnp.concatenate(parts, axis=0) * (real * near[i : i + 1, :]))
            scaled = norm_rows(jnp.concatenate(products, axis=0), gain_out[0:1, :], shift_out[0:1, :])
            held = jnp.concatenate([z[t * pitch : t * pitch + tokens, :] for t in range(group)], axis=0)
            middle[p * chunk : (p + 1) * chunk, :] = held + gate[...] * matmul(scaled, gate_out)

        proj, gate_in, gate_out = proj_weight[1] * half, gate_weight[1] * half, out_weight[1] * half
        for p in range(last + 1):
            at = slice(p * chunk, (p + 1) * chunk)
            normed = norm_rows(middle[at, :], gain_in[1:2, :], shift_in[1:2, :])
            right1[at, :] = gated(matmul(normed, proj[:, 2 * width :]), width)

        ours = [*range(per, 2 * per), *range(per)]
        columns = jnp.concatenate([middle[pl.ds(r, tokens, stride=tokens), :] for r in ours], axis=0)
        normed = norm_rows(columns, gain_in[1:2, :], shift_in[1:2, :])
        left1[...] = gated(matmul(normed, proj[:, 0 : 2 * width]), width) * jnp.concatenate([real] * len(ours), axis=0)
        totals = [jnp.zeros((tokens, width), jnp.float32)] * len(ours)
        for k in range(tokens):
            row = right1[k * tokens : (k + 1) * tokens, :]
            for r in range(len(ours)):
                totals[r] = totals[r] + left1[r * tokens + k : r * tokens + k + 1, :] * row
        near = done[0][4]
        product = jnp.concatenate([t * (real * near[r : r + 1, :]) for r, t in zip(ours, totals, strict=True)], axis=0)
        scaled = norm_rows(product, gain_out[1:2, :], shift_out[1:2, :])
        held = jnp.concatenate([middle[rows : 2 * rows, :], middle[0:rows, :]], axis=0)
        gate = jnp.tanh(matmul(norm_rows(held, gain_in[1:2, :], shift_in[1:2, :]), gate_in)) + 1.0
        result = held + gate * matmul(scaled, gate_out)
        rough = scratch[1]
        for r in range(len(ours)):
            rough[r * pitch : r * pitch + tokens, :] = result[r * tokens : (r + 1) * tokens, :]
        for first, at in lay.places():
            for t in range(per):
                row = rough[pl.ds(first + t, len(ours), stride=pitch), :]
                result1[pl.ds(at * per + t, len(ours), stride=pitch), :] = row
        halves = [result1[r * pitch : r * pitch + tokens, :] for r in range(len(ours))]
        out_even[...] = jnp.concatenate(halves[:per], axis=0).astype(jnp.bfloat16)
        out_odd[...] = jnp.concatenate(halves[per:], axis=0).astype(jnp.bfloat16)

    pl.when(lax.axis_index("row") % 2 == 1)(run)


def updates(lay, blocks, params):
    width = blocks[0].shape[-1]
    rows = lay.per * lay.tokens
    pairs = lay.tokens * lay.tokens
    done = []
    for n, block in enumerate(blocks[:-1]):
        lefts, rights = [arrays[1] for arrays in done], [arrays[2] for arrays in done]
        done.append(complete_group(lay, n, block, lefts, rights, params[:4]))
    arrays = [array for arrays in done for array in arrays]
    vmem = pl.BlockSpec(memory_space=pltpu.VMEM)
    shapes = group_shapes(lay, len(blocks) - 1, width)
    tail = [(pairs, width), (pairs, width), (2 * rows, width), (2 * lay.per * lay.pitch, width)]
    return pl.pallas_call(
        functools.partial(updates_kernel, lay),
        out_shape=[jax.ShapeDtypeStruct((rows, width), jnp.bfloat16)] * 2,
        in_specs=[vmem] * (1 + len(arrays) + 7),
        out_specs=[vmem] * 2,
        scratch_shapes=[pltpu.VMEM(shape, jnp.float32) for shape in shapes]
        + scratch_shapes(lay, width)
        + [pltpu.VMEM(shape, jnp.float32) for shape in tail],
        compiler_params=pltpu.CompilerParams(vmem_limit_bytes=8 << 20),
    )(blocks[-1], *arrays, *params)


def swap(values, step, n_row):
    return lax.ppermute(values, "row", [(i, i ^ step) for i in range(n_row)])


def odd_swap(values, step, n_group, n_row):
    if n_group % 2:
        return swap(values, step, n_row)
    target = [(g, i ^ step) if i % 2 else (g ^ 1, i) for g in range(n_group) for i in range(n_row)]
    pairs = [(source, g * n_row + i) for source, (g, i) in enumerate(target)]
    return lax.ppermute(values, ("groups", "row"), pairs)


def merge(first, second, rows):
    return jnp.concatenate([first[:rows], second[:rows], first[rows:] + second[rows:]], axis=0)


def gathered(n_group, n_row, pair_rep, pair_mask, *params):
    per, tokens, width = pair_rep.shape
    rows = per * tokens
    me = lax.axis_index("row")
    held = pack(n_row, pair_rep, pair_mask)
    held = merge(held, swap(held, 1, n_row), rows)
    order = [0, 1]
    step = n_row // 2
    while step > 4:
        count = len(order)
        held = merge(held, odd_swap(held, step, n_group, n_row), count * rows)
        order = order + [place ^ step for place in order]
        step //= 2
    held, *params = lax.optimization_barrier((held, *load(*params)))
    steps = [0] + list(range(2, 2 * step, 2))
    blocks = [held] + [odd_swap(held, place, n_group, n_row) for place in steps[1:]]
    even, odd = updates(Layout(n_row, order, steps, tokens), blocks, params)
    out = jnp.where(me % 2 == 1, odd, swap(even, 1, n_row))
    return out.reshape(per, tokens, width)


H = 128


def layer_norm(values, gain, offset, axis):
    mean = jnp.mean(values, axis=axis, keepdims=True)
    centered = values - mean
    variance = jnp.mean(centered * centered, axis=axis, keepdims=True)
    return centered * lax.rsqrt(variance + 1e-05) * gain + offset


def triangle(
    pair_now,
    pair_mask,
    layer_index,
    gain_in,
    shift_in,
    proj_weight,
    gate_weight,
    gain_out,
    shift_out,
    out_weight,
):
    normed = layer_norm(
        pair_now.astype(jnp.float32), gain_in[layer_index], shift_in[layer_index], -1
    ).astype(jnp.bfloat16)
    packed = jnp.einsum(
        "rnc,ch->hrn", normed, proj_weight[layer_index], preferred_element_type=jnp.float32
    )
    masked = pair_mask.astype(jnp.float32)[None, :, :]
    left = (masked * jax.nn.sigmoid(packed[0:H]) * packed[H : 2 * H]).astype(jnp.bfloat16)
    right = (masked * jax.nn.sigmoid(packed[2 * H : 3 * H]) * packed[3 * H :]).astype(jnp.bfloat16)
    gating = jax.nn.sigmoid(
        jnp.einsum(
            "rnc,cd->rnd", normed, gate_weight[layer_index], preferred_element_type=jnp.float32
        )
    )
    lifted_left, lifted_right = (
        lax.all_to_all(left, "row", split_axis=0, concat_axis=1, tiled=True),
        lax.all_to_all(right, "row", split_axis=0, concat_axis=1, tiled=True),
    )
    if layer_index == 0:
        product = jnp.einsum(
            "hik,hjk->hij", lifted_left, lifted_right, preferred_element_type=jnp.float32
        )
    else:
        product = jnp.einsum(
            "hki,hkj->hij", lifted_left, lifted_right, preferred_element_type=jnp.float32
        )
    product = product.astype(jnp.bfloat16)
    out_gain = gain_out[layer_index][:, None, None]
    out_shift = shift_out[layer_index][:, None, None]
    out_proj = out_weight[layer_index]
    returned = lax.all_to_all(product, "row", split_axis=1, concat_axis=0, tiled=True)
    scaled = layer_norm(returned.astype(jnp.float32), out_gain, out_shift, 0).astype(jnp.bfloat16)
    update = jnp.einsum("hrn,hc->rnc", scaled, out_proj, preferred_element_type=jnp.float32)
    return (pair_now.astype(jnp.float32) + gating * update).astype(jnp.bfloat16)


def exchanged(
    pair_rep,
    pair_mask,
    gain_in,
    shift_in,
    proj_weight,
    gate_weight,
    gain_out,
    shift_out,
    out_weight,
):
    current = pair_rep
    for layer_index in range(2):
        current = triangle(
            current,
            pair_mask,
            layer_index,
            gain_in,
            shift_in,
            proj_weight,
            gate_weight,
            gain_out,
            shift_out,
            out_weight,
        )
    return current


def solution(mesh):
    n_group, n_row = mesh.shape["groups"], mesh.shape["row"]

    def shards(pair_rep, *rest):
        per, tokens, _ = pair_rep.shape
        small = pair_rep.size * n_row * 2 <= GATHER_LIMIT
        fits = n_row & (n_row - 1) == 0 and n_row > 3 and tokens % 32 == 0
        if small and fits:
            return gathered(n_group, n_row, pair_rep, *rest)
        return exchanged(pair_rep, *rest)

    in_specs = (
        P(("groups", "row"), None, None),
        P(("groups", "row"), None),
        P(),
        P(),
        P(),
        P(),
        P(),
        P(),
        P(),
    )
    out_specs = P(("groups", "row"), None, None)
    return jax.shard_map(shards, mesh=mesh, in_specs=in_specs, out_specs=out_specs, check_vma=False)
```

time: 19 us -> 18.4 us (0.968)
  starting transfers between devices: 10.7 us -> 9.73 us
  Pallas kernels: 3.12 us -> 4.08 us
  waiting for transfers between devices: 4.37 us -> 3.66 us
    pallas_call x4, Pallas kernels: 1.17 us -> 2.22 us  [the longest x3 2.19 us: complete_group(): pl.pallas_call(functools.partial(group_kernel, lay, n), out_shape=[jax.Sh...]
    ppermute x2, starting transfers between devices: 3.67 us -> 2.73 us  [swap(): return lax.ppermute(values, 'row', [(i, i ^ step) for i in range(n_row)])]
    ppermute x4, waiting for transfers between devices: 2.69 us -> 1.96 us  [odd_swap(): return lax.ppermute(values, ('groups', 'row'), pairs)]
  transfers between devices with their start and end apart: 6 -> 6, of which waited for: 5 -> 4; matrix products, arithmetic and copies ran while one was open for 0% -> 0% of each run, Pallas kernels for 12% -> 18%
where the time goes in v5:
time: 18.4 us; the launch traced here: 18.2 us
  starting transfers between devices  9.73 us (53%)
  Pallas kernels  4.08 us (22%)
  waiting for transfers between devices  3.66 us (20%)
  other arithmetic  0.63 us (3%)
    ppermute x4, starting transfers between devices, odd_swap(): return lax.ppermute(values, ('groups', 'row'), pairs)  7.01 us
    ppermute x2, starting transfers between devices, swap(): return lax.ppermute(values, 'row', [(i, i ^ step) for i in range(n_row)])  2.73 us
    pallas_call x3, Pallas kernels, complete_group(): pl.pallas_call(functools.partial(group_kernel, lay, n), out_shape=[jax.Sh...  2.19 us
    ppermute x4, waiting for transfers between devices, odd_swap(): return lax.ppermute(values, ('groups', 'row'), pairs)  1.96 us
    ppermute x2, waiting for transfers between devices, swap(): return lax.ppermute(values, 'row', [(i, i ^ step) for i in range(n_row)])  1.69 us
    pallas_call x1, Pallas kernels, load(): pl.pallas_call(functools.partial(load_kernel, count), out_shape=[jax.Shap...  1.07 us
    pallas_call x1, Pallas kernels, pack(): pl.pallas_call(functools.partial(pack_kernel, n_row), out_shape=jax.Shape...  0.79 us
    select_n x1, other arithmetic, gathered(): out = jnp.where(me % 2 == 1, odd, swap(even, 1, n_row))  0.61 us
  transfers between devices with their start and end apart: 6, of which 4 were waited for; matrix products, arithmetic and copies ran while one was open for 0% of the time, Pallas kernels for 18%

profile of v5, /device:TPU:0, one launch (start us, length us, event | category | flops | bytes accessed | tf_op | source)
XLA Modules:
  0.0 18.2 jit_solution(14643753223039809229)
XLA Ops:
  0.0 0.8 %shard_map.91 = bf16[112,128]{1,0:T(8,128)(2,1)S(1)} custom-call(bf16[64,128]{1,0:T(8,128)(2,1)} %bitcast.2, s32[2,32]{1,0:T(2,128)} %mask_ref.1), custom_call_target="tpu_custom_call" | custom-call | tf_op jit(solution)/shard_map/pallas_call | solution.py:77
  0.8 0.5 %collective-permute-start = (bf16[112,128]{1,0:T(8,128)(2,1)S(1)}, bf16[112,128]{1,0:T(8,128)(2,1)S(1)}, u32[]{:S(2)}, u32[]{:S(2)}) collective-permute-start(bf16[112,128]{1,0:T(8,128)(2,1)S(1)} %shard_map.91), channel_id=1, source_target_pairs={{0,1},{1,0},{2,3},{3,2},{4,5},{5,4},{6,7},{7,6},{8,9},{9,8},{10,11... | collective-permute-start | bytes 86024 | tf_op jit(solution)/shard_map/ppermute | solution.py:314
  1.3 0.9 %collective-permute-done = bf16[112,128]{1,0:T(8,128)(2,1)S(1)} collective-permute-done((bf16[112,128]{1,0:T(8,128)(2,1)S(1)}, bf16[112,128]{1,0:T(8,128)(2,1)S(1)}, u32[]{:S(2)}, u32[]{:S(2)}) %collective-permute-start) | collective-permute-done | bytes 28704 | tf_op jit(solution)/shard_map/ppermute | solution.py:314
  2.2 2.9 %collective-permute-start.1 = (bf16[176,128]{1,0:T(8,128)(2,1)S(1)}, bf16[176,128]{1,0:T(8,128)(2,1)S(1)}, u32[]{:S(2)}, u32[]{:S(2)}) collective-permute-start(bf16[176,128]{1,0:T(8,128)(2,1)S(1)} %pad_maximum_fusion.1), channel_id=1, source_target_pairs={{0,16},{1,9},{2,18},{3,11},{4,20},{5,13},{6,22},{7,15},{8,24},{9,1... | collective-permute-start | bytes 135176 | tf_op jit(solution)/shard_map/ppermute | solution.py:322
  5.1 1.1 %shard_map.92 = (f32[2,128]{1,0:T(2,128)S(1)}, f32[2,128]{1,0:T(2,128)S(1)}, bf16[2,128,512]{2,1,0:T(8,128)(2,1)S(1)}, bf16[2,128,128]{2,1,0:T(8,128)(2,1)S(1)},...) custom-call(f32[2,128]{1,0:T(2,128)} %refs_0_.1, f32[2,128]{1,0:T(2,128)} %refs_1_.1, ...), custom_call_target="tpu_custom_call" | custom-call | tf_op jit(solution)/shard_map/pallas_call | solution.py:102
  6.2 0.9 %collective-permute-done.1 = bf16[176,128]{1,0:T(8,128)(2,1)S(1)} collective-permute-done((bf16[176,128]{1,0:T(8,128)(2,1)S(1)}, bf16[176,128]{1,0:T(8,128)(2,1)S(1)}, u32[]{:S(2)}, u32[]{:S(2)}) %collective-permute-start.1) | collective-permute-done | bytes 45088 | tf_op jit(solution)/shard_map/ppermute | solution.py:322
  7.1 2.1 %collective-permute-start.3 = (bf16[304,128]{1,0:T(8,128)(2,1)S(1)}, bf16[304,128]{1,0:T(8,128)(2,1)S(1)}, u32[]{:S(2)}, u32[]{:S(2)}) collective-permute-start(bf16[304,128]{1,0:T(8,128)(2,1)S(1)} %pad_maximum_fusion.block), channel_id=1, source_target_pairs={{0,16},{1,3},{2,18},{3,1},{4,20},{5,7},{6,22},{7,5},{8,24},{9,11},... | collective-permute-start | bytes 233480 | tf_op jit(solution)/shard_map/ppermute | solution.py:322
  9.2 0.1 collective-permute-start.4
  9.3 1.9 %collective-permute-start.2 = (bf16[304,128]{1,0:T(8,128)(2,1)S(1)}, bf16[304,128]{1,0:T(8,128)(2,1)S(1)}, u32[]{:S(2)}, u32[]{:S(2)}) collective-permute-start(bf16[304,128]{1,0:T(8,128)(2,1)S(1)} %pad_maximum_fusion.block), channel_id=1, source_target_pairs={{0,16},{1,7},{2,18},{3,5},{4,20},{5,3},{6,22},{7,1},{8,24},{9,15},... | collective-permute-start | bytes 233480 | tf_op jit(solution)/shard_map/ppermute | solution.py:322
  11.2 0.6 %shard_map.93 = (f32[320,128]{1,0:T(8,128)S(1)}, f32[256,128]{1,0:T(8,128)S(1)}, f32[256,128]{1,0:T(8,128)S(1)}, f32[256,128]{1,0:T(8,128)S(1)}, f32[8,128]{1,0:T(8,128)S(1)}, /*index=5*/f32[64,128]{1,0:T(8,128)S(1)}) custom-call(bf16[304,128]{1,0:T(8,128)(2,1)S(1)} %pad_maximum_fusion.block, ...), custom_call_target="tpu_custom_call" | custom-call | flops 42467328 | bytes 655360 | tf_op jit(solution)/shard_map/pallas_call | solution.py:205
  11.9 0.0 collective-permute-done.3.block
  11.9 0.7 %shard_map.94 = (f32[320,128]{1,0:T(8,128)S(1)}, f32[256,128]{1,0:T(8,128)S(1)}, f32[256,128]{1,0:T(8,128)S(1)}, f32[256,128]{1,0:T(8,128)S(1)}, f32[8,128]{1,0:T(8,128)S(1)}, /*index=5*/f32[192,128]{1,0:T(8,128)S(1)}) custom-call(bf16[304,128]{1,0:T(8,128)(2,1)S(1)} %collective-permute-done.3.block, f32[256,128]{1,0:T(8,128)S(1)} %get-tuple-element.53.refs_0_.refs_1_, ...), custom_call_target="tpu_custom_call" | custom-call | flops 43515904 | bytes 655360 | tf_op jit(solution)/shard_map/pallas_call | solution.py:205
  12.6 1.0 %collective-permute-done.4.block = bf16[304,128]{1,0:T(8,128)(2,1)S(1)} collective-permute-done((bf16[304,128]{1,0:T(8,128)(2,1)S(1)}, bf16[304,128]{1,0:T(8,128)(2,1)S(1)}, u32[]{:S(2)}, u32[]{:S(2)}) %collective-permute-start.4) | collective-permute-done | bytes 77856 | tf_op jit(solution)/shard_map/ppermute | solution.py:322
  13.6 0.9 %shard_map.95 = (f32[320,128]{1,0:T(8,128)S(1)}, f32[256,128]{1,0:T(8,128)S(1)}, f32[256,128]{1,0:T(8,128)S(1)}, f32[256,128]{1,0:T(8,128)S(1)}, f32[8,128]{1,0:T(8,128)S(1)}, /*index=5*/f32[320,128]{1,0:T(8,128)S(1)}) custom-call(bf16[304,128]{1,0:T(8,128)(2,1)S(1)} %collective-permute-done.4.block, f32[256,128]{1,0:T(8,128)S(1)} %get-tuple-element.53.refs_0_.refs_1_, ...), custom_call_target="tpu_custom_call" | custom-call | flops 44564480 | bytes 655360 | tf_op jit(solution)/shard_map/pallas_call | solution.py:205
  14.5 0.0 collective-permute-done.2.block
  14.5 2.2 %collective-permute-start.5 = (bf16[64,128]{1,0:T(8,128)(2,1)S(1)}, bf16[64,128]{1,0:T(8,128)(2,1)S(1)}, u32[]{:S(2)}, u32[]{:S(2)}) collective-permute-start(bf16[64,128]{1,0:T(8,128)(2,1)S(1)} %get-tuple-element.74), channel_id=1, source_target_pairs={{0,1},{1,0},{2,3},{3,2},{4,5},{5,4},{6,7},{7,6},{8,9},{9,8},{10,11... | collective-permute-start | bytes 49160 | tf_op jit(solution)/shard_map/ppermute | solution.py:314
  16.7 0.8 %collective-permute-done.5 = bf16[64,128]{1,0:T(8,128)(2,1)S(1)} collective-permute-done((bf16[64,128]{1,0:T(8,128)(2,1)S(1)}, bf16[64,128]{1,0:T(8,128)(2,1)S(1)}, u32[]{:S(2)}, u32[]{:S(2)}) %collective-permute-start.5) | collective-permute-done | bytes 16416 | tf_op jit(solution)/shard_map/ppermute | solution.py:314
  17.6 0.6 %broadcast_select_fusion = bf16[64,128]{1,0:T(8,128)(2,1)} fusion(bf16[64,128]{1,0:T(8,128)(2,1)S(1)} %get-tuple-element.73, bf16[64,128]{1,0:T(8,128)(2,1)S(1)} %collective-permute-done.5, pred[]{:T(512)S(6)} %eq.5), kind=kLoop, calls=%fused_computation.2 | loop fusion | flops 8192 | bytes 49153 | tf_op jit(solution)/shard_map/jit(_where)/select_n | solution.py:346
  (8 shorter events, 0.1 us)
Async XLA Ops:
  0.8 1.4 %collective-permute-start = (bf16[112,128]{1,0:T(8,128)(2,1)S(1)}, bf16[112,128]{1,0:T(8,128)(2,1)S(1)}, u32[]{:S(2)}, u32[]{:S(2)}) collective-permute-start(bf16[112,128]{1,0:T(8,128)(2,1)S(1)} %shard_map.91), channel_id=1, source_target_pairs={{0,1},{1,0},{2,3},{3,2},{4,5},{5,4},{6,7},{7,6},{8,9},{9,8},{10,11... | collective-permute-start | bytes 86024 | tf_op jit(solution)/shard_map/ppermute | solution.py:314
  2.2 4.9 %collective-permute-start.1 = (bf16[176,128]{1,0:T(8,128)(2,1)S(1)}, bf16[176,128]{1,0:T(8,128)(2,1)S(1)}, u32[]{:S(2)}, u32[]{:S(2)}) collective-permute-start(bf16[176,128]{1,0:T(8,128)(2,1)S(1)} %pad_maximum_fusion.1), channel_id=1, source_target_pairs={{0,16},{1,9},{2,18},{3,11},{4,20},{5,13},{6,22},{7,15},{8,24},{9,1... | collective-permute-start | bytes 135176 | tf_op jit(solution)/shard_map/ppermute | solution.py:322
  7.1 4.7 %collective-permute-start.3 = (bf16[304,128]{1,0:T(8,128)(2,1)S(1)}, bf16[304,128]{1,0:T(8,128)(2,1)S(1)}, u32[]{:S(2)}, u32[]{:S(2)}) collective-permute-start(bf16[304,128]{1,0:T(8,128)(2,1)S(1)} %pad_maximum_fusion.block), channel_id=1, source_target_pairs={{0,16},{1,3},{2,18},{3,1},{4,20},{5,7},{6,22},{7,5},{8,24},{9,11},... | collective-permute-start | bytes 233480 | tf_op jit(solution)/shard_map/ppermute | solution.py:322
  9.2 4.4 %collective-permute-start.4 = (bf16[304,128]{1,0:T(8,128)(2,1)S(1)}, bf16[304,128]{1,0:T(8,128)(2,1)S(1)}, u32[]{:S(2)}, u32[]{:S(2)}) collective-permute-start(bf16[304,128]{1,0:T(8,128)(2,1)S(1)} %pad_maximum_fusion.block), channel_id=1, source_target_pairs={{0,16},{1,5},{2,18},{3,7},{4,20},{5,1},{6,22},{7,3},{8,24},{9,13},... | collective-permute-start | bytes 233480 | tf_op jit(solution)/shard_map/ppermute | solution.py:322
  9.3 5.2 %collective-permute-start.2 = (bf16[304,128]{1,0:T(8,128)(2,1)S(1)}, bf16[304,128]{1,0:T(8,128)(2,1)S(1)}, u32[]{:S(2)}, u32[]{:S(2)}) collective-permute-start(bf16[304,128]{1,0:T(8,128)(2,1)S(1)} %pad_maximum_fusion.block), channel_id=1, source_target_pairs={{0,16},{1,7},{2,18},{3,5},{4,20},{5,3},{6,22},{7,1},{8,24},{9,15},... | collective-permute-start | bytes 233480 | tf_op jit(solution)/shard_map/ppermute | solution.py:322
  14.5 3.0 %collective-permute-start.5 = (bf16[64,128]{1,0:T(8,128)(2,1)S(1)}, bf16[64,128]{1,0:T(8,128)(2,1)S(1)}, u32[]{:S(2)}, u32[]{:S(2)}) collective-permute-start(bf16[64,128]{1,0:T(8,128)(2,1)S(1)} %get-tuple-element.74), channel_id=1, source_target_pairs={{0,1},{1,0},{2,3},{3,2},{4,5},{5,4},{6,7},{7,6},{8,9},{9,8},{10,11... | collective-permute-start | bytes 49160 | tf_op jit(solution)/shard_map/ppermute | solution.py:314

commit v6 on v5

--- a/solution.py
+++ b/solution.py
@@ -12,15 +12,15 @@
 GATHER_LIMIT = 4 << 20
 
 
-def norm_rows(values, gain, offset):
-    mean = jnp.mean(values, axis=-1, keepdims=True)
-    centered = values - mean
-    variance = jnp.mean(centered * centered, axis=-1, keepdims=True)
-    return (centered * lax.rsqrt(variance + EPS) * gain + offset).astype(jnp.bfloat16)
-
-
 def matmul(left, right):
     return jnp.dot(left, right, preferred_element_type=jnp.float32)
+
+
+def normed_matmul(values, gain, weights, biases):
+    centered = values - jnp.mean(values, axis=-1, keepdims=True)
+    scale = lax.rsqrt(jnp.mean(centered * centered, axis=-1, keepdims=True) + EPS)
+    factor = (centered * gain).astype(jnp.bfloat16)
+    return [matmul(factor, weight) * scale + bias for weight, bias in zip(weights, biases, strict=True)]
 
 
 def gated(packed, width):
@@ -49,15 +49,13 @@
     part.start()
     whole.start()
     first = seat(lax.axis_index("row"), n_row) * per
+    last = seats(n_row) * per
     marks[...] = jnp.zeros_like(marks)
-    diagonal = lax.broadcasted_iota(jnp.int32, (tokens, tokens), 0)
-    diagonal = diagonal == lax.broadcasted_iota(jnp.int32, (tokens, tokens), 1)
     part.wait()
     mine = mask[...].astype(jnp.float32)
     marks[pl.ds(first, per), :] = jnp.broadcast_to(jnp.max(mine, axis=1, keepdims=True), (per, width))
-    seen = jnp.where(diagonal, jnp.max(mine, axis=0, keepdims=True), 0.0)
-    seen = jnp.broadcast_to(jnp.sum(seen, axis=1, keepdims=True), (tokens, width))
-    out_ref[rows:, :] = jnp.concatenate([marks[...], seen], axis=0).astype(jnp.bfloat16)
+    marks[last : last + 1, 0:tokens] = jnp.max(mine, axis=0, keepdims=True)
+    out_ref[rows:, :] = marks[...].astype(jnp.bfloat16)
     whole.wait()
 
 
@@ -66,7 +64,7 @@
 
 
 def mark_rows(n_row, per):
-    return -(-seats(n_row) * per // MARK_ROWS) * MARK_ROWS
+    return -(-(seats(n_row) * per + 1) // MARK_ROWS) * MARK_ROWS
 
 
 def pack(n_row, pair_rep, pair_mask):
@@ -76,7 +74,7 @@
     hbm = pl.BlockSpec(memory_space=pltpu.HBM)
     return pl.pallas_call(
         functools.partial(pack_kernel, n_row),
-        out_shape=jax.ShapeDtypeStruct((rows + extra + tokens, width), jnp.bfloat16),
+        out_shape=jax.ShapeDtypeStruct((rows + extra, width), jnp.bfloat16),
         in_specs=[hbm, hbm],
         out_specs=pl.BlockSpec(memory_space=pltpu.VMEM),
         scratch_shapes=[
@@ -88,23 +86,54 @@
     )(hold(pair_rep.reshape(rows, width)), hold(pair_mask))
 
 
-def load_kernel(count, *refs):
-    sources, targets, sems = refs[:count], refs[count : 2 * count], refs[2 * count]
-    copies = [pltpu.make_async_copy(s, t, sems.at[n]) for n, (s, t) in enumerate(zip(sources, targets, strict=True))]
+def load_kernel(sources, targets):
+    (gain_in, shift_in, proj, gate, gain_out, shift_out, out), sems = sources[:7], sources[-1]
+    held = sources[7:-1]
+    copies = [
+        pltpu.make_async_copy(source, target, sems.at[n])
+        for n, (source, target) in enumerate(
+            zip((proj, gate, out, shift_in, shift_out, gain_in, gain_out), (*held, targets[0], targets[1]), strict=True)
+        )
+    ]
     for copy in copies:
         copy.start()
     for copy in copies:
         copy.wait()
-
-
-def load(*arrays):
-    count = len(arrays)
+    proj, gate, out, shift_in, shift_out = held
+    _, _, proj_half, gate_half, out_half, proj_bias, gate_bias, out_bias = targets
+    half = jnp.array(0.5, jnp.bfloat16)
+    for weight, halved, bias, shift in (
+        (proj, proj_half, proj_bias, shift_in),
+        (gate, gate_half, gate_bias, shift_in),
+        (out, out_half, out_bias, shift_out),
+    ):
+        halved[...] = weight[...] * half
+        exact = shift[...]
+        high = exact.astype(jnp.bfloat16)
+        low = (exact - high.astype(jnp.float32)).astype(jnp.bfloat16)
+        rows = jnp.concatenate([high, low] + [jnp.zeros_like(high)] * 6, axis=0)
+        for u in range(2):
+            both = matmul(rows, weight[u])
+            bias[u : u + 1, :] = 0.5 * (both[u : u + 1, :] + both[u + 2 : u + 3, :])
+
+
+def load(gain_in, shift_in, proj, gate, gain_out, shift_out, out):
+    arrays = (gain_in, shift_in, proj, gate, gain_out, shift_out, out)
+    weights = (proj, gate, out)
+    shapes = [(a.shape, a.dtype) for a in (gain_in, gain_out, *weights)]
+    shapes += [((a.shape[0], a.shape[2]), jnp.float32) for a in weights]
+    vmem = pl.BlockSpec(memory_space=pltpu.VMEM)
+
+    def kernel(*refs):
+        load_kernel((*refs[:7], *refs[7 + len(shapes) :]), refs[7 : 7 + len(shapes)])
+
     return pl.pallas_call(
-        functools.partial(load_kernel, count),
-        out_shape=[jax.ShapeDtypeStruct(a.shape, a.dtype) for a in arrays],
-        in_specs=[pl.BlockSpec(memory_space=pltpu.HBM)] * count,
-        out_specs=[pl.BlockSpec(memory_space=pltpu.VMEM)] * count,
-        scratch_shapes=[pltpu.SemaphoreType.DMA((count,))],
+        kernel,
+        out_shape=[jax.ShapeDtypeStruct(*shape) for shape in shapes],
+        in_specs=[pl.BlockSpec(memory_space=pltpu.HBM)] * len(arrays),
+        out_specs=[vmem] * len(shapes),
+        scratch_shapes=[pltpu.VMEM(a.shape, a.dtype) for a in (*weights, shift_in, shift_out)]
+        + [pltpu.SemaphoreType.DMA((len(arrays),))],
         compiler_params=pltpu.CompilerParams(vmem_limit_bytes=4 << 20),
     )(*[hold(a) for a in arrays])
 
@@ -117,6 +146,7 @@
         self.chunk = self.group * tokens
         self.pitch = tokens + 8
         self.marks = mark_rows(n_row, self.per)
+        self.column_marks = seats(n_row) * self.per
 
     def places(self):
         me = lax.axis_index("row")
@@ -128,16 +158,20 @@
         return [(n, q) for q in range(n + 1)] + [(p, n) for p in range(n)]
 
 
-def prepare(lay, n, block, gain_in, shift_in, proj_weight, gate_weight, outs, scratch):
-    z, left, right, gate, near = outs
-    marks, rough, seen = scratch
+def prepare(lay, n, block, gain, proj, gate_weight, proj_bias, gate_bias, outs, scratch):
+    z, left, right_t, gate, near = outs
+    marks, rough, right, columns, seen = scratch
     tokens, group, per, chunk, pitch = lay.tokens, lay.group, lay.per, lay.chunk, lay.pitch
     width = z.shape[-1]
-    half = jnp.array(0.5, jnp.bfloat16)
     places = list(lay.places())
     marks[...] = block[chunk:, :].astype(jnp.float32)
+    diagonal = lax.broadcasted_iota(jnp.int32, (tokens, tokens), 0)
+    diagonal = diagonal == lax.broadcasted_iota(jnp.int32, (tokens, tokens), 1)
+    row = jnp.minimum(marks[lay.column_marks : lay.column_marks + 1, 0:tokens], 1.0)
+    column = jnp.sum(jnp.where(diagonal, row, 0.0), axis=1, keepdims=True)
+    columns[...] = jnp.broadcast_to(column, (tokens, width))
     for first, at in places:
-        seen[first : first + per, :] = jnp.minimum(marks[pl.ds(lay.marks + at * per, per), :], 1.0)
+        seen[first : first + per, :] = columns[pl.ds(at * per, per), :]
     for first, at in places[n * len(lay.order) : (n + 1) * len(lay.order)]:
         near[first - n * group : first - n * group + per, :] = marks[pl.ds(seat(at, lay.n_row) * per, per), :]
     for t in range(group):
@@ -146,15 +180,16 @@
         for t in range(per):
             z[pl.ds(first + t, group, stride=pitch), :] = rough[pl.ds(at * per + t, group, stride=pitch), :]
     values = jnp.concatenate([z[t * pitch : t * pitch + tokens, :] for t in range(group)], axis=0)
-    normed = norm_rows(values, gain_in[0:1, :], shift_in[0:1, :])
-    packed = matmul(normed, proj_weight[0] * half)
-    rights = gated(packed[:, 2 * width :], width)
+    packed, gates = normed_matmul(
+        values, gain[0:1, :], (proj[0], gate_weight[0]), (proj_bias[0:1, :], gate_bias[0:1, :])
+    )
+    left[...] = gated(packed[:, 0 : 2 * width], width)
+    value = gated(packed[:, 2 * width :], width)
     for t in range(group):
-        rough[t * pitch : t * pitch + tokens, :] = rights[t * tokens : (t + 1) * tokens, :]
-    left[...] = gated(packed[:, 0 : 2 * width], width)
+        right[t * pitch : t * pitch + tokens, :] = value[t * tokens : (t + 1) * tokens, :]
     for k in range(tokens):
-        right[k * group : (k + 1) * group, :] = rough[pl.ds(k, group, stride=pitch), :] * seen[k : k + 1, :]
-    gate[...] = jnp.tanh(matmul(normed, gate_weight[0] * half)) + 1.0
+        right_t[k * group : (k + 1) * group, :] = right[pl.ds(k, group, stride=pitch), :] * seen[k : k + 1, :]
+    gate[...] = jnp.tanh(gates) + 1.0
 
 
 def block_sums(lay, left, rights):
@@ -181,7 +216,7 @@
 
 def group_kernel(lay, n, block, *refs):
     lefts, rights, refs = refs[:n], refs[n : 2 * n], refs[2 * n :]
-    params, outs, sums, scratch = refs[:4], refs[4:9], refs[9], refs[10:]
+    params, outs, sums, scratch = refs[:5], refs[5:10], refs[10], refs[11:]
     prepare(lay, n, block, *params, outs, scratch)
     complete(lay, n, [*lefts, outs[1]], [*rights, outs[2]], sums)
 
@@ -193,7 +228,7 @@
 
 
 def scratch_shapes(lay, width):
-    rows = [lay.marks + lay.tokens, lay.group * lay.pitch, lay.tokens]
+    rows = [lay.marks] + [lay.group * lay.pitch] * 2 + [lay.tokens] * 2
     return [pltpu.VMEM((r, width), jnp.float32) for r in rows]
 
 
@@ -205,7 +240,7 @@
     return pl.pallas_call(
         functools.partial(group_kernel, lay, n),
         out_shape=[jax.ShapeDtypeStruct(shape, jnp.float32) for shape in shapes],
-        in_specs=[vmem] * (5 + 2 * n),
+        in_specs=[vmem] * (1 + 2 * n + len(params)),
         out_specs=[vmem] * len(shapes),
         scratch_shapes=scratch_shapes(lay, width),
         cost_estimate=pl.CostEstimate(
@@ -221,22 +256,20 @@
     last = len(lay.steps) - 1
     done = [refs[6 * n : 6 * n + 6] for n in range(last)]
     refs = refs[6 * last :]
-    gain_in, shift_in, proj_weight, gate_weight, gain_out, shift_out, out_weight = refs[:7]
-    out_even, out_odd = refs[7:9]
-    own, scratch = refs[9:15], refs[15:18]
-    right1, middle, left1, result1 = refs[18:]
+    gain_in, gain_out, proj, gate_weight, out_weight, proj_bias, gate_bias, out_bias = refs[:8]
+    out_even, out_odd = refs[8:10]
+    own, scratch = refs[10:16], refs[16:21]
+    right1, middle, left1, result1 = refs[21:]
     tokens, per, group, chunk, pitch = lay.tokens, lay.per, lay.group, lay.chunk, lay.pitch
     width = out_even.shape[-1]
     rows = per * tokens
     done = done + [own]
 
     def run():
-        prepare(lay, last, block, gain_in, shift_in, proj_weight, gate_weight, own[:5], scratch)
+        prepare(lay, last, block, gain_in, proj, gate_weight, proj_bias, gate_bias, own[:5], scratch)
         complete(lay, last, [arrays[1] for arrays in done], [arrays[2] for arrays in done], own[5])
 
-        half = jnp.array(0.5, jnp.bfloat16)
         real = jnp.concatenate([arrays[4][...] for arrays in done], axis=0)
-        gate_out = out_weight[0] * half
         for p in range(last + 1):
             z, _, _, gate, near, _ = done[p]
             products = []
@@ -247,20 +280,24 @@
                     start = (lay.pairs(n).index((p, q)) * group + i) * group
                     parts.append(done[n][5][start : start + group, :])
                 products.append(jnp.concatenate(parts, axis=0) * (real * near[i : i + 1, :]))
-            scaled = norm_rows(jnp.concatenate(products, axis=0), gain_out[0:1, :], shift_out[0:1, :])
+            products = jnp.concatenate(products, axis=0)
+            (change,) = normed_matmul(products, gain_out[0:1, :], (out_weight[0],), (out_bias[0:1, :],))
             held = jnp.concatenate([z[t * pitch : t * pitch + tokens, :] for t in range(group)], axis=0)
-            middle[p * chunk : (p + 1) * chunk, :] = held + gate[...] * matmul(scaled, gate_out)
-
-        proj, gate_in, gate_out = proj_weight[1] * half, gate_weight[1] * half, out_weight[1] * half
+            middle[p * chunk : (p + 1) * chunk, :] = held + gate[...] * change
+
         for p in range(last + 1):
             at = slice(p * chunk, (p + 1) * chunk)
-            normed = norm_rows(middle[at, :], gain_in[1:2, :], shift_in[1:2, :])
-            right1[at, :] = gated(matmul(normed, proj[:, 2 * width :]), width)
+            (packed,) = normed_matmul(
+                middle[at, :], gain_in[1:2, :], (proj[1, :, 2 * width :],), (proj_bias[1:2, 2 * width :],)
+            )
+            right1[at, :] = gated(packed, width)
 
         ours = [*range(per, 2 * per), *range(per)]
         columns = jnp.concatenate([middle[pl.ds(r, tokens, stride=tokens), :] for r in ours], axis=0)
-        normed = norm_rows(columns, gain_in[1:2, :], shift_in[1:2, :])
-        left1[...] = gated(matmul(normed, proj[:, 0 : 2 * width]), width) * jnp.concatenate([real] * len(ours), axis=0)
+        (packed,) = normed_matmul(
+            columns, gain_in[1:2, :], (proj[1, :, 0 : 2 * width],), (proj_bias[1:2, 0 : 2 * width],)
+        )
+        left1[...] = gated(packed, width) * jnp.concatenate([real] * len(ours), axis=0)
         totals = [jnp.zeros((tokens, width), jnp.float32)] * len(ours)
         for k in range(tokens):
             row = right1[k * tokens : (k + 1) * tokens, :]
@@ -268,10 +305,10 @@
                 totals[r] = totals[r] + left1[r * tokens + k : r * tokens + k + 1, :] * row
         near = done[0][4]
         product = jnp.concatenate([t * (real * near[r : r + 1, :]) for r, t in zip(ours, totals, strict=True)], axis=0)
-        scaled = norm_rows(product, gain_out[1:2, :], shift_out[1:2, :])
+        (change,) = normed_matmul(product, gain_out[1:2, :], (out_weight[1],), (out_bias[1:2, :],))
         held = jnp.concatenate([middle[rows : 2 * rows, :], middle[0:rows, :]], axis=0)
-        gate = jnp.tanh(matmul(norm_rows(held, gain_in[1:2, :], shift_in[1:2, :]), gate_in)) + 1.0
-        result = held + gate * matmul(scaled, gate_out)
+        (gates,) = normed_matmul(held, gain_in[1:2, :], (gate_weight[1],), (gate_bias[1:2, :],))
+        result = held + (jnp.tanh(gates) + 1.0) * change
         rough = scratch[1]
         for r in range(len(ours)):
             rough[r * pitch : r * pitch + tokens, :] = result[r * tokens : (r + 1) * tokens, :]
@@ -290,10 +327,12 @@
     width = blocks[0].shape[-1]
     rows = lay.per * lay.tokens
     pairs = lay.tokens * lay.tokens
+    gain_in, _, proj, gate_weight, _, proj_bias, gate_bias, _ = params
+    group_params = (gain_in, proj, gate_weight, proj_bias, gate_bias)
     done = []
     for n, block in enumerate(blocks[:-1]):
         lefts, rights = [arrays[1] for arrays in done], [arrays[2] for arrays in done]
-        done.append(complete_group(lay, n, block, lefts, rights, params[:4]))
+        done.append(complete_group(lay, n, block, lefts, rights, group_params))
     arrays = [array for arrays in done for array in arrays]
     vmem = pl.BlockSpec(memory_space=pltpu.VMEM)
     shapes = group_shapes(lay, len(blocks) - 1, width)
@@ -301,7 +340,7 @@
     return pl.pallas_call(
         functools.partial(updates_kernel, lay),
         out_shape=[jax.ShapeDtypeStruct((rows, width), jnp.bfloat16)] * 2,
-        in_specs=[vmem] * (1 + len(arrays) + 7),
+        in_specs=[vmem] * (1 + len(arrays) + len(params)),
         out_specs=[vmem] * 2,
         scratch_shapes=[pltpu.VMEM(shape, jnp.float32) for shape in shapes]
         + scratch_shapes(lay, width)
@@ -341,6 +380,7 @@
         step //= 2
     held, *params = lax.optimization_barrier((held, *load(*params)))
     steps = [0] + list(range(2, 2 * step, 2))
+    steps[2:] = reversed(steps[2:])
     blocks = [held] + [odd_swap(held, place, n_group, n_row) for place in steps[1:]]
     even, odd = updates(Layout(n_row, order, steps, tokens), blocks, params)
     out = jnp.where(me % 2 == 1, odd, swap(even, 1, n_row))
@@ -439,7 +479,7 @@
     def shards(pair_rep, *rest):
         per, tokens, _ = pair_rep.shape
         small = pair_rep.size * n_row * 2 <= GATHER_LIMIT
-        fits = n_row & (n_row - 1) == 0 and n_row > 3 and tokens % 32 == 0
+        fits = n_row & (n_row - 1) == 0 and n_row > 3 and tokens % 32 == 0 and tokens <= pair_rep.shape[2]
         if small and fits:
             return gathered(n_group, n_row, pair_rep, *rest)
         return exchanged(pair_rep, *rest)

time: 18.4 us -> 17.5 us (0.951)
  starting transfers between devices: 9.73 us -> 9.1 us
    ppermute x2, starting transfers between devices: 2.73 us -> 2.1 us  [swap(): return lax.ppermute(values, 'row', [(i, i ^ step) for i in range(n_row)])]
    pallas_call x3, Pallas kernels: 2.19 us -> 1.92 us  [complete_group(): pl.pallas_call(functools.partial(group_kernel, lay, n), out_shape=[jax.Sh...]
where the time goes in v6:
time: 17.5 us; the launch traced here: 17.3 us
  starting transfers between devices  9.1 us (52%)
  Pallas kernels  3.98 us (23%)
  waiting for transfers between devices  3.52 us (20%)
  other arithmetic  0.63 us (4%)
    ppermute x4, starting transfers between devices, odd_swap(): return lax.ppermute(values, ('groups', 'row'), pairs)  7.01 us
    ppermute x2, starting transfers between devices, swap(): return lax.ppermute(values, 'row', [(i, i ^ step) for i in range(n_row)])  2.1 us
    pallas_call x3, Pallas kernels, complete_group(): pl.pallas_call(functools.partial(group_kernel, lay, n), out_shape=[jax.Sh...  1.92 us
    ppermute x4, waiting for transfers between devices, odd_swap(): return lax.ppermute(values, ('groups', 'row'), pairs)  1.84 us
    ppermute x2, waiting for transfers between devices, swap(): return lax.ppermute(values, 'row', [(i, i ^ step) for i in range(n_row)])  1.68 us
    pallas_call x1, Pallas kernels, load(): pl.pallas_call(kernel, out_shape=[jax.ShapeDtypeStruct(*shape) for shape...  1.25 us
    pallas_call x1, Pallas kernels, pack(): pl.pallas_call(functools.partial(pack_kernel, n_row), out_shape=jax.Shape...  0.78 us
    select_n x1, other arithmetic, gathered(): out = jnp.where(me % 2 == 1, odd, swap(even, 1, n_row))  0.61 us
  transfers between devices with their start and end apart: 6, of which 4 were waited for; matrix products, arithmetic and copies ran while one was open for 0% of the time, Pallas kernels for 18%

profile of v6, /device:TPU:0, one launch (start us, length us, event | category | flops | bytes accessed | tf_op | source)
XLA Modules:
  0.0 17.3 jit_solution(15713360463505486223)
XLA Ops:
  0.0 0.8 %shard_map.91 = bf16[80,128]{1,0:T(8,128)(2,1)S(1)} custom-call(bf16[64,128]{1,0:T(8,128)(2,1)} %bitcast.2, s32[2,32]{1,0:T(2,128)} %mask_ref.1), custom_call_target="tpu_custom_call" | custom-call | tf_op jit(solution)/shard_map/pallas_call | solution.py:75
  0.8 0.5 %collective-permute-start = (bf16[80,128]{1,0:T(8,128)(2,1)S(1)}, bf16[80,128]{1,0:T(8,128)(2,1)S(1)}, u32[]{:S(2)}, u32[]{:S(2)}) collective-permute-start(bf16[80,128]{1,0:T(8,128)(2,1)S(1)} %shard_map.91), channel_id=1, source_target_pairs={{0,1},{1,0},{2,3},{3,2},{4,5},{5,4},{6,7},{7,6},{8,9},{9,8},{10,11... | collective-permute-start | bytes 61448 | tf_op jit(solution)/shard_map/ppermute | solution.py:353
  1.3 0.8 %collective-permute-done = bf16[80,128]{1,0:T(8,128)(2,1)S(1)} collective-permute-done((bf16[80,128]{1,0:T(8,128)(2,1)S(1)}, bf16[80,128]{1,0:T(8,128)(2,1)S(1)}, u32[]{:S(2)}, u32[]{:S(2)}) %collective-permute-start) | collective-permute-done | bytes 20512 | tf_op jit(solution)/shard_map/ppermute | solution.py:353
  2.2 2.9 %collective-permute-start.1 = (bf16[144,128]{1,0:T(8,128)(2,1)S(1)}, bf16[144,128]{1,0:T(8,128)(2,1)S(1)}, u32[]{:S(2)}, u32[]{:S(2)}) collective-permute-start(bf16[144,128]{1,0:T(8,128)(2,1)S(1)} %pad_maximum_fusion.1), channel_id=1, source_target_pairs={{0,16},{1,9},{2,18},{3,11},{4,20},{5,13},{6,22},{7,15},{8,24},{9,1... | collective-permute-start | bytes 110600 | tf_op jit(solution)/shard_map/ppermute | solution.py:361
  5.1 1.2 %shard_map.92 = (f32[2,128]{1,0:T(2,128)S(1)}, f32[2,128]{1,0:T(2,128)S(1)}, bf16[2,128,512]{2,1,0:T(8,128)(2,1)S(1)}, bf16[2,128,128]{2,1,0:T(8,128)(2,1)S(1)},...) custom-call(f32[2,128]{1,0:T(2,128)} %refs_0_.1, ...), custom_call_target="tpu_custom_call" | custom-call | tf_op jit(solution)/shard_map/pallas_call | solution.py:130
  6.3 0.7 %collective-permute-done.1 = bf16[144,128]{1,0:T(8,128)(2,1)S(1)} collective-permute-done((bf16[144,128]{1,0:T(8,128)(2,1)S(1)}, bf16[144,128]{1,0:T(8,128)(2,1)S(1)}, u32[]{:S(2)}, u32[]{:S(2)}) %collective-permute-start.1) | collective-permute-done | bytes 36896 | tf_op jit(solution)/shard_map/ppermute | solution.py:361
  7.0 2.1 %collective-permute-start.3 = (bf16[272,128]{1,0:T(8,128)(2,1)S(1)}, bf16[272,128]{1,0:T(8,128)(2,1)S(1)}, u32[]{:S(2)}, u32[]{:S(2)}) collective-permute-start(bf16[272,128]{1,0:T(8,128)(2,1)S(1)} %pad_maximum_fusion.block), channel_id=1, source_target_pairs={{0,16},{1,3},{2,18},{3,1},{4,20},{5,7},{6,22},{7,5},{8,24},{9,11},... | collective-permute-start | bytes 208904 | tf_op jit(solution)/shard_map/ppermute | solution.py:361
  9.1 0.1 collective-permute-start.4
  9.2 1.9 %collective-permute-start.2 = (bf16[272,128]{1,0:T(8,128)(2,1)S(1)}, bf16[272,128]{1,0:T(8,128)(2,1)S(1)}, u32[]{:S(2)}, u32[]{:S(2)}) collective-permute-start(bf16[272,128]{1,0:T(8,128)(2,1)S(1)} %pad_maximum_fusion.block), channel_id=1, source_target_pairs={{0,16},{1,5},{2,18},{3,7},{4,20},{5,1},{6,22},{7,3},{8,24},{9,13},... | collective-permute-start | bytes 208904 | tf_op jit(solution)/shard_map/ppermute | solution.py:361
  11.1 0.5 %shard_map.93 = (f32[320,128]{1,0:T(8,128)S(1)}, f32[256,128]{1,0:T(8,128)S(1)}, f32[256,128]{1,0:T(8,128)S(1)}, f32[256,128]{1,0:T(8,128)S(1)}, f32[8,128]{1,0:T(8,128)S(1)}, /*index=5*/f32[64,128]{1,0:T(8,128)S(1)}) custom-call(bf16[272,128]{1,0:T(8,128)(2,1)S(1)} %pad_maximum_fusion.block, ...), custom_call_target="tpu_custom_call" | custom-call | flops 42467328 | bytes 655360 | tf_op jit(solution)/shard_map/pallas_call | solution.py:240
  11.6 0.0 collective-permute-done.3.block
  11.6 0.6 %shard_map.94 = (f32[320,128]{1,0:T(8,128)S(1)}, f32[256,128]{1,0:T(8,128)S(1)}, f32[256,128]{1,0:T(8,128)S(1)}, f32[256,128]{1,0:T(8,128)S(1)}, f32[8,128]{1,0:T(8,128)S(1)}, /*index=5*/f32[192,128]{1,0:T(8,128)S(1)}) custom-call(bf16[272,128]{1,0:T(8,128)(2,1)S(1)} %collective-permute-done.3.block, f32[256,128]{1,0:T(8,128)S(1)} %get-tuple-element.57.refs_0_.refs_1_, ...), custom_call_target="tpu_custom_call" | custom-call | flops 43515904 | bytes 655360 | tf_op jit(solution)/shard_map/pallas_call | solution.py:240
  12.3 1.2 %collective-permute-done.4.block = bf16[272,128]{1,0:T(8,128)(2,1)S(1)} collective-permute-done((bf16[272,128]{1,0:T(8,128)(2,1)S(1)}, bf16[272,128]{1,0:T(8,128)(2,1)S(1)}, u32[]{:S(2)}, u32[]{:S(2)}) %collective-permute-start.4) | collective-permute-done | bytes 69664 | tf_op jit(solution)/shard_map/ppermute | solution.py:361
  13.4 0.8 %shard_map.95 = (f32[320,128]{1,0:T(8,128)S(1)}, f32[256,128]{1,0:T(8,128)S(1)}, f32[256,128]{1,0:T(8,128)S(1)}, f32[256,128]{1,0:T(8,128)S(1)}, f32[8,128]{1,0:T(8,128)S(1)}, /*index=5*/f32[320,128]{1,0:T(8,128)S(1)}) custom-call(bf16[272,128]{1,0:T(8,128)(2,1)S(1)} %collective-permute-done.4.block, f32[256,128]{1,0:T(8,128)S(1)} %get-tuple-element.57.refs_0_.refs_1_, ...), custom_call_target="tpu_custom_call" | custom-call | flops 44564480 | bytes 655360 | tf_op jit(solution)/shard_map/pallas_call | solution.py:240
  14.2 0.0 collective-permute-done.2.block
  14.3 1.6 %collective-permute-start.5 = (bf16[64,128]{1,0:T(8,128)(2,1)S(1)}, bf16[64,128]{1,0:T(8,128)(2,1)S(1)}, u32[]{:S(2)}, u32[]{:S(2)}) collective-permute-start(bf16[64,128]{1,0:T(8,128)(2,1)S(1)} %get-tuple-element.78), channel_id=1, source_target_pairs={{0,1},{1,0},{2,3},{3,2},{4,5},{5,4},{6,7},{7,6},{8,9},{9,8},{10,11... | collective-permute-start | bytes 49160 | tf_op jit(solution)/shard_map/ppermute | solution.py:353
  15.9 0.8 %collective-permute-done.5 = bf16[64,128]{1,0:T(8,128)(2,1)S(1)} collective-permute-done((bf16[64,128]{1,0:T(8,128)(2,1)S(1)}, bf16[64,128]{1,0:T(8,128)(2,1)S(1)}, u32[]{:S(2)}, u32[]{:S(2)}) %collective-permute-start.5) | collective-permute-done | bytes 16416 | tf_op jit(solution)/shard_map/ppermute | solution.py:353
  16.7 0.6 %broadcast_select_fusion = bf16[64,128]{1,0:T(8,128)(2,1)} fusion(bf16[64,128]{1,0:T(8,128)(2,1)S(1)} %get-tuple-element.77, bf16[64,128]{1,0:T(8,128)(2,1)S(1)} %collective-permute-done.5, pred[]{:T(512)S(6)} %eq.5), kind=kLoop, calls=%fused_computation.2 | loop fusion | flops 8192 | bytes 49153 | tf_op jit(solution)/shard_map/jit(_where)/select_n | solution.py:386
  (8 shorter events, 0.1 us)
Async XLA Ops:
  0.8 1.4 %collective-permute-start = (bf16[80,128]{1,0:T(8,128)(2,1)S(1)}, bf16[80,128]{1,0:T(8,128)(2,1)S(1)}, u32[]{:S(2)}, u32[]{:S(2)}) collective-permute-start(bf16[80,128]{1,0:T(8,128)(2,1)S(1)} %shard_map.91), channel_id=1, source_target_pairs={{0,1},{1,0},{2,3},{3,2},{4,5},{5,4},{6,7},{7,6},{8,9},{9,8},{10,11... | collective-permute-start | bytes 61448 | tf_op jit(solution)/shard_map/ppermute | solution.py:353
  2.2 4.8 %collective-permute-start.1 = (bf16[144,128]{1,0:T(8,128)(2,1)S(1)}, bf16[144,128]{1,0:T(8,128)(2,1)S(1)}, u32[]{:S(2)}, u32[]{:S(2)}) collective-permute-start(bf16[144,128]{1,0:T(8,128)(2,1)S(1)} %pad_maximum_fusion.1), channel_id=1, source_target_pairs={{0,16},{1,9},{2,18},{3,11},{4,20},{5,13},{6,22},{7,15},{8,24},{9,1... | collective-permute-start | bytes 110600 | tf_op jit(solution)/shard_map/ppermute | solution.py:361
  7.0 4.6 %collective-permute-start.3 = (bf16[272,128]{1,0:T(8,128)(2,1)S(1)}, bf16[272,128]{1,0:T(8,128)(2,1)S(1)}, u32[]{:S(2)}, u32[]{:S(2)}) collective-permute-start(bf16[272,128]{1,0:T(8,128)(2,1)S(1)} %pad_maximum_fusion.block), channel_id=1, source_target_pairs={{0,16},{1,3},{2,18},{3,1},{4,20},{5,7},{6,22},{7,5},{8,24},{9,11},... | collective-permute-start | bytes 208904 | tf_op jit(solution)/shard_map/ppermute | solution.py:361
  9.1 4.3 %collective-permute-start.4 = (bf16[272,128]{1,0:T(8,128)(2,1)S(1)}, bf16[272,128]{1,0:T(8,128)(2,1)S(1)}, u32[]{:S(2)}, u32[]{:S(2)}) collective-permute-start(bf16[272,128]{1,0:T(8,128)(2,1)S(1)} %pad_maximum_fusion.block), channel_id=1, source_target_pairs={{0,16},{1,7},{2,18},{3,5},{4,20},{5,3},{6,22},{7,1},{8,24},{9,15},... | collective-permute-start | bytes 208904 | tf_op jit(solution)/shard_map/ppermute | solution.py:361
  9.2 5.1 %collective-permute-start.2 = (bf16[272,128]{1,0:T(8,128)(2,1)S(1)}, bf16[272,128]{1,0:T(8,128)(2,1)S(1)}, u32[]{:S(2)}, u32[]{:S(2)}) collective-permute-start(bf16[272,128]{1,0:T(8,128)(2,1)S(1)} %pad_maximum_fusion.block), channel_id=1, source_target_pairs={{0,16},{1,5},{2,18},{3,7},{4,20},{5,1},{6,22},{7,3},{8,24},{9,13},... | collective-permute-start | bytes 208904 | tf_op jit(solution)/shard_map/ppermute | solution.py:361
  14.3 2.4 %collective-permute-start.5 = (bf16[64,128]{1,0:T(8,128)(2,1)S(1)}, bf16[64,128]{1,0:T(8,128)(2,1)S(1)}, u32[]{:S(2)}, u32[]{:S(2)}) collective-permute-start(bf16[64,128]{1,0:T(8,128)(2,1)S(1)} %get-tuple-element.78), channel_id=1, source_target_pairs={{0,1},{1,0},{2,3},{3,2},{4,5},{5,4},{6,7},{7,6},{8,9},{9,8},{10,11... | collective-permute-start | bytes 49160 | tf_op jit(solution)/shard_map/ppermute | solution.py:353

commit v7 on v6

--- a/solution.py
+++ b/solution.py
@@ -40,25 +40,6 @@
     return max(2, n_row // 4)
 
 
-def pack_kernel(n_row, pair_ref, mask_ref, out_ref, mask, marks, sems):
-    rows = pair_ref.shape[0]
-    per, tokens = mask_ref.shape
-    width = out_ref.shape[1]
-    whole = pltpu.make_async_copy(pair_ref, out_ref.at[0:rows], sems.at[0])
-    part = pltpu.make_async_copy(mask_ref, mask, sems.at[1])
-    part.start()
-    whole.start()
-    first = seat(lax.axis_index("row"), n_row) * per
-    last = seats(n_row) * per
-    marks[...] = jnp.zeros_like(marks)
-    part.wait()
-    mine = mask[...].astype(jnp.float32)
-    marks[pl.ds(first, per), :] = jnp.broadcast_to(jnp.max(mine, axis=1, keepdims=True), (per, width))
-    marks[last : last + 1, 0:tokens] = jnp.max(mine, axis=0, keepdims=True)
-    out_ref[rows:, :] = marks[...].astype(jnp.bfloat16)
-    whole.wait()
-
-
 def hold(values):
     return pltpu.with_memory_space_constraint(values, pltpu.HBM)
 
@@ -67,23 +48,58 @@
     return -(-(seats(n_row) * per + 1) // MARK_ROWS) * MARK_ROWS
 
 
-def pack(n_row, pair_rep, pair_mask):
-    per, tokens, width = pair_rep.shape
-    rows = per * tokens
-    extra = mark_rows(n_row, per)
-    hbm = pl.BlockSpec(memory_space=pltpu.HBM)
+def join_kernel(n_row, own, mask, other, other_mask, out_ref, marks):
+    rows = own.shape[0]
+    per, tokens = mask.shape
+    width = out_ref.shape[1]
+    me = lax.axis_index("row")
+    out_ref[0:rows, :] = own[...]
+    out_ref[rows : 2 * rows, :] = other[...]
+    marks[...] = jnp.zeros_like(marks)
+    last = seats(n_row) * per
+    seen = []
+    for device, ref in ((me, mask), (me ^ 1, other_mask)):
+        mine = ref[...].astype(jnp.float32)
+        first = seat(device, n_row) * per
+        marks[pl.ds(first, per), :] = jnp.broadcast_to(jnp.max(mine, axis=1, keepdims=True), (per, width))
+        seen.append(jnp.max(mine, axis=0, keepdims=True))
+    marks[last : last + 1, 0:tokens] = jnp.maximum(*seen)
+    out_ref[2 * rows :, :] = marks[...].astype(jnp.bfloat16)
+
+
+def join(n_row, own, mask, other, other_mask):
+    rows, width = own.shape
+    extra = mark_rows(n_row, mask.shape[0])
+    vmem = pl.BlockSpec(memory_space=pltpu.VMEM)
     return pl.pallas_call(
-        functools.partial(pack_kernel, n_row),
-        out_shape=jax.ShapeDtypeStruct((rows + extra, width), jnp.bfloat16),
-        in_specs=[hbm, hbm],
-        out_specs=pl.BlockSpec(memory_space=pltpu.VMEM),
-        scratch_shapes=[
-            pltpu.VMEM((per, tokens), jnp.int32),
-            pltpu.VMEM((extra, width), jnp.float32),
-            pltpu.SemaphoreType.DMA((2,)),
-        ],
+        functools.partial(join_kernel, n_row),
+        out_shape=jax.ShapeDtypeStruct((2 * rows + extra, width), jnp.bfloat16),
+        in_specs=[vmem] * 4,
+        out_specs=vmem,
+        scratch_shapes=[pltpu.VMEM((extra, width), jnp.float32)],
         compiler_params=pltpu.CompilerParams(vmem_limit_bytes=1 << 20),
-    )(hold(pair_rep.reshape(rows, width)), hold(pair_mask))
+    )(own, mask, other, other_mask)
+
+
+def fetch_kernel(count, *refs):
+    sources, targets, sems = refs[:count], refs[count : 2 * count], refs[2 * count]
+    copies = [pltpu.make_async_copy(s, t, sems.at[n]) for n, (s, t) in enumerate(zip(sources, targets, strict=True))]
+    for copy in copies:
+        copy.start()
+    for copy in copies:
+        copy.wait()
+
+
+def fetch(*arrays):
+    count = len(arrays)
+    return pl.pallas_call(
+        functools.partial(fetch_kernel, count),
+        out_shape=[jax.ShapeDtypeStruct(a.shape, a.dtype) for a in arrays],
+        in_specs=[pl.BlockSpec(memory_space=pltpu.HBM)] * count,
+        out_specs=[pl.BlockSpec(memory_space=pltpu.VMEM)] * count,
+        scratch_shapes=[pltpu.SemaphoreType.DMA((count,))],
+        compiler_params=pltpu.CompilerParams(vmem_limit_bytes=1 << 20),
+    )(*[hold(a) for a in arrays])
 
 
 def load_kernel(sources, targets):
@@ -369,8 +385,12 @@
     per, tokens, width = pair_rep.shape
     rows = per * tokens
     me = lax.axis_index("row")
-    held = pack(n_row, pair_rep, pair_mask)
-    held = merge(held, swap(held, 1, n_row), rows)
+    own = pair_rep.reshape(rows, width)
+    other = swap(own, 1, n_row)
+    other_mask = swap(pair_mask, 1, n_row)
+    own, mask = fetch(own, pair_mask)
+    other, other_mask, own, mask = lax.optimization_barrier((other, other_mask, own, mask))
+    held = join(n_row, own, mask, other, other_mask)
     order = [0, 1]
     step = n_row // 2
     while step > 4:

time: 17.5 us -> 17.4 us (level)
  waiting for transfers between devices: 3.52 us -> 2.74 us
  starting transfers between devices: 9.1 us -> 9.44 us
  local copies, waits for them, and re-layouts: 0.01 us -> 0.23 us
    ppermute x2 -> x3, waiting for transfers between devices: 1.68 us -> 0.92 us  [swap(): return lax.ppermute(values, 'row', [(i, i ^ step) for i in range(n_row)])]
    ppermute x2 -> x3, starting transfers between devices: 2.1 us -> 2.51 us  [swap(): return lax.ppermute(values, 'row', [(i, i ^ step) for i in range(n_row)])]
    unnamed x0 -> x2, local copies, waits for them, and re-layouts: none -> 0.23 us
    pallas_call x1 -> x2, Pallas kernels: 0.78 us -> 0.82 us  [the longest x1 0.74 us: fetch(): pl.pallas_call(functools.partial(fetch_kernel, count), out_shape=[jax.Sha...]
  transfers between devices with their start and end apart: 6 -> 7, of which waited for: 4 -> 4; matrix products, arithmetic and copies ran while one was open for 0% -> 0% of each run, Pallas kernels for 18% -> 23%
where the time goes in v7:
time: 17.4 us; the launch traced here: 17.1 us
  starting transfers between devices  9.44 us (54%)
  Pallas kernels  4.02 us (23%)
  waiting for transfers between devices  2.74 us (16%)
  other arithmetic  0.62 us (4%)
  local copies, waits for them, and re-layouts  0.23 us (1%)
    ppermute x4, starting transfers between devices, odd_swap(): return lax.ppermute(values, ('groups', 'row'), pairs)  6.93 us
    ppermute x3, starting transfers between devices, swap(): return lax.ppermute(values, 'row', [(i, i ^ step) for i in range(n_row)])  2.51 us
    pallas_call x3, Pallas kernels, complete_group(): pl.pallas_call(functools.partial(group_kernel, lay, n), out_shape=[jax.Sh...  1.92 us
    ppermute x4, waiting for transfers between devices, odd_swap(): return lax.ppermute(values, ('groups', 'row'), pairs)  1.82 us
    pallas_call x1, Pallas kernels, load(): pl.pallas_call(kernel, out_shape=[jax.ShapeDtypeStruct(*shape) for shape...  1.25 us
    ppermute x3, waiting for transfers between devices, swap(): return lax.ppermute(values, 'row', [(i, i ^ step) for i in range(n_row)])  0.92 us
    pallas_call x1, Pallas kernels, fetch(): pl.pallas_call(functools.partial(fetch_kernel, count), out_shape=[jax.Sha...  0.74 us
    select_n x1, other arithmetic, gathered(): out = jnp.where(me % 2 == 1, odd, swap(even, 1, n_row))  0.61 us
  transfers between devices with their start and end apart: 7, of which 4 were waited for; matrix products, arithmetic and copies ran while one was open for 0% of the time, Pallas kernels for 23%

profile of v7, /device:TPU:0, one launch (start us, length us, event | category | flops | bytes accessed | tf_op | source)
XLA Modules:
  0.0 17.1 jit_solution(3624596230298307006)
XLA Ops:
  0.0 0.0 copy-start
  0.0 0.5 %collective-permute-start = (bf16[64,128]{1,0:T(8,128)(2,1)}, bf16[64,128]{1,0:T(8,128)(2,1)S(1)}, u32[]{:S(2)}, u32[]{:S(2)}) collective-permute-start(bf16[64,128]{1,0:T(8,128)(2,1)} %bitcast.2), channel_id=1, source_target_pairs={{0,1},{1,0},{2,3},{3,2},{4,5},{5,4},{6,7},{7,6},{8,9},{9,8},{10,11... | collective-permute-start | bytes 49160 | tf_op jit(solution)/shard_map/ppermute | solution.py:369
  0.5 0.2 %copy-done = s32[2,32]{1,0:T(2,128)S(1)} copy-done((s32[2,32]{1,0:T(2,128)S(1)}, s32[2,32]{1,0:T(2,128)}, u32[]{:S(2)}) %copy-start) | copy-done | bytes 280
  0.7 0.5 %collective-permute-start.1 = (s32[2,32]{1,0:T(2,128)S(1)}, s32[2,32]{1,0:T(2,128)S(1)}, u32[]{:S(2)}, u32[]{:S(2)}) collective-permute-start(s32[2,32]{1,0:T(2,128)S(1)} %copy-done), channel_id=1, source_target_pairs={{0,1},{1,0},{2,3},{3,2},{4,5},{5,4},{6,7},{7,6},{8,9},{9,8},{10,11... | collective-permute-start | bytes 776 | tf_op jit(solution)/shard_map/ppermute | solution.py:369
  1.1 0.7 %shard_map.91 = (bf16[64,128]{1,0:T(8,128)(2,1)S(1)}, s32[2,32]{1,0:T(2,128)S(1)}) custom-call(bf16[64,128]{1,0:T(8,128)(2,1)} %bitcast.3, s32[2,32]{1,0:T(2,128)} %refs_1_.2), custom_call_target="tpu_custom_call" | custom-call | tf_op jit(solution)/shard_map/pallas_call | solution.py:95
  1.9 0.1 collective-permute-done.1.other_mask
  2.0 0.0 collective-permute-done.other
  2.0 0.1 shard_map.92
  2.0 2.8 %collective-permute-start.2 = (bf16[144,128]{1,0:T(8,128)(2,1)S(1)}, bf16[144,128]{1,0:T(8,128)(2,1)S(1)}, u32[]{:S(2)}, u32[]{:S(2)}) collective-permute-start(bf16[144,128]{1,0:T(8,128)(2,1)S(1)} %shard_map.92), channel_id=1, source_target_pairs={{0,16},{1,9},{2,18},{3,11},{4,20},{5,13},{6,22},{7,15},{8,24},{9,1... | collective-permute-start | bytes 110600 | tf_op jit(solution)/shard_map/ppermute | solution.py:377
  4.9 1.2 %shard_map.93 = (f32[2,128]{1,0:T(2,128)S(1)}, f32[2,128]{1,0:T(2,128)S(1)}, bf16[2,128,512]{2,1,0:T(8,128)(2,1)S(1)}, bf16[2,128,128]{2,1,0:T(8,128)(2,1)S(1)},...) custom-call(f32[2,128]{1,0:T(2,128)} %refs_0_.1, ...), custom_call_target="tpu_custom_call" | custom-call | tf_op jit(solution)/shard_map/pallas_call | solution.py:146
  6.1 0.7 %collective-permute-done.2 = bf16[144,128]{1,0:T(8,128)(2,1)S(1)} collective-permute-done((bf16[144,128]{1,0:T(8,128)(2,1)S(1)}, bf16[144,128]{1,0:T(8,128)(2,1)S(1)}, u32[]{:S(2)}, u32[]{:S(2)}) %collective-permute-start.2) | collective-permute-done | bytes 36896 | tf_op jit(solution)/shard_map/ppermute | solution.py:377
  6.8 2.1 %collective-permute-start.4 = (bf16[272,128]{1,0:T(8,128)(2,1)S(1)}, bf16[272,128]{1,0:T(8,128)(2,1)S(1)}, u32[]{:S(2)}, u32[]{:S(2)}) collective-permute-start(bf16[272,128]{1,0:T(8,128)(2,1)S(1)} %pad_maximum_fusion.block), channel_id=1, source_target_pairs={{0,16},{1,3},{2,18},{3,1},{4,20},{5,7},{6,22},{7,5},{8,24},{9,11},... | collective-permute-start | bytes 208904 | tf_op jit(solution)/shard_map/ppermute | solution.py:377
  8.9 0.1 collective-permute-start.5
  9.0 1.9 %collective-permute-start.3 = (bf16[272,128]{1,0:T(8,128)(2,1)S(1)}, bf16[272,128]{1,0:T(8,128)(2,1)S(1)}, u32[]{:S(2)}, u32[]{:S(2)}) collective-permute-start(bf16[272,128]{1,0:T(8,128)(2,1)S(1)} %pad_maximum_fusion.block), channel_id=1, source_target_pairs={{0,16},{1,5},{2,18},{3,7},{4,20},{5,1},{6,22},{7,3},{8,24},{9,13},... | collective-permute-start | bytes 208904 | tf_op jit(solution)/shard_map/ppermute | solution.py:377
  10.9 0.5 %shard_map.94 = (f32[320,128]{1,0:T(8,128)S(1)}, f32[256,128]{1,0:T(8,128)S(1)}, f32[256,128]{1,0:T(8,128)S(1)}, f32[256,128]{1,0:T(8,128)S(1)}, f32[8,128]{1,0:T(8,128)S(1)}, /*index=5*/f32[64,128]{1,0:T(8,128)S(1)}) custom-call(bf16[272,128]{1,0:T(8,128)(2,1)S(1)} %pad_maximum_fusion.block, ...), custom_call_target="tpu_custom_call" | custom-call | flops 42467328 | bytes 655360 | tf_op jit(solution)/shard_map/pallas_call | solution.py:256
  11.4 0.0 collective-permute-done.4.block
  11.4 0.6 %shard_map.95 = (f32[320,128]{1,0:T(8,128)S(1)}, f32[256,128]{1,0:T(8,128)S(1)}, f32[256,128]{1,0:T(8,128)S(1)}, f32[256,128]{1,0:T(8,128)S(1)}, f32[8,128]{1,0:T(8,128)S(1)}, /*index=5*/f32[192,128]{1,0:T(8,128)S(1)}) custom-call(bf16[272,128]{1,0:T(8,128)(2,1)S(1)} %collective-permute-done.4.block, f32[256,128]{1,0:T(8,128)S(1)} %get-tuple-element.69.refs_0_.refs_1_, ...), custom_call_target="tpu_custom_call" | custom-call | flops 43515904 | bytes 655360 | tf_op jit(solution)/shard_map/pallas_call | solution.py:256
  12.1 1.1 %collective-permute-done.5.block = bf16[272,128]{1,0:T(8,128)(2,1)S(1)} collective-permute-done((bf16[272,128]{1,0:T(8,128)(2,1)S(1)}, bf16[272,128]{1,0:T(8,128)(2,1)S(1)}, u32[]{:S(2)}, u32[]{:S(2)}) %collective-permute-start.5) | collective-permute-done | bytes 69664 | tf_op jit(solution)/shard_map/ppermute | solution.py:377
  13.2 0.8 %shard_map.96 = (f32[320,128]{1,0:T(8,128)S(1)}, f32[256,128]{1,0:T(8,128)S(1)}, f32[256,128]{1,0:T(8,128)S(1)}, f32[256,128]{1,0:T(8,128)S(1)}, f32[8,128]{1,0:T(8,128)S(1)}, /*index=5*/f32[320,128]{1,0:T(8,128)S(1)}) custom-call(bf16[272,128]{1,0:T(8,128)(2,1)S(1)} %collective-permute-done.5.block, f32[256,128]{1,0:T(8,128)S(1)} %get-tuple-element.69.refs_0_.refs_1_, ...), custom_call_target="tpu_custom_call" | custom-call | flops 44564480 | bytes 655360 | tf_op jit(solution)/shard_map/pallas_call | solution.py:256
  14.0 0.0 collective-permute-done.3.block
  14.1 1.6 %collective-permute-start.6 = (bf16[64,128]{1,0:T(8,128)(2,1)S(1)}, bf16[64,128]{1,0:T(8,128)(2,1)S(1)}, u32[]{:S(2)}, u32[]{:S(2)}) collective-permute-start(bf16[64,128]{1,0:T(8,128)(2,1)S(1)} %get-tuple-element.90), channel_id=1, source_target_pairs={{0,1},{1,0},{2,3},{3,2},{4,5},{5,4},{6,7},{7,6},{8,9},{9,8},{10,11... | collective-permute-start | bytes 49160 | tf_op jit(solution)/shard_map/ppermute | solution.py:369
  15.7 0.8 %collective-permute-done.6 = bf16[64,128]{1,0:T(8,128)(2,1)S(1)} collective-permute-done((bf16[64,128]{1,0:T(8,128)(2,1)S(1)}, bf16[64,128]{1,0:T(8,128)(2,1)S(1)}, u32[]{:S(2)}, u32[]{:S(2)}) %collective-permute-start.6) | collective-permute-done | bytes 16416 | tf_op jit(solution)/shard_map/ppermute | solution.py:369
  16.5 0.6 %broadcast_select_fusion = bf16[64,128]{1,0:T(8,128)(2,1)} fusion(bf16[64,128]{1,0:T(8,128)(2,1)S(1)} %get-tuple-element.89, bf16[64,128]{1,0:T(8,128)(2,1)S(1)} %collective-permute-done.6, pred[]{:T(512)S(6)} %eq.5), kind=kLoop, calls=%fused_computation.1 | loop fusion | flops 8192 | bytes 49153 | tf_op jit(solution)/shard_map/jit(_where)/select_n | solution.py:406
  (5 shorter events, 0.0 us)
Async XLA Ops:
  0.0 0.7 %copy-start = (s32[2,32]{1,0:T(2,128)S(1)}, s32[2,32]{1,0:T(2,128)}, u32[]{:S(2)}) copy-start(s32[2,32]{1,0:T(2,128)} %refs_1_.2) | copy-start | bytes 772
  0.0 2.0 %collective-permute-start = (bf16[64,128]{1,0:T(8,128)(2,1)}, bf16[64,128]{1,0:T(8,128)(2,1)S(1)}, u32[]{:S(2)}, u32[]{:S(2)}) collective-permute-start(bf16[64,128]{1,0:T(8,128)(2,1)} %bitcast.2), channel_id=1, source_target_pairs={{0,1},{1,0},{2,3},{3,2},{4,5},{5,4},{6,7},{7,6},{8,9},{9,8},{10,11... | collective-permute-start | bytes 49160 | tf_op jit(solution)/shard_map/ppermute | solution.py:369
  0.7 1.3 %collective-permute-start.1 = (s32[2,32]{1,0:T(2,128)S(1)}, s32[2,32]{1,0:T(2,128)S(1)}, u32[]{:S(2)}, u32[]{:S(2)}) collective-permute-start(s32[2,32]{1,0:T(2,128)S(1)} %copy-done), channel_id=1, source_target_pairs={{0,1},{1,0},{2,3},{3,2},{4,5},{5,4},{6,7},{7,6},{8,9},{9,8},{10,11... | collective-permute-start | bytes 776 | tf_op jit(solution)/shard_map/ppermute | solution.py:369
  2.0 4.8 %collective-permute-start.2 = (bf16[144,128]{1,0:T(8,128)(2,1)S(1)}, bf16[144,128]{1,0:T(8,128)(2,1)S(1)}, u32[]{:S(2)}, u32[]{:S(2)}) collective-permute-start(bf16[144,128]{1,0:T(8,128)(2,1)S(1)} %shard_map.92), channel_id=1, source_target_pairs={{0,16},{1,9},{2,18},{3,11},{4,20},{5,13},{6,22},{7,15},{8,24},{9,1... | collective-permute-start | bytes 110600 | tf_op jit(solution)/shard_map/ppermute | solution.py:377
  6.8 4.6 %collective-permute-start.4 = (bf16[272,128]{1,0:T(8,128)(2,1)S(1)}, bf16[272,128]{1,0:T(8,128)(2,1)S(1)}, u32[]{:S(2)}, u32[]{:S(2)}) collective-permute-start(bf16[272,128]{1,0:T(8,128)(2,1)S(1)} %pad_maximum_fusion.block), channel_id=1, source_target_pairs={{0,16},{1,3},{2,18},{3,1},{4,20},{5,7},{6,22},{7,5},{8,24},{9,11},... | collective-permute-start | bytes 208904 | tf_op jit(solution)/shard_map/ppermute | solution.py:377
  8.9 4.3 %collective-permute-start.5 = (bf16[272,128]{1,0:T(8,128)(2,1)S(1)}, bf16[272,128]{1,0:T(8,128)(2,1)S(1)}, u32[]{:S(2)}, u32[]{:S(2)}) collective-permute-start(bf16[272,128]{1,0:T(8,128)(2,1)S(1)} %pad_maximum_fusion.block), channel_id=1, source_target_pairs={{0,16},{1,7},{2,18},{3,5},{4,20},{5,3},{6,22},{7,1},{8,24},{9,15},... | collective-permute-start | bytes 208904 | tf_op jit(solution)/shard_map/ppermute | solution.py:377
  9.0 5.1 %collective-permute-start.3 = (bf16[272,128]{1,0:T(8,128)(2,1)S(1)}, bf16[272,128]{1,0:T(8,128)(2,1)S(1)}, u32[]{:S(2)}, u32[]{:S(2)}) collective-permute-start(bf16[272,128]{1,0:T(8,128)(2,1)S(1)} %pad_maximum_fusion.block), channel_id=1, source_target_pairs={{0,16},{1,5},{2,18},{3,7},{4,20},{5,1},{6,22},{7,3},{8,24},{9,13},... | collective-permute-start | bytes 208904 | tf_op jit(solution)/shard_map/ppermute | solution.py:377
  14.1 2.4 %collective-permute-start.6 = (bf16[64,128]{1,0:T(8,128)(2,1)S(1)}, bf16[64,128]{1,0:T(8,128)(2,1)S(1)}, u32[]{:S(2)}, u32[]{:S(2)}) collective-permute-start(bf16[64,128]{1,0:T(8,128)(2,1)S(1)} %get-tuple-element.90), channel_id=1, source_target_pairs={{0,1},{1,0},{2,3},{3,2},{4,5},{5,4},{6,7},{7,6},{8,9},{9,8},{10,11... | collective-permute-start | bytes 49160 | tf_op jit(solution)/shard_map/ppermute | solution.py:369

commit v8 on v7

--- a/solution.py
+++ b/solution.py
@@ -239,12 +239,12 @@
 
 def group_shapes(lay, n, width):
     count = len(lay.pairs(n)) * lay.group * lay.group
-    rows = [lay.group * lay.pitch, lay.chunk, lay.chunk, lay.chunk, lay.group, count]
+    rows = [(lay.group + 1) * lay.pitch, lay.chunk, lay.chunk, lay.chunk, lay.group, count]
     return [(r, width) for r in rows]
 
 
 def scratch_shapes(lay, width):
-    rows = [lay.marks] + [lay.group * lay.pitch] * 2 + [lay.tokens] * 2
+    rows = [lay.marks] + [(lay.group + 1) * lay.pitch] * 2 + [lay.tokens] * 2
     return [pltpu.VMEM((r, width), jnp.float32) for r in rows]
 
 
@@ -268,24 +268,64 @@
     )(block, *lefts, *rights, *params)
 
 
+def finish(lay, ours, middle, right, real, params, scratch, out):
+    gain_in, gain_out, proj, gate_weight, out_weight, proj_bias, gate_bias, out_bias = params
+    left, rough, result = scratch
+    tokens, per, pitch = lay.tokens, lay.per, lay.pitch
+    width = out.shape[-1]
+    marks = real[...]
+    columns = jnp.concatenate([middle[pl.ds(r, tokens, stride=pitch), :] for r in ours], axis=0)
+    (packed,) = normed_matmul(columns, gain_in[1:2, :], (proj[1, :, 0 : 2 * width],), (proj_bias[1:2, 0 : 2 * width],))
+    left[...] = gated(packed, width) * jnp.concatenate([marks] * len(ours), axis=0)
+    held = jnp.concatenate([middle[r * pitch : r * pitch + tokens, :] for r in ours], axis=0)
+    (gates,) = normed_matmul(held, gain_in[1:2, :], (gate_weight[1],), (gate_bias[1:2, :],))
+    gates = jnp.tanh(gates) + 1.0
+    totals = [jnp.zeros((tokens, width), jnp.float32)] * len(ours)
+    for k in range(tokens):
+        row = right[k * tokens : (k + 1) * tokens, :]
+        for r in range(len(ours)):
+            totals[r] = totals[r] + left[r * tokens + k : r * tokens + k + 1, :] * row
+    product = jnp.concatenate([t * (marks * real[r : r + 1, :]) for r, t in zip(ours, totals, strict=True)], axis=0)
+    (change,) = normed_matmul(product, gain_out[1:2, :], (out_weight[1],), (out_bias[1:2, :],))
+    value = held + gates * change
+    for r in range(len(ours)):
+        rough[r * pitch : r * pitch + tokens, :] = value[r * tokens : (r + 1) * tokens, :]
+    for first, at in lay.places():
+        for t in range(per):
+            row = rough[pl.ds(first + t, len(ours), stride=pitch), :]
+            result[pl.ds(at * per + t, len(ours), stride=pitch), :] = row
+    halves = [result[r * pitch : r * pitch + tokens, :] for r in range(len(ours))]
+    out[...] = jnp.concatenate(halves, axis=0).astype(jnp.bfloat16)
+
+
+def finish_scratch(lay, width):
+    rows = [lay.per * lay.tokens, (lay.per + 1) * lay.pitch, (lay.per + 1) * lay.pitch]
+    return [pltpu.VMEM((r, width), jnp.float32) for r in rows]
+
+
+def odd_kernel(lay, middle, right, real, *refs):
+    params, out, scratch = refs[:8], refs[8], refs[9:]
+    odd = lax.axis_index("row") % 2 == 1
+    pl.when(odd)(lambda: finish(lay, range(lay.per), middle, right, real, params, scratch, out))
+
+
 def updates_kernel(lay, block, *refs):
     last = len(lay.steps) - 1
     done = [refs[6 * n : 6 * n + 6] for n in range(last)]
-    refs = refs[6 * last :]
-    gain_in, gain_out, proj, gate_weight, out_weight, proj_bias, gate_bias, out_bias = refs[:8]
-    out_even, out_odd = refs[8:10]
-    own, scratch = refs[10:16], refs[16:21]
-    right1, middle, left1, result1 = refs[21:]
+    params, refs = refs[6 * last : 6 * last + 8], refs[6 * last + 8 :]
+    gain_in, gain_out, proj, gate_weight, out_weight, proj_bias, gate_bias, out_bias = params
+    out, middle, right1, real = refs[:4]
+    own, scratch, last_scratch = refs[4:10], refs[10:15], refs[15:]
     tokens, per, group, chunk, pitch = lay.tokens, lay.per, lay.group, lay.chunk, lay.pitch
-    width = out_even.shape[-1]
-    rows = per * tokens
+    width = out.shape[-1]
     done = done + [own]
 
     def run():
         prepare(lay, last, block, gain_in, proj, gate_weight, proj_bias, gate_bias, own[:5], scratch)
         complete(lay, last, [arrays[1] for arrays in done], [arrays[2] for arrays in done], own[5])
 
-        real = jnp.concatenate([arrays[4][...] for arrays in done], axis=0)
+        marks = jnp.concatenate([arrays[4][...] for arrays in done], axis=0)
+        real[...] = marks
         for p in range(last + 1):
             z, _, _, gate, near, _ = done[p]
             products = []
@@ -295,46 +335,24 @@
                     n = max(p, q)
                     start = (lay.pairs(n).index((p, q)) * group + i) * group
                     parts.append(done[n][5][start : start + group, :])
-                products.append(jnp.concatenate(parts, axis=0) * (real * near[i : i + 1, :]))
+                products.append(jnp.concatenate(parts, axis=0) * (marks * near[i : i + 1, :]))
             products = jnp.concatenate(products, axis=0)
             (change,) = normed_matmul(products, gain_out[0:1, :], (out_weight[0],), (out_bias[0:1, :],))
             held = jnp.concatenate([z[t * pitch : t * pitch + tokens, :] for t in range(group)], axis=0)
-            middle[p * chunk : (p + 1) * chunk, :] = held + gate[...] * change
+            moved = held + gate[...] * change
+            for t in range(group):
+                at = (p * group + t) * pitch
+                middle[at : at + tokens, :] = moved[t * tokens : (t + 1) * tokens, :]
 
         for p in range(last + 1):
-            at = slice(p * chunk, (p + 1) * chunk)
+            starts = [(p * group + t) * pitch for t in range(group)]
+            values = jnp.concatenate([middle[at : at + tokens, :] for at in starts], axis=0)
             (packed,) = normed_matmul(
-                middle[at, :], gain_in[1:2, :], (proj[1, :, 2 * width :],), (proj_bias[1:2, 2 * width :],)
+                values, gain_in[1:2, :], (proj[1, :, 2 * width :],), (proj_bias[1:2, 2 * width :],)
             )
-            right1[at, :] = gated(packed, width)
-
-        ours = [*range(per, 2 * per), *range(per)]
-        columns = jnp.concatenate([middle[pl.ds(r, tokens, stride=tokens), :] for r in ours], axis=0)
-        (packed,) = normed_matmul(
-            columns, gain_in[1:2, :], (proj[1, :, 0 : 2 * width],), (proj_bias[1:2, 0 : 2 * width],)
-        )
-        left1[...] = gated(packed, width) * jnp.concatenate([real] * len(ours), axis=0)
-        totals = [jnp.zeros((tokens, width), jnp.float32)] * len(ours)
-        for k in range(tokens):
-            row = right1[k * tokens : (k + 1) * tokens, :]
-            for r in range(len(ours)):
-                totals[r] = totals[r] + left1[r * tokens + k : r * tokens + k + 1, :] * row
-        near = done[0][4]
-        product = jnp.concatenate([t * (real * near[r : r + 1, :]) for r, t in zip(ours, totals, strict=True)], axis=0)
-        (change,) = normed_matmul(product, gain_out[1:2, :], (out_weight[1],), (out_bias[1:2, :],))
-        held = jnp.concatenate([middle[rows : 2 * rows, :], middle[0:rows, :]], axis=0)
-        (gates,) = normed_matmul(held, gain_in[1:2, :], (gate_weight[1],), (gate_bias[1:2, :],))
-        result = held + (jnp.tanh(gates) + 1.0) * change
-        rough = scratch[1]
-        for r in range(len(ours)):
-            rough[r * pitch : r * pitch + tokens, :] = result[r * tokens : (r + 1) * tokens, :]
-        for first, at in lay.places():
-            for t in range(per):
-                row = rough[pl.ds(first + t, len(ours), stride=pitch), :]
-                result1[pl.ds(at * per + t, len(ours), stride=pitch), :] = row
-        halves = [result1[r * pitch : r * pitch + tokens, :] for r in range(len(ours))]
-        out_even[...] = jnp.concatenate(halves[:per], axis=0).astype(jnp.bfloat16)
-        out_odd[...] = jnp.concatenate(halves[per:], axis=0).astype(jnp.bfloat16)
+            right1[p * chunk : (p + 1) * chunk, :] = gated(packed, width)
+
+        finish(lay, range(per, 2 * per), middle, right1, real, params, last_scratch, out)
 
     pl.when(lax.axis_index("row") % 2 == 1)(run)
 
@@ -351,18 +369,30 @@
         done.append(complete_group(lay, n, block, lefts, rights, group_params))
     arrays = [array for arrays in done for array in arrays]
     vmem = pl.BlockSpec(memory_space=pltpu.VMEM)
-    shapes = group_shapes(lay, len(blocks) - 1, width)
-    tail = [(pairs, width), (pairs, width), (2 * rows, width), (2 * lay.per * lay.pitch, width)]
-    return pl.pallas_call(
+    out = jax.ShapeDtypeStruct((rows, width), jnp.bfloat16)
+    shared = [((lay.tokens + 1) * lay.pitch, width), (pairs, width), (lay.tokens, width)]
+    even, *shared = pl.pallas_call(
         functools.partial(updates_kernel, lay),
-        out_shape=[jax.ShapeDtypeStruct((rows, width), jnp.bfloat16)] * 2,
+        out_shape=[out] + [jax.ShapeDtypeStruct(shape, jnp.float32) for shape in shared],
         in_specs=[vmem] * (1 + len(arrays) + len(params)),
-        out_specs=[vmem] * 2,
-        scratch_shapes=[pltpu.VMEM(shape, jnp.float32) for shape in shapes]
+        out_specs=[vmem] * 4,
+        scratch_shapes=[pltpu.VMEM(shape, jnp.float32) for shape in group_shapes(lay, len(blocks) - 1, width)]
         + scratch_shapes(lay, width)
-        + [pltpu.VMEM(shape, jnp.float32) for shape in tail],
+        + finish_scratch(lay, width),
         compiler_params=pltpu.CompilerParams(vmem_limit_bytes=8 << 20),
     )(blocks[-1], *arrays, *params)
+    odd = pl.pallas_call(
+        functools.partial(odd_kernel, lay),
+        out_shape=out,
+        in_specs=[vmem] * (3 + len(params)),
+        out_specs=vmem,
+        scratch_shapes=finish_scratch(lay, width),
+        cost_estimate=pl.CostEstimate(
+            flops=8 * rows * width * width, bytes_accessed=8 * pairs * width, transcendentals=2 * rows * width
+        ),
+        compiler_params=pltpu.CompilerParams(vmem_limit_bytes=4 << 20),
+    )(*shared, *params)
+    return even, odd
 
 
 def swap(values, step, n_row):
@@ -499,7 +529,7 @@
     def shards(pair_rep, *rest):
         per, tokens, _ = pair_rep.shape
         small = pair_rep.size * n_row * 2 <= GATHER_LIMIT
-        fits = n_row & (n_row - 1) == 0 and n_row > 3 and tokens % 32 == 0 and tokens <= pair_rep.shape[2]
+        fits = n_row & (n_row - 1) == 0 and n_row > 7 and tokens % 32 == 0 and tokens <= pair_rep.shape[2]
         if small and fits:
             return gathered(n_group, n_row, pair_rep, *rest)
         return exchanged(pair_rep, *rest)

time: 17.4 us -> 17.3 us (level)
  no operation moved by 1% of the time
where the time goes in v8:
time: 17.3 us; the launch traced here: 17 us
  starting transfers between devices  9.33 us (54%)
  Pallas kernels  4.04 us (23%)
  waiting for transfers between devices  2.73 us (16%)
  other arithmetic  0.62 us (4%)
  local copies, waits for them, and re-layouts  0.23 us (1%)
    ppermute x4, starting transfers between devices, odd_swap(): return lax.ppermute(values, ('groups', 'row'), pairs)  6.93 us
    ppermute x3, starting transfers between devices, swap(): return lax.ppermute(values, 'row', [(i, i ^ step) for i in range(n_row)])  2.4 us
    pallas_call x3, Pallas kernels, complete_group(): pl.pallas_call(functools.partial(group_kernel, lay, n), out_shape=[jax.Sh...  1.91 us
    ppermute x4, waiting for transfers between devices, odd_swap(): return lax.ppermute(values, ('groups', 'row'), pairs)  1.82 us
    pallas_call x1, Pallas kernels, load(): pl.pallas_call(kernel, out_shape=[jax.ShapeDtypeStruct(*shape) for shape...  1.25 us
    ppermute x3, waiting for transfers between devices, swap(): return lax.ppermute(values, 'row', [(i, i ^ step) for i in range(n_row)])  0.92 us
    pallas_call x1, Pallas kernels, fetch(): pl.pallas_call(functools.partial(fetch_kernel, count), out_shape=[jax.Sha...  0.74 us
    select_n x1, other arithmetic, gathered(): out = jnp.where(me % 2 == 1, odd, swap(even, 1, n_row))  0.61 us
  transfers between devices with their start and end apart: 7, of which 4 were waited for; matrix products, arithmetic and copies ran while one was open for 0% of the time, Pallas kernels for 23%

profile of v8, /device:TPU:0, one launch (start us, length us, event | category | flops | bytes accessed | tf_op | source)
XLA Modules:
  0.0 17.0 jit_solution(6235321386457472965)
XLA Ops:
  0.0 0.0 copy-start
  0.0 0.5 %collective-permute-start = (bf16[64,128]{1,0:T(8,128)(2,1)}, bf16[64,128]{1,0:T(8,128)(2,1)S(1)}, u32[]{:S(2)}, u32[]{:S(2)}) collective-permute-start(bf16[64,128]{1,0:T(8,128)(2,1)} %bitcast.2), channel_id=1, source_target_pairs={{0,1},{1,0},{2,3},{3,2},{4,5},{5,4},{6,7},{7,6},{8,9},{9,8},{10,11... | collective-permute-start | bytes 49160 | tf_op jit(solution)/shard_map/ppermute | solution.py:399
  0.5 0.2 %copy-done = s32[2,32]{1,0:T(2,128)S(1)} copy-done((s32[2,32]{1,0:T(2,128)S(1)}, s32[2,32]{1,0:T(2,128)}, u32[]{:S(2)}) %copy-start) | copy-done | bytes 280
  0.7 0.5 %collective-permute-start.1 = (s32[2,32]{1,0:T(2,128)S(1)}, s32[2,32]{1,0:T(2,128)S(1)}, u32[]{:S(2)}, u32[]{:S(2)}) collective-permute-start(s32[2,32]{1,0:T(2,128)S(1)} %copy-done), channel_id=1, source_target_pairs={{0,1},{1,0},{2,3},{3,2},{4,5},{5,4},{6,7},{7,6},{8,9},{9,8},{10,11... | collective-permute-start | bytes 776 | tf_op jit(solution)/shard_map/ppermute | solution.py:399
  1.1 0.7 %shard_map.91 = (bf16[64,128]{1,0:T(8,128)(2,1)S(1)}, s32[2,32]{1,0:T(2,128)S(1)}) custom-call(bf16[64,128]{1,0:T(8,128)(2,1)} %bitcast.3, s32[2,32]{1,0:T(2,128)} %refs_1_.2), custom_call_target="tpu_custom_call" | custom-call | tf_op jit(solution)/shard_map/pallas_call | solution.py:95
  1.9 0.1 collective-permute-done.1.other_mask
  2.0 0.0 collective-permute-done.other
  2.0 0.1 shard_map.92
  2.0 2.8 %collective-permute-start.2 = (bf16[144,128]{1,0:T(8,128)(2,1)S(1)}, bf16[144,128]{1,0:T(8,128)(2,1)S(1)}, u32[]{:S(2)}, u32[]{:S(2)}) collective-permute-start(bf16[144,128]{1,0:T(8,128)(2,1)S(1)} %shard_map.92), channel_id=1, source_target_pairs={{0,16},{1,9},{2,18},{3,11},{4,20},{5,13},{6,22},{7,15},{8,24},{9,1... | collective-permute-start | bytes 110600 | tf_op jit(solution)/shard_map/ppermute | solution.py:407
  4.9 1.2 %shard_map.93 = (f32[2,128]{1,0:T(2,128)S(1)}, f32[2,128]{1,0:T(2,128)S(1)}, bf16[2,128,512]{2,1,0:T(8,128)(2,1)S(1)}, bf16[2,128,128]{2,1,0:T(8,128)(2,1)S(1)},...) custom-call(f32[2,128]{1,0:T(2,128)} %refs_0_.1, ...), custom_call_target="tpu_custom_call" | custom-call | tf_op jit(solution)/shard_map/pallas_call | solution.py:146
  6.1 0.7 %collective-permute-done.2 = bf16[144,128]{1,0:T(8,128)(2,1)S(1)} collective-permute-done((bf16[144,128]{1,0:T(8,128)(2,1)S(1)}, bf16[144,128]{1,0:T(8,128)(2,1)S(1)}, u32[]{:S(2)}, u32[]{:S(2)}) %collective-permute-start.2) | collective-permute-done | bytes 36896 | tf_op jit(solution)/shard_map/ppermute | solution.py:407
  6.8 2.1 %collective-permute-start.4 = (bf16[272,128]{1,0:T(8,128)(2,1)S(1)}, bf16[272,128]{1,0:T(8,128)(2,1)S(1)}, u32[]{:S(2)}, u32[]{:S(2)}) collective-permute-start(bf16[272,128]{1,0:T(8,128)(2,1)S(1)} %pad_maximum_fusion.block), channel_id=1, source_target_pairs={{0,16},{1,3},{2,18},{3,1},{4,20},{5,7},{6,22},{7,5},{8,24},{9,11},... | collective-permute-start | bytes 208904 | tf_op jit(solution)/shard_map/ppermute | solution.py:407
  8.9 0.1 collective-permute-start.5
  9.0 1.9 %collective-permute-start.3 = (bf16[272,128]{1,0:T(8,128)(2,1)S(1)}, bf16[272,128]{1,0:T(8,128)(2,1)S(1)}, u32[]{:S(2)}, u32[]{:S(2)}) collective-permute-start(bf16[272,128]{1,0:T(8,128)(2,1)S(1)} %pad_maximum_fusion.block), channel_id=1, source_target_pairs={{0,16},{1,5},{2,18},{3,7},{4,20},{5,1},{6,22},{7,3},{8,24},{9,13},... | collective-permute-start | bytes 208904 | tf_op jit(solution)/shard_map/ppermute | solution.py:407
  10.9 0.5 %shard_map.94 = (f32[360,128]{1,0:T(8,128)S(1)}, f32[256,128]{1,0:T(8,128)S(1)}, f32[256,128]{1,0:T(8,128)S(1)}, f32[256,128]{1,0:T(8,128)S(1)}, f32[8,128]{1,0:T(8,128)S(1)}, /*index=5*/f32[64,128]{1,0:T(8,128)S(1)}) custom-call(bf16[272,128]{1,0:T(8,128)(2,1)S(1)} %pad_maximum_fusion.block, ...), custom_call_target="tpu_custom_call" | custom-call | flops 42467328 | bytes 655360 | tf_op jit(solution)/shard_map/pallas_call | solution.py:256
  11.4 0.0 collective-permute-done.4.block
  11.4 0.6 %shard_map.95 = (f32[360,128]{1,0:T(8,128)S(1)}, f32[256,128]{1,0:T(8,128)S(1)}, f32[256,128]{1,0:T(8,128)S(1)}, f32[256,128]{1,0:T(8,128)S(1)}, f32[8,128]{1,0:T(8,128)S(1)}, /*index=5*/f32[192,128]{1,0:T(8,128)S(1)}) custom-call(bf16[272,128]{1,0:T(8,128)(2,1)S(1)} %collective-permute-done.4.block, f32[256,128]{1,0:T(8,128)S(1)} %get-tuple-element.71.refs_0_.refs_1_, ...), custom_call_target="tpu_custom_call" | custom-call | flops 43515904 | bytes 655360 | tf_op jit(solution)/shard_map/pallas_call | solution.py:256
  12.1 1.1 %collective-permute-done.5.block = bf16[272,128]{1,0:T(8,128)(2,1)S(1)} collective-permute-done((bf16[272,128]{1,0:T(8,128)(2,1)S(1)}, bf16[272,128]{1,0:T(8,128)(2,1)S(1)}, u32[]{:S(2)}, u32[]{:S(2)}) %collective-permute-start.5) | collective-permute-done | bytes 69664 | tf_op jit(solution)/shard_map/ppermute | solution.py:407
  13.2 0.8 %shard_map.96 = (f32[360,128]{1,0:T(8,128)S(1)}, f32[256,128]{1,0:T(8,128)S(1)}, f32[256,128]{1,0:T(8,128)S(1)}, f32[256,128]{1,0:T(8,128)S(1)}, f32[8,128]{1,0:T(8,128)S(1)}, /*index=5*/f32[320,128]{1,0:T(8,128)S(1)}) custom-call(bf16[272,128]{1,0:T(8,128)(2,1)S(1)} %collective-permute-done.5.block, f32[256,128]{1,0:T(8,128)S(1)} %get-tuple-element.71.refs_0_.refs_1_, ...), custom_call_target="tpu_custom_call" | custom-call | flops 44564480 | bytes 655360 | tf_op jit(solution)/shard_map/pallas_call | solution.py:256
  14.0 0.0 collective-permute-done.3.block
  14.0 0.1 shard_map.97
  14.1 1.5 %collective-permute-start.6 = (bf16[64,128]{1,0:T(8,128)(2,1)S(1)}, bf16[64,128]{1,0:T(8,128)(2,1)S(1)}, u32[]{:S(2)}, u32[]{:S(2)}) collective-permute-start(bf16[64,128]{1,0:T(8,128)(2,1)S(1)} %get-tuple-element.94), channel_id=1, source_target_pairs={{0,1},{1,0},{2,3},{3,2},{4,5},{5,4},{6,7},{7,6},{8,9},{9,8},{10,11... | collective-permute-start | bytes 49160 | tf_op jit(solution)/shard_map/ppermute | solution.py:399
  15.6 0.8 %collective-permute-done.6 = bf16[64,128]{1,0:T(8,128)(2,1)S(1)} collective-permute-done((bf16[64,128]{1,0:T(8,128)(2,1)S(1)}, bf16[64,128]{1,0:T(8,128)(2,1)S(1)}, u32[]{:S(2)}, u32[]{:S(2)}) %collective-permute-start.6) | collective-permute-done | bytes 16416 | tf_op jit(solution)/shard_map/ppermute | solution.py:399
  16.4 0.6 %broadcast_select_fusion = bf16[64,128]{1,0:T(8,128)(2,1)} fusion(bf16[64,128]{1,0:T(8,128)(2,1)S(1)} %shard_map.98, bf16[64,128]{1,0:T(8,128)(2,1)S(1)} %collective-permute-done.6, pred[]{:T(512)S(6)} %eq.5), kind=kLoop, calls=%fused_computation.1 | loop fusion | flops 8192 | bytes 49153 | tf_op jit(solution)/shard_map/jit(_where)/select_n | solution.py:436
  (5 shorter events, 0.0 us)
Async XLA Ops:
  0.0 0.7 %copy-start = (s32[2,32]{1,0:T(2,128)S(1)}, s32[2,32]{1,0:T(2,128)}, u32[]{:S(2)}) copy-start(s32[2,32]{1,0:T(2,128)} %refs_1_.2) | copy-start | bytes 772
  0.0 2.0 %collective-permute-start = (bf16[64,128]{1,0:T(8,128)(2,1)}, bf16[64,128]{1,0:T(8,128)(2,1)S(1)}, u32[]{:S(2)}, u32[]{:S(2)}) collective-permute-start(bf16[64,128]{1,0:T(8,128)(2,1)} %bitcast.2), channel_id=1, source_target_pairs={{0,1},{1,0},{2,3},{3,2},{4,5},{5,4},{6,7},{7,6},{8,9},{9,8},{10,11... | collective-permute-start | bytes 49160 | tf_op jit(solution)/shard_map/ppermute | solution.py:399
  0.7 1.3 %collective-permute-start.1 = (s32[2,32]{1,0:T(2,128)S(1)}, s32[2,32]{1,0:T(2,128)S(1)}, u32[]{:S(2)}, u32[]{:S(2)}) collective-permute-start(s32[2,32]{1,0:T(2,128)S(1)} %copy-done), channel_id=1, source_target_pairs={{0,1},{1,0},{2,3},{3,2},{4,5},{5,4},{6,7},{7,6},{8,9},{9,8},{10,11... | collective-permute-start | bytes 776 | tf_op jit(solution)/shard_map/ppermute | solution.py:399
  2.0 4.8 %collective-permute-start.2 = (bf16[144,128]{1,0:T(8,128)(2,1)S(1)}, bf16[144,128]{1,0:T(8,128)(2,1)S(1)}, u32[]{:S(2)}, u32[]{:S(2)}) collective-permute-start(bf16[144,128]{1,0:T(8,128)(2,1)S(1)} %shard_map.92), channel_id=1, source_target_pairs={{0,16},{1,9},{2,18},{3,11},{4,20},{5,13},{6,22},{7,15},{8,24},{9,1... | collective-permute-start | bytes 110600 | tf_op jit(solution)/shard_map/ppermute | solution.py:407
  6.8 4.6 %collective-permute-start.4 = (bf16[272,128]{1,0:T(8,128)(2,1)S(1)}, bf16[272,128]{1,0:T(8,128)(2,1)S(1)}, u32[]{:S(2)}, u32[]{:S(2)}) collective-permute-start(bf16[272,128]{1,0:T(8,128)(2,1)S(1)} %pad_maximum_fusion.block), channel_id=1, source_target_pairs={{0,16},{1,3},{2,18},{3,1},{4,20},{5,7},{6,22},{7,5},{8,24},{9,11},... | collective-permute-start | bytes 208904 | tf_op jit(solution)/shard_map/ppermute | solution.py:407
  8.9 4.3 %collective-permute-start.5 = (bf16[272,128]{1,0:T(8,128)(2,1)S(1)}, bf16[272,128]{1,0:T(8,128)(2,1)S(1)}, u32[]{:S(2)}, u32[]{:S(2)}) collective-permute-start(bf16[272,128]{1,0:T(8,128)(2,1)S(1)} %pad_maximum_fusion.block), channel_id=1, source_target_pairs={{0,16},{1,7},{2,18},{3,5},{4,20},{5,3},{6,22},{7,1},{8,24},{9,15},... | collective-permute-start | bytes 208904 | tf_op jit(solution)/shard_map/ppermute | solution.py:407
  9.0 5.0 %collective-permute-start.3 = (bf16[272,128]{1,0:T(8,128)(2,1)S(1)}, bf16[272,128]{1,0:T(8,128)(2,1)S(1)}, u32[]{:S(2)}, u32[]{:S(2)}) collective-permute-start(bf16[272,128]{1,0:T(8,128)(2,1)S(1)} %pad_maximum_fusion.block), channel_id=1, source_target_pairs={{0,16},{1,5},{2,18},{3,7},{4,20},{5,1},{6,22},{7,3},{8,24},{9,13},... | collective-permute-start | bytes 208904 | tf_op jit(solution)/shard_map/ppermute | solution.py:407
  14.1 2.3 %collective-permute-start.6 = (bf16[64,128]{1,0:T(8,128)(2,1)S(1)}, bf16[64,128]{1,0:T(8,128)(2,1)S(1)}, u32[]{:S(2)}, u32[]{:S(2)}) collective-permute-start(bf16[64,128]{1,0:T(8,128)(2,1)S(1)} %get-tuple-element.94), channel_id=1, source_target_pairs={{0,1},{1,0},{2,3},{3,2},{4,5},{5,4},{6,7},{7,6},{8,9},{9,8},{10,11... | collective-permute-start | bytes 49160 | tf_op jit(solution)/shard_map/ppermute | solution.py:399

commit v9 on v8

--- a/solution.py
+++ b/solution.py
@@ -16,11 +16,17 @@
     return jnp.dot(left, right, preferred_element_type=jnp.float32)
 
 
+def normed_piece(values, gain, weights, biases):
+    width = values.shape[-1]
+    centered = values - jnp.mean(values, axis=-1, keepdims=True)
+    scale = lax.rsqrt(jnp.sum(centered * centered, axis=-1, keepdims=True) + width * EPS)
+    factor = (centered * (gain * width**0.5)).astype(jnp.bfloat16)
+    return [matmul(factor, weight) * scale + bias for weight, bias in zip(weights, biases, strict=True)]
+
+
 def normed_matmul(values, gain, weights, biases):
-    centered = values - jnp.mean(values, axis=-1, keepdims=True)
-    scale = lax.rsqrt(jnp.mean(centered * centered, axis=-1, keepdims=True) + EPS)
-    factor = (centered * gain).astype(jnp.bfloat16)
-    return [matmul(factor, weight) * scale + bias for weight, bias in zip(weights, biases, strict=True)]
+    pieces = [normed_piece(values[at : at + 128], gain, weights, biases) for at in range(0, values.shape[0], 128)]
+    return [jnp.concatenate(parts, axis=0) for parts in zip(*pieces, strict=True)]
 
 
 def gated(packed, width):
@@ -199,33 +205,38 @@
     packed, gates = normed_matmul(
         values, gain[0:1, :], (proj[0], gate_weight[0]), (proj_bias[0:1, :], gate_bias[0:1, :])
     )
-    left[...] = gated(packed[:, 0 : 2 * width], width)
+    value = gated(packed[:, 0 : 2 * width], width)
+    for t in range(group):
+        left[t * tokens : (t + 1) * tokens, :] = value[t * tokens : (t + 1) * tokens, :] * near[t : t + 1, :]
     value = gated(packed[:, 2 * width :], width)
     for t in range(group):
         right[t * pitch : t * pitch + tokens, :] = value[t * tokens : (t + 1) * tokens, :]
     for k in range(tokens):
-        right_t[k * group : (k + 1) * group, :] = right[pl.ds(k, group, stride=pitch), :] * seen[k : k + 1, :]
+        real = near[...] * seen[k : k + 1, :]
+        right_t[k * group : (k + 1) * group, :] = right[pl.ds(k, group, stride=pitch), :] * real
     gate[...] = jnp.tanh(gates) + 1.0
 
 
-def block_sums(lay, left, rights):
+def block_sums(lay, blocks, size):
     tokens, group = lay.tokens, lay.group
-    width = left.shape[-1]
-    totals = [[jnp.zeros((group, width), jnp.float32)] * group for _ in rights]
-    for k in range(tokens):
-        rows = [right[k * group : (k + 1) * group, :] for right in rights]
-        for i in range(group):
-            value = left[i * tokens + k : i * tokens + k + 1, :]
-            for q, row in enumerate(rows):
-                totals[q][i] = totals[q][i] + value * row
-    return totals
+    width = blocks[0][0].shape[-1]
+    results = []
+    for start in range(0, len(blocks), size):
+        some = blocks[start : start + size]
+        totals = [[jnp.zeros((group, width), jnp.float32)] * group for _ in some]
+        for k in range(tokens):
+            rows = {id(right): right[k * group : (k + 1) * group, :] for _, right in some}
+            for i in range(group):
+                values = {id(left): left[i * tokens + k : i * tokens + k + 1, :] for left, _ in some}
+                for total, (left, right) in zip(totals, some, strict=True):
+                    total[i] = total[i] + values[id(left)] * rows[id(right)]
+        results += totals
+    return results
 
 
 def complete(lay, n, lefts, rights, sums):
     size = lay.group * lay.group
-    totals = block_sums(lay, lefts[n], rights)
-    for p in range(n):
-        totals += block_sums(lay, lefts[p], rights[n : n + 1])
+    totals = block_sums(lay, [(lefts[p], rights[q]) for p, q in lay.pairs(n)], 5)
     for place, total in enumerate(totals):
         sums[place * size : (place + 1) * size, :] = jnp.concatenate(total, axis=0)
 
@@ -233,8 +244,12 @@
 def group_kernel(lay, n, block, *refs):
     lefts, rights, refs = refs[:n], refs[n : 2 * n], refs[2 * n :]
     params, outs, sums, scratch = refs[:5], refs[5:10], refs[10], refs[11:]
-    prepare(lay, n, block, *params, outs, scratch)
-    complete(lay, n, [*lefts, outs[1]], [*rights, outs[2]], sums)
+
+    def run():
+        prepare(lay, n, block, *params, outs, scratch)
+        complete(lay, n, [*lefts, outs[1]], [*rights, outs[2]], sums)
+
+    pl.when(lax.axis_index("row") % 2 == 1)(run)
 
 
 def group_shapes(lay, n, width):
@@ -327,7 +342,7 @@
         marks = jnp.concatenate([arrays[4][...] for arrays in done], axis=0)
         real[...] = marks
         for p in range(last + 1):
-            z, _, _, gate, near, _ = done[p]
+            z, _, _, gate, _, _ = done[p]
             products = []
             for i in range(group):
                 parts = []
@@ -335,7 +350,7 @@
                     n = max(p, q)
                     start = (lay.pairs(n).index((p, q)) * group + i) * group
                     parts.append(done[n][5][start : start + group, :])
-                products.append(jnp.concatenate(parts, axis=0) * (marks * near[i : i + 1, :]))
+                products += parts
             products = jnp.concatenate(products, axis=0)
             (change,) = normed_matmul(products, gain_out[0:1, :], (out_weight[0],), (out_bias[0:1, :],))
             held = jnp.concatenate([z[t * pitch : t * pitch + tokens, :] for t in range(group)], axis=0)
@@ -399,10 +414,11 @@
     return lax.ppermute(values, "row", [(i, i ^ step) for i in range(n_row)])
 
 
-def odd_swap(values, step, n_group, n_row):
+def odd_swap(values, step, n_group, n_row, even_step=0):
     if n_group % 2:
         return swap(values, step, n_row)
-    target = [(g, i ^ step) if i % 2 else (g ^ 1, i) for g in range(n_group) for i in range(n_row)]
+    idle = [(g, i ^ even_step) if even_step else (g ^ 1, i) for g in range(n_group) for i in range(n_row)]
+    target = [(n // n_row, n % n_row ^ step) if n % 2 else place for n, place in enumerate(idle)]
     pairs = [(source, g * n_row + i) for source, (g, i) in enumerate(target)]
     return lax.ppermute(values, ("groups", "row"), pairs)
 
@@ -425,7 +441,7 @@
     step = n_row // 2
     while step > 4:
         count = len(order)
-        held = merge(held, odd_swap(held, step, n_group, n_row), count * rows)
+        held = merge(held, odd_swap(held, step, n_group, n_row, 2), count * rows)
         order = order + [place ^ step for place in order]
         step //= 2
     held, *params = lax.optimization_barrier((held, *load(*params)))

time: 17.3 us -> 17.3 us (level)
  Pallas kernels: 4.04 us -> 2.07 us
  waiting for transfers between devices: 2.73 us -> 4.61 us
    pallas_call x3, Pallas kernels: 1.91 us -> 0.01 us  [complete_group(): pl.pallas_call(functools.partial(group_kernel, lay, n), out_shape=[jax.Sh...]
    ppermute x4, waiting for transfers between devices: 1.82 us -> 3.69 us  [odd_swap(): return lax.ppermute(values, ('groups', 'row'), pairs)]
  transfers between devices with their start and end apart: 7 -> 7, of which waited for: 4 -> 6; matrix products, arithmetic and copies ran while one was open for 0% -> 0% of each run, Pallas kernels for 23% -> 12%
where the time goes in v9:
time: 17.3 us; the launch traced here: 17 us
  starting transfers between devices  9.43 us (55%)
  waiting for transfers between devices  4.61 us (27%)
  Pallas kernels  2.07 us (12%)
  other arithmetic  0.62 us (4%)
  local copies, waits for them, and re-layouts  0.23 us (1%)
    ppermute x4, starting transfers between devices, odd_swap(): return lax.ppermute(values, ('groups', 'row'), pairs)  6.93 us
    ppermute x4, waiting for transfers between devices, odd_swap(): return lax.ppermute(values, ('groups', 'row'), pairs)  3.69 us
    ppermute x3, starting transfers between devices, swap(): return lax.ppermute(values, 'row', [(i, i ^ step) for i in range(n_row)])  2.5 us
    pallas_call x1, Pallas kernels, load(): pl.pallas_call(kernel, out_shape=[jax.ShapeDtypeStruct(*shape) for shape...  1.25 us
    ppermute x3, waiting for transfers between devices, swap(): return lax.ppermute(values, 'row', [(i, i ^ step) for i in range(n_row)])  0.92 us
    pallas_call x1, Pallas kernels, fetch(): pl.pallas_call(functools.partial(fetch_kernel, count), out_shape=[jax.Sha...  0.74 us
    select_n x1, other arithmetic, gathered(): out = jnp.where(me % 2 == 1, odd, swap(even, 1, n_row))  0.61 us
  transfers between devices with their start and end apart: 7, of which 6 were waited for; matrix products, arithmetic and copies ran while one was open for 0% of the time, Pallas kernels for 12%

profile of v9, /device:TPU:0, one launch (start us, length us, event | category | flops | bytes accessed | tf_op | source)
XLA Modules:
  0.0 17.0 jit_solution(16765250981872460447)
XLA Ops:
  0.0 0.0 copy-start
  0.0 0.5 %collective-permute-start = (bf16[64,128]{1,0:T(8,128)(2,1)}, bf16[64,128]{1,0:T(8,128)(2,1)S(1)}, u32[]{:S(2)}, u32[]{:S(2)}) collective-permute-start(bf16[64,128]{1,0:T(8,128)(2,1)} %bitcast.2), channel_id=1, source_target_pairs={{0,1},{1,0},{2,3},{3,2},{4,5},{5,4},{6,7},{7,6},{8,9},{9,8},{10,11... | collective-permute-start | bytes 49160 | tf_op jit(solution)/shard_map/ppermute | solution.py:414
  0.5 0.2 %copy-done = s32[2,32]{1,0:T(2,128)S(1)} copy-done((s32[2,32]{1,0:T(2,128)S(1)}, s32[2,32]{1,0:T(2,128)}, u32[]{:S(2)}) %copy-start) | copy-done | bytes 280
  0.7 0.5 %collective-permute-start.1 = (s32[2,32]{1,0:T(2,128)S(1)}, s32[2,32]{1,0:T(2,128)S(1)}, u32[]{:S(2)}, u32[]{:S(2)}) collective-permute-start(s32[2,32]{1,0:T(2,128)S(1)} %copy-done), channel_id=1, source_target_pairs={{0,1},{1,0},{2,3},{3,2},{4,5},{5,4},{6,7},{7,6},{8,9},{9,8},{10,11... | collective-permute-start | bytes 776 | tf_op jit(solution)/shard_map/ppermute | solution.py:414
  1.1 0.7 %shard_map.91 = (bf16[64,128]{1,0:T(8,128)(2,1)S(1)}, s32[2,32]{1,0:T(2,128)S(1)}) custom-call(bf16[64,128]{1,0:T(8,128)(2,1)} %bitcast.3, s32[2,32]{1,0:T(2,128)} %refs_1_.2), custom_call_target="tpu_custom_call" | custom-call | tf_op jit(solution)/shard_map/pallas_call | solution.py:101
  1.9 0.1 collective-permute-done.1.other_mask
  2.0 0.0 collective-permute-done.other
  2.0 0.1 shard_map.92
  2.0 2.8 %collective-permute-start.2 = (bf16[144,128]{1,0:T(8,128)(2,1)S(1)}, bf16[144,128]{1,0:T(8,128)(2,1)S(1)}, u32[]{:S(2)}, u32[]{:S(2)}) collective-permute-start(bf16[144,128]{1,0:T(8,128)(2,1)S(1)} %shard_map.92), channel_id=1, source_target_pairs={{0,2},{1,9},{2,0},{3,11},{4,6},{5,13},{6,4},{7,15},{8,10},{9,1},{1... | collective-permute-start | bytes 110600 | tf_op jit(solution)/shard_map/ppermute | solution.py:423
  4.9 1.2 %shard_map.93 = (f32[2,128]{1,0:T(2,128)S(1)}, f32[2,128]{1,0:T(2,128)S(1)}, bf16[2,128,512]{2,1,0:T(8,128)(2,1)S(1)}, bf16[2,128,128]{2,1,0:T(8,128)(2,1)S(1)},...) custom-call(f32[2,128]{1,0:T(2,128)} %refs_0_.1, ...), custom_call_target="tpu_custom_call" | custom-call | tf_op jit(solution)/shard_map/pallas_call | solution.py:152
  6.2 0.7 %collective-permute-done.2 = bf16[144,128]{1,0:T(8,128)(2,1)S(1)} collective-permute-done((bf16[144,128]{1,0:T(8,128)(2,1)S(1)}, bf16[144,128]{1,0:T(8,128)(2,1)S(1)}, u32[]{:S(2)}, u32[]{:S(2)}) %collective-permute-start.2) | collective-permute-done | bytes 36896 | tf_op jit(solution)/shard_map/ppermute | solution.py:423
  6.8 2.1 %collective-permute-start.4 = (bf16[272,128]{1,0:T(8,128)(2,1)S(1)}, bf16[272,128]{1,0:T(8,128)(2,1)S(1)}, u32[]{:S(2)}, u32[]{:S(2)}) collective-permute-start(bf16[272,128]{1,0:T(8,128)(2,1)S(1)} %pad_maximum_fusion.block), channel_id=1, source_target_pairs={{0,16},{1,3},{2,18},{3,1},{4,20},{5,7},{6,22},{7,5},{8,24},{9,11},... | collective-permute-start | bytes 208904 | tf_op jit(solution)/shard_map/ppermute | solution.py:423
  8.9 0.1 collective-permute-start.5
  9.0 1.9 %collective-permute-start.3 = (bf16[272,128]{1,0:T(8,128)(2,1)S(1)}, bf16[272,128]{1,0:T(8,128)(2,1)S(1)}, u32[]{:S(2)}, u32[]{:S(2)}) collective-permute-start(bf16[272,128]{1,0:T(8,128)(2,1)S(1)} %pad_maximum_fusion.block), channel_id=1, source_target_pairs={{0,16},{1,5},{2,18},{3,7},{4,20},{5,1},{6,22},{7,3},{8,24},{9,13},... | collective-permute-start | bytes 208904 | tf_op jit(solution)/shard_map/ppermute | solution.py:423
  10.9 0.3 %collective-permute-done.4.block = bf16[272,128]{1,0:T(8,128)(2,1)S(1)} collective-permute-done((bf16[272,128]{1,0:T(8,128)(2,1)S(1)}, bf16[272,128]{1,0:T(8,128)(2,1)S(1)}, u32[]{:S(2)}, u32[]{:S(2)}) %collective-permute-start.4) | collective-permute-done | bytes 69664 | tf_op jit(solution)/shard_map/ppermute | solution.py:423
  11.2 2.0 %collective-permute-done.5.block = bf16[272,128]{1,0:T(8,128)(2,1)S(1)} collective-permute-done((bf16[272,128]{1,0:T(8,128)(2,1)S(1)}, bf16[272,128]{1,0:T(8,128)(2,1)S(1)}, u32[]{:S(2)}, u32[]{:S(2)}) %collective-permute-start.5) | collective-permute-done | bytes 69664 | tf_op jit(solution)/shard_map/ppermute | solution.py:423
  13.2 0.7 %collective-permute-done.3.block = bf16[272,128]{1,0:T(8,128)(2,1)S(1)} collective-permute-done((bf16[272,128]{1,0:T(8,128)(2,1)S(1)}, bf16[272,128]{1,0:T(8,128)(2,1)S(1)}, u32[]{:S(2)}, u32[]{:S(2)}) %collective-permute-start.3) | collective-permute-done | bytes 69664 | tf_op jit(solution)/shard_map/ppermute | solution.py:423
  14.0 1.6 %collective-permute-start.6 = (bf16[64,128]{1,0:T(8,128)(2,1)S(1)}, bf16[64,128]{1,0:T(8,128)(2,1)S(1)}, u32[]{:S(2)}, u32[]{:S(2)}) collective-permute-start(bf16[64,128]{1,0:T(8,128)(2,1)S(1)} %get-tuple-element.94), channel_id=1, source_target_pairs={{0,1},{1,0},{2,3},{3,2},{4,5},{5,4},{6,7},{7,6},{8,9},{9,8},{10,11... | collective-permute-start | bytes 49160 | tf_op jit(solution)/shard_map/ppermute | solution.py:414
  15.6 0.8 %collective-permute-done.6 = bf16[64,128]{1,0:T(8,128)(2,1)S(1)} collective-permute-done((bf16[64,128]{1,0:T(8,128)(2,1)S(1)}, bf16[64,128]{1,0:T(8,128)(2,1)S(1)}, u32[]{:S(2)}, u32[]{:S(2)}) %collective-permute-start.6) | collective-permute-done | bytes 16416 | tf_op jit(solution)/shard_map/ppermute | solution.py:414
  16.4 0.6 %broadcast_select_fusion = bf16[64,128]{1,0:T(8,128)(2,1)} fusion(bf16[64,128]{1,0:T(8,128)(2,1)S(1)} %shard_map.98, bf16[64,128]{1,0:T(8,128)(2,1)S(1)} %collective-permute-done.6, pred[]{:T(512)S(6)} %eq.5), kind=kLoop, calls=%fused_computation.1 | loop fusion | flops 8192 | bytes 49153 | tf_op jit(solution)/shard_map/jit(_where)/select_n | solution.py:452
  (9 shorter events, 0.0 us)
Async XLA Ops:
  0.0 0.7 %copy-start = (s32[2,32]{1,0:T(2,128)S(1)}, s32[2,32]{1,0:T(2,128)}, u32[]{:S(2)}) copy-start(s32[2,32]{1,0:T(2,128)} %refs_1_.2) | copy-start | bytes 772
  0.0 2.0 %collective-permute-start = (bf16[64,128]{1,0:T(8,128)(2,1)}, bf16[64,128]{1,0:T(8,128)(2,1)S(1)}, u32[]{:S(2)}, u32[]{:S(2)}) collective-permute-start(bf16[64,128]{1,0:T(8,128)(2,1)} %bitcast.2), channel_id=1, source_target_pairs={{0,1},{1,0},{2,3},{3,2},{4,5},{5,4},{6,7},{7,6},{8,9},{9,8},{10,11... | collective-permute-start | bytes 49160 | tf_op jit(solution)/shard_map/ppermute | solution.py:414
  0.7 1.3 %collective-permute-start.1 = (s32[2,32]{1,0:T(2,128)S(1)}, s32[2,32]{1,0:T(2,128)S(1)}, u32[]{:S(2)}, u32[]{:S(2)}) collective-permute-start(s32[2,32]{1,0:T(2,128)S(1)} %copy-done), channel_id=1, source_target_pairs={{0,1},{1,0},{2,3},{3,2},{4,5},{5,4},{6,7},{7,6},{8,9},{9,8},{10,11... | collective-permute-start | bytes 776 | tf_op jit(solution)/shard_map/ppermute | solution.py:414
  2.0 4.8 %collective-permute-start.2 = (bf16[144,128]{1,0:T(8,128)(2,1)S(1)}, bf16[144,128]{1,0:T(8,128)(2,1)S(1)}, u32[]{:S(2)}, u32[]{:S(2)}) collective-permute-start(bf16[144,128]{1,0:T(8,128)(2,1)S(1)} %shard_map.92), channel_id=1, source_target_pairs={{0,2},{1,9},{2,0},{3,11},{4,6},{5,13},{6,4},{7,15},{8,10},{9,1},{1... | collective-permute-start | bytes 110600 | tf_op jit(solution)/shard_map/ppermute | solution.py:423
  6.8 4.4 %collective-permute-start.4 = (bf16[272,128]{1,0:T(8,128)(2,1)S(1)}, bf16[272,128]{1,0:T(8,128)(2,1)S(1)}, u32[]{:S(2)}, u32[]{:S(2)}) collective-permute-start(bf16[272,128]{1,0:T(8,128)(2,1)S(1)} %pad_maximum_fusion.block), channel_id=1, source_target_pairs={{0,16},{1,3},{2,18},{3,1},{4,20},{5,7},{6,22},{7,5},{8,24},{9,11},... | collective-permute-start | bytes 208904 | tf_op jit(solution)/shard_map/ppermute | solution.py:423
  8.9 4.3 %collective-permute-start.5 = (bf16[272,128]{1,0:T(8,128)(2,1)S(1)}, bf16[272,128]{1,0:T(8,128)(2,1)S(1)}, u32[]{:S(2)}, u32[]{:S(2)}) collective-permute-start(bf16[272,128]{1,0:T(8,128)(2,1)S(1)} %pad_maximum_fusion.block), channel_id=1, source_target_pairs={{0,16},{1,7},{2,18},{3,5},{4,20},{5,3},{6,22},{7,1},{8,24},{9,15},... | collective-permute-start | bytes 208904 | tf_op jit(solution)/shard_map/ppermute | solution.py:423
  9.0 5.0 %collective-permute-start.3 = (bf16[272,128]{1,0:T(8,128)(2,1)S(1)}, bf16[272,128]{1,0:T(8,128)(2,1)S(1)}, u32[]{:S(2)}, u32[]{:S(2)}) collective-permute-start(bf16[272,128]{1,0:T(8,128)(2,1)S(1)} %pad_maximum_fusion.block), channel_id=1, source_target_pairs={{0,16},{1,5},{2,18},{3,7},{4,20},{5,1},{6,22},{7,3},{8,24},{9,13},... | collective-permute-start | bytes 208904 | tf_op jit(solution)/shard_map/ppermute | solution.py:423
  14.0 2.4 %collective-permute-start.6 = (bf16[64,128]{1,0:T(8,128)(2,1)S(1)}, bf16[64,128]{1,0:T(8,128)(2,1)S(1)}, u32[]{:S(2)}, u32[]{:S(2)}) collective-permute-start(bf16[64,128]{1,0:T(8,128)(2,1)S(1)} %get-tuple-element.94), channel_id=1, source_target_pairs={{0,1},{1,0},{2,3},{3,2},{4,5},{5,4},{6,7},{7,6},{8,9},{9,8},{10,11... | collective-permute-start | bytes 49160 | tf_op jit(solution)/shard_map/ppermute | solution.py:414

commit v10 on v9

--- a/solution.py
+++ b/solution.py
@@ -236,7 +236,7 @@
 
 def complete(lay, n, lefts, rights, sums):
     size = lay.group * lay.group
-    totals = block_sums(lay, [(lefts[p], rights[q]) for p, q in lay.pairs(n)], 5)
+    totals = block_sums(lay, [(lefts[p], rights[q]) for p, q in lay.pairs(n)], 4)
     for place, total in enumerate(totals):
         sums[place * size : (place + 1) * size, :] = jnp.concatenate(total, axis=0)
 

time: 17.3 us -> 17.2 us (level)
  no operation moved by 1% of the time
where the time goes in v10:
time: 17.2 us; the launch traced here: 17 us
  starting transfers between devices  9.4 us (55%)
  waiting for transfers between devices  4.61 us (27%)
  Pallas kernels  2.07 us (12%)
  other arithmetic  0.62 us (4%)
  local copies, waits for them, and re-layouts  0.23 us (1%)
    ppermute x4, starting transfers between devices, odd_swap(): return lax.ppermute(values, ('groups', 'row'), pairs)  6.93 us
    ppermute x4, waiting for transfers between devices, odd_swap(): return lax.ppermute(values, ('groups', 'row'), pairs)  3.69 us
    ppermute x3, starting transfers between devices, swap(): return lax.ppermute(values, 'row', [(i, i ^ step) for i in range(n_row)])  2.48 us
    pallas_call x1, Pallas kernels, load(): pl.pallas_call(kernel, out_shape=[jax.ShapeDtypeStruct(*shape) for shape...  1.25 us
    ppermute x3, waiting for transfers between devices, swap(): return lax.ppermute(values, 'row', [(i, i ^ step) for i in range(n_row)])  0.92 us
    pallas_call x1, Pallas kernels, fetch(): pl.pallas_call(functools.partial(fetch_kernel, count), out_shape=[jax.Sha...  0.74 us
    select_n x1, other arithmetic, gathered(): out = jnp.where(me % 2 == 1, odd, swap(even, 1, n_row))  0.61 us
  transfers between devices with their start and end apart: 7, of which 6 were waited for; matrix products, arithmetic and copies ran while one was open for 0% of the time, Pallas kernels for 12%

profile of v10, /device:TPU:0, one launch (start us, length us, event | category | flops | bytes accessed | tf_op | source)
XLA Modules:
  0.0 17.0 jit_solution(8268990652560722963)
XLA Ops:
  0.0 0.0 copy-start
  0.0 0.5 %collective-permute-start = (bf16[64,128]{1,0:T(8,128)(2,1)}, bf16[64,128]{1,0:T(8,128)(2,1)S(1)}, u32[]{:S(2)}, u32[]{:S(2)}) collective-permute-start(bf16[64,128]{1,0:T(8,128)(2,1)} %bitcast.2), channel_id=1, source_target_pairs={{0,1},{1,0},{2,3},{3,2},{4,5},{5,4},{6,7},{7,6},{8,9},{9,8},{10,11... | collective-permute-start | bytes 49160 | tf_op jit(solution)/shard_map/ppermute | solution.py:414
  0.5 0.2 %copy-done = s32[2,32]{1,0:T(2,128)S(1)} copy-done((s32[2,32]{1,0:T(2,128)S(1)}, s32[2,32]{1,0:T(2,128)}, u32[]{:S(2)}) %copy-start) | copy-done | bytes 280
  0.7 0.5 %collective-permute-start.1 = (s32[2,32]{1,0:T(2,128)S(1)}, s32[2,32]{1,0:T(2,128)S(1)}, u32[]{:S(2)}, u32[]{:S(2)}) collective-permute-start(s32[2,32]{1,0:T(2,128)S(1)} %copy-done), channel_id=1, source_target_pairs={{0,1},{1,0},{2,3},{3,2},{4,5},{5,4},{6,7},{7,6},{8,9},{9,8},{10,11... | collective-permute-start | bytes 776 | tf_op jit(solution)/shard_map/ppermute | solution.py:414
  1.1 0.7 %shard_map.91 = (bf16[64,128]{1,0:T(8,128)(2,1)S(1)}, s32[2,32]{1,0:T(2,128)S(1)}) custom-call(bf16[64,128]{1,0:T(8,128)(2,1)} %bitcast.3, s32[2,32]{1,0:T(2,128)} %refs_1_.2), custom_call_target="tpu_custom_call" | custom-call | tf_op jit(solution)/shard_map/pallas_call | solution.py:101
  1.9 0.1 collective-permute-done.1.other_mask
  2.0 0.0 collective-permute-done.other
  2.0 0.1 shard_map.92
  2.0 2.8 %collective-permute-start.2 = (bf16[144,128]{1,0:T(8,128)(2,1)S(1)}, bf16[144,128]{1,0:T(8,128)(2,1)S(1)}, u32[]{:S(2)}, u32[]{:S(2)}) collective-permute-start(bf16[144,128]{1,0:T(8,128)(2,1)S(1)} %shard_map.92), channel_id=1, source_target_pairs={{0,2},{1,9},{2,0},{3,11},{4,6},{5,13},{6,4},{7,15},{8,10},{9,1},{1... | collective-permute-start | bytes 110600 | tf_op jit(solution)/shard_map/ppermute | solution.py:423
  4.9 1.2 %shard_map.93 = (f32[2,128]{1,0:T(2,128)S(1)}, f32[2,128]{1,0:T(2,128)S(1)}, bf16[2,128,512]{2,1,0:T(8,128)(2,1)S(1)}, bf16[2,128,128]{2,1,0:T(8,128)(2,1)S(1)},...) custom-call(f32[2,128]{1,0:T(2,128)} %refs_0_.1, ...), custom_call_target="tpu_custom_call" | custom-call | tf_op jit(solution)/shard_map/pallas_call | solution.py:152
  6.2 0.7 %collective-permute-done.2 = bf16[144,128]{1,0:T(8,128)(2,1)S(1)} collective-permute-done((bf16[144,128]{1,0:T(8,128)(2,1)S(1)}, bf16[144,128]{1,0:T(8,128)(2,1)S(1)}, u32[]{:S(2)}, u32[]{:S(2)}) %collective-permute-start.2) | collective-permute-done | bytes 36896 | tf_op jit(solution)/shard_map/ppermute | solution.py:423
  6.8 2.1 %collective-permute-start.4 = (bf16[272,128]{1,0:T(8,128)(2,1)S(1)}, bf16[272,128]{1,0:T(8,128)(2,1)S(1)}, u32[]{:S(2)}, u32[]{:S(2)}) collective-permute-start(bf16[272,128]{1,0:T(8,128)(2,1)S(1)} %pad_maximum_fusion.block), channel_id=1, source_target_pairs={{0,16},{1,3},{2,18},{3,1},{4,20},{5,7},{6,22},{7,5},{8,24},{9,11},... | collective-permute-start | bytes 208904 | tf_op jit(solution)/shard_map/ppermute | solution.py:423
  8.9 0.1 collective-permute-start.5
  9.0 1.9 %collective-permute-start.3 = (bf16[272,128]{1,0:T(8,128)(2,1)S(1)}, bf16[272,128]{1,0:T(8,128)(2,1)S(1)}, u32[]{:S(2)}, u32[]{:S(2)}) collective-permute-start(bf16[272,128]{1,0:T(8,128)(2,1)S(1)} %pad_maximum_fusion.block), channel_id=1, source_target_pairs={{0,16},{1,5},{2,18},{3,7},{4,20},{5,1},{6,22},{7,3},{8,24},{9,13},... | collective-permute-start | bytes 208904 | tf_op jit(solution)/shard_map/ppermute | solution.py:423
  10.9 0.3 %collective-permute-done.4.block = bf16[272,128]{1,0:T(8,128)(2,1)S(1)} collective-permute-done((bf16[272,128]{1,0:T(8,128)(2,1)S(1)}, bf16[272,128]{1,0:T(8,128)(2,1)S(1)}, u32[]{:S(2)}, u32[]{:S(2)}) %collective-permute-start.4) | collective-permute-done | bytes 69664 | tf_op jit(solution)/shard_map/ppermute | solution.py:423
  11.2 2.0 %collective-permute-done.5.block = bf16[272,128]{1,0:T(8,128)(2,1)S(1)} collective-permute-done((bf16[272,128]{1,0:T(8,128)(2,1)S(1)}, bf16[272,128]{1,0:T(8,128)(2,1)S(1)}, u32[]{:S(2)}, u32[]{:S(2)}) %collective-permute-start.5) | collective-permute-done | bytes 69664 | tf_op jit(solution)/shard_map/ppermute | solution.py:423
  13.2 0.7 %collective-permute-done.3.block = bf16[272,128]{1,0:T(8,128)(2,1)S(1)} collective-permute-done((bf16[272,128]{1,0:T(8,128)(2,1)S(1)}, bf16[272,128]{1,0:T(8,128)(2,1)S(1)}, u32[]{:S(2)}, u32[]{:S(2)}) %collective-permute-start.3) | collective-permute-done | bytes 69664 | tf_op jit(solution)/shard_map/ppermute | solution.py:423
  14.0 1.6 %collective-permute-start.6 = (bf16[64,128]{1,0:T(8,128)(2,1)S(1)}, bf16[64,128]{1,0:T(8,128)(2,1)S(1)}, u32[]{:S(2)}, u32[]{:S(2)}) collective-permute-start(bf16[64,128]{1,0:T(8,128)(2,1)S(1)} %get-tuple-element.94), channel_id=1, source_target_pairs={{0,1},{1,0},{2,3},{3,2},{4,5},{5,4},{6,7},{7,6},{8,9},{9,8},{10,11... | collective-permute-start | bytes 49160 | tf_op jit(solution)/shard_map/ppermute | solution.py:414
  15.5 0.8 %collective-permute-done.6 = bf16[64,128]{1,0:T(8,128)(2,1)S(1)} collective-permute-done((bf16[64,128]{1,0:T(8,128)(2,1)S(1)}, bf16[64,128]{1,0:T(8,128)(2,1)S(1)}, u32[]{:S(2)}, u32[]{:S(2)}) %collective-permute-start.6) | collective-permute-done | bytes 16416 | tf_op jit(solution)/shard_map/ppermute | solution.py:414
  16.4 0.6 %broadcast_select_fusion = bf16[64,128]{1,0:T(8,128)(2,1)} fusion(bf16[64,128]{1,0:T(8,128)(2,1)S(1)} %shard_map.98, bf16[64,128]{1,0:T(8,128)(2,1)S(1)} %collective-permute-done.6, pred[]{:T(512)S(6)} %eq.5), kind=kLoop, calls=%fused_computation.1 | loop fusion | flops 8192 | bytes 49153 | tf_op jit(solution)/shard_map/jit(_where)/select_n | solution.py:452
  (9 shorter events, 0.0 us)
Async XLA Ops:
  0.0 0.7 %copy-start = (s32[2,32]{1,0:T(2,128)S(1)}, s32[2,32]{1,0:T(2,128)}, u32[]{:S(2)}) copy-start(s32[2,32]{1,0:T(2,128)} %refs_1_.2) | copy-start | bytes 772
  0.0 2.0 %collective-permute-start = (bf16[64,128]{1,0:T(8,128)(2,1)}, bf16[64,128]{1,0:T(8,128)(2,1)S(1)}, u32[]{:S(2)}, u32[]{:S(2)}) collective-permute-start(bf16[64,128]{1,0:T(8,128)(2,1)} %bitcast.2), channel_id=1, source_target_pairs={{0,1},{1,0},{2,3},{3,2},{4,5},{5,4},{6,7},{7,6},{8,9},{9,8},{10,11... | collective-permute-start | bytes 49160 | tf_op jit(solution)/shard_map/ppermute | solution.py:414
  0.7 1.3 %collective-permute-start.1 = (s32[2,32]{1,0:T(2,128)S(1)}, s32[2,32]{1,0:T(2,128)S(1)}, u32[]{:S(2)}, u32[]{:S(2)}) collective-permute-start(s32[2,32]{1,0:T(2,128)S(1)} %copy-done), channel_id=1, source_target_pairs={{0,1},{1,0},{2,3},{3,2},{4,5},{5,4},{6,7},{7,6},{8,9},{9,8},{10,11... | collective-permute-start | bytes 776 | tf_op jit(solution)/shard_map/ppermute | solution.py:414
  2.0 4.8 %collective-permute-start.2 = (bf16[144,128]{1,0:T(8,128)(2,1)S(1)}, bf16[144,128]{1,0:T(8,128)(2,1)S(1)}, u32[]{:S(2)}, u32[]{:S(2)}) collective-permute-start(bf16[144,128]{1,0:T(8,128)(2,1)S(1)} %shard_map.92), channel_id=1, source_target_pairs={{0,2},{1,9},{2,0},{3,11},{4,6},{5,13},{6,4},{7,15},{8,10},{9,1},{1... | collective-permute-start | bytes 110600 | tf_op jit(solution)/shard_map/ppermute | solution.py:423
  6.8 4.4 %collective-permute-start.4 = (bf16[272,128]{1,0:T(8,128)(2,1)S(1)}, bf16[272,128]{1,0:T(8,128)(2,1)S(1)}, u32[]{:S(2)}, u32[]{:S(2)}) collective-permute-start(bf16[272,128]{1,0:T(8,128)(2,1)S(1)} %pad_maximum_fusion.block), channel_id=1, source_target_pairs={{0,16},{1,3},{2,18},{3,1},{4,20},{5,7},{6,22},{7,5},{8,24},{9,11},... | collective-permute-start | bytes 208904 | tf_op jit(solution)/shard_map/ppermute | solution.py:423
  8.9 4.3 %collective-permute-start.5 = (bf16[272,128]{1,0:T(8,128)(2,1)S(1)}, bf16[272,128]{1,0:T(8,128)(2,1)S(1)}, u32[]{:S(2)}, u32[]{:S(2)}) collective-permute-start(bf16[272,128]{1,0:T(8,128)(2,1)S(1)} %pad_maximum_fusion.block), channel_id=1, source_target_pairs={{0,16},{1,7},{2,18},{3,5},{4,20},{5,3},{6,22},{7,1},{8,24},{9,15},... | collective-permute-start | bytes 208904 | tf_op jit(solution)/shard_map/ppermute | solution.py:423
  9.0 5.0 %collective-permute-start.3 = (bf16[272,128]{1,0:T(8,128)(2,1)S(1)}, bf16[272,128]{1,0:T(8,128)(2,1)S(1)}, u32[]{:S(2)}, u32[]{:S(2)}) collective-permute-start(bf16[272,128]{1,0:T(8,128)(2,1)S(1)} %pad_maximum_fusion.block), channel_id=1, source_target_pairs={{0,16},{1,5},{2,18},{3,7},{4,20},{5,1},{6,22},{7,3},{8,24},{9,13},... | collective-permute-start | bytes 208904 | tf_op jit(solution)/shard_map/ppermute | solution.py:423
  14.0 2.4 %collective-permute-start.6 = (bf16[64,128]{1,0:T(8,128)(2,1)S(1)}, bf16[64,128]{1,0:T(8,128)(2,1)S(1)}, u32[]{:S(2)}, u32[]{:S(2)}) collective-permute-start(bf16[64,128]{1,0:T(8,128)(2,1)S(1)} %get-tuple-element.94), channel_id=1, source_target_pairs={{0,1},{1,0},{2,3},{3,2},{4,5},{5,4},{6,7},{7,6},{8,9},{9,8},{10,11... | collective-permute-start | bytes 49160 | tf_op jit(solution)/shard_map/ppermute | solution.py:414

commit v11 on v10

--- a/solution.py
+++ b/solution.py
@@ -177,7 +177,7 @@
                 yield n * self.group + slot * self.per, me ^ (step ^ place)
 
     def pairs(self, n):
-        return [(n, q) for q in range(n + 1)] + [(p, n) for p in range(n)]
+        return [(p, n) for p in range(n)] + [(n, q) for q in range(n + 1)]
 
 
 def prepare(lay, n, block, gain, proj, gate_weight, proj_bias, gate_bias, outs, scratch):

time: 17.2 us -> 17.2 us (level)
  no operation moved by 1% of the time
where the time goes in v11:
time: 17.2 us; the launch traced here: 17 us
  starting transfers between devices  9.41 us (55%)
  waiting for transfers between devices  4.61 us (27%)
  Pallas kernels  2.07 us (12%)
  other arithmetic  0.62 us (4%)
  local copies, waits for them, and re-layouts  0.23 us (1%)
    ppermute x4, starting transfers between devices, odd_swap(): return lax.ppermute(values, ('groups', 'row'), pairs)  6.93 us
    ppermute x4, waiting for transfers between devices, odd_swap(): return lax.ppermute(values, ('groups', 'row'), pairs)  3.69 us
    ppermute x3, starting transfers between devices, swap(): return lax.ppermute(values, 'row', [(i, i ^ step) for i in range(n_row)])  2.49 us
    pallas_call x1, Pallas kernels, load(): pl.pallas_call(kernel, out_shape=[jax.ShapeDtypeStruct(*shape) for shape...  1.25 us
    ppermute x3, waiting for transfers between devices, swap(): return lax.ppermute(values, 'row', [(i, i ^ step) for i in range(n_row)])  0.92 us
    pallas_call x1, Pallas kernels, fetch(): pl.pallas_call(functools.partial(fetch_kernel, count), out_shape=[jax.Sha...  0.74 us
    select_n x1, other arithmetic, gathered(): out = jnp.where(me % 2 == 1, odd, swap(even, 1, n_row))  0.61 us
  transfers between devices with their start and end apart: 7, of which 6 were waited for; matrix products, arithmetic and copies ran while one was open for 0% of the time, Pallas kernels for 12%

profile of v11, /device:TPU:0, one launch (start us, length us, event | category | flops | bytes accessed | tf_op | source)
XLA Modules:
  0.0 17.0 jit_solution(16112707699206119131)
XLA Ops:
  0.0 0.0 copy-start
  0.0 0.5 %collective-permute-start = (bf16[64,128]{1,0:T(8,128)(2,1)}, bf16[64,128]{1,0:T(8,128)(2,1)S(1)}, u32[]{:S(2)}, u32[]{:S(2)}) collective-permute-start(bf16[64,128]{1,0:T(8,128)(2,1)} %bitcast.2), channel_id=1, source_target_pairs={{0,1},{1,0},{2,3},{3,2},{4,5},{5,4},{6,7},{7,6},{8,9},{9,8},{10,11... | collective-permute-start | bytes 49160 | tf_op jit(solution)/shard_map/ppermute | solution.py:414
  0.5 0.2 %copy-done = s32[2,32]{1,0:T(2,128)S(1)} copy-done((s32[2,32]{1,0:T(2,128)S(1)}, s32[2,32]{1,0:T(2,128)}, u32[]{:S(2)}) %copy-start) | copy-done | bytes 280
  0.7 0.5 %collective-permute-start.1 = (s32[2,32]{1,0:T(2,128)S(1)}, s32[2,32]{1,0:T(2,128)S(1)}, u32[]{:S(2)}, u32[]{:S(2)}) collective-permute-start(s32[2,32]{1,0:T(2,128)S(1)} %copy-done), channel_id=1, source_target_pairs={{0,1},{1,0},{2,3},{3,2},{4,5},{5,4},{6,7},{7,6},{8,9},{9,8},{10,11... | collective-permute-start | bytes 776 | tf_op jit(solution)/shard_map/ppermute | solution.py:414
  1.1 0.7 %shard_map.91 = (bf16[64,128]{1,0:T(8,128)(2,1)S(1)}, s32[2,32]{1,0:T(2,128)S(1)}) custom-call(bf16[64,128]{1,0:T(8,128)(2,1)} %bitcast.3, s32[2,32]{1,0:T(2,128)} %refs_1_.2), custom_call_target="tpu_custom_call" | custom-call | tf_op jit(solution)/shard_map/pallas_call | solution.py:101
  1.9 0.1 collective-permute-done.1.other_mask
  2.0 0.0 collective-permute-done.other
  2.0 0.1 shard_map.92
  2.0 2.8 %collective-permute-start.2 = (bf16[144,128]{1,0:T(8,128)(2,1)S(1)}, bf16[144,128]{1,0:T(8,128)(2,1)S(1)}, u32[]{:S(2)}, u32[]{:S(2)}) collective-permute-start(bf16[144,128]{1,0:T(8,128)(2,1)S(1)} %shard_map.92), channel_id=1, source_target_pairs={{0,2},{1,9},{2,0},{3,11},{4,6},{5,13},{6,4},{7,15},{8,10},{9,1},{1... | collective-permute-start | bytes 110600 | tf_op jit(solution)/shard_map/ppermute | solution.py:423
  4.9 1.2 %shard_map.93 = (f32[2,128]{1,0:T(2,128)S(1)}, f32[2,128]{1,0:T(2,128)S(1)}, bf16[2,128,512]{2,1,0:T(8,128)(2,1)S(1)}, bf16[2,128,128]{2,1,0:T(8,128)(2,1)S(1)},...) custom-call(f32[2,128]{1,0:T(2,128)} %refs_0_.1, ...), custom_call_target="tpu_custom_call" | custom-call | tf_op jit(solution)/shard_map/pallas_call | solution.py:152
  6.2 0.7 %collective-permute-done.2 = bf16[144,128]{1,0:T(8,128)(2,1)S(1)} collective-permute-done((bf16[144,128]{1,0:T(8,128)(2,1)S(1)}, bf16[144,128]{1,0:T(8,128)(2,1)S(1)}, u32[]{:S(2)}, u32[]{:S(2)}) %collective-permute-start.2) | collective-permute-done | bytes 36896 | tf_op jit(solution)/shard_map/ppermute | solution.py:423
  6.8 2.1 %collective-permute-start.4 = (bf16[272,128]{1,0:T(8,128)(2,1)S(1)}, bf16[272,128]{1,0:T(8,128)(2,1)S(1)}, u32[]{:S(2)}, u32[]{:S(2)}) collective-permute-start(bf16[272,128]{1,0:T(8,128)(2,1)S(1)} %pad_maximum_fusion.block), channel_id=1, source_target_pairs={{0,16},{1,3},{2,18},{3,1},{4,20},{5,7},{6,22},{7,5},{8,24},{9,11},... | collective-permute-start | bytes 208904 | tf_op jit(solution)/shard_map/ppermute | solution.py:423
  8.9 0.1 collective-permute-start.5
  9.0 1.9 %collective-permute-start.3 = (bf16[272,128]{1,0:T(8,128)(2,1)S(1)}, bf16[272,128]{1,0:T(8,128)(2,1)S(1)}, u32[]{:S(2)}, u32[]{:S(2)}) collective-permute-start(bf16[272,128]{1,0:T(8,128)(2,1)S(1)} %pad_maximum_fusion.block), channel_id=1, source_target_pairs={{0,16},{1,5},{2,18},{3,7},{4,20},{5,1},{6,22},{7,3},{8,24},{9,13},... | collective-permute-start | bytes 208904 | tf_op jit(solution)/shard_map/ppermute | solution.py:423
  10.9 0.3 %collective-permute-done.4.block = bf16[272,128]{1,0:T(8,128)(2,1)S(1)} collective-permute-done((bf16[272,128]{1,0:T(8,128)(2,1)S(1)}, bf16[272,128]{1,0:T(8,128)(2,1)S(1)}, u32[]{:S(2)}, u32[]{:S(2)}) %collective-permute-start.4) | collective-permute-done | bytes 69664 | tf_op jit(solution)/shard_map/ppermute | solution.py:423
  11.2 2.0 %collective-permute-done.5.block = bf16[272,128]{1,0:T(8,128)(2,1)S(1)} collective-permute-done((bf16[272,128]{1,0:T(8,128)(2,1)S(1)}, bf16[272,128]{1,0:T(8,128)(2,1)S(1)}, u32[]{:S(2)}, u32[]{:S(2)}) %collective-permute-start.5) | collective-permute-done | bytes 69664 | tf_op jit(solution)/shard_map/ppermute | solution.py:423
  13.2 0.7 %collective-permute-done.3.block = bf16[272,128]{1,0:T(8,128)(2,1)S(1)} collective-permute-done((bf16[272,128]{1,0:T(8,128)(2,1)S(1)}, bf16[272,128]{1,0:T(8,128)(2,1)S(1)}, u32[]{:S(2)}, u32[]{:S(2)}) %collective-permute-start.3) | collective-permute-done | bytes 69664 | tf_op jit(solution)/shard_map/ppermute | solution.py:423
  14.0 1.6 %collective-permute-start.6 = (bf16[64,128]{1,0:T(8,128)(2,1)S(1)}, bf16[64,128]{1,0:T(8,128)(2,1)S(1)}, u32[]{:S(2)}, u32[]{:S(2)}) collective-permute-start(bf16[64,128]{1,0:T(8,128)(2,1)S(1)} %get-tuple-element.94), channel_id=1, source_target_pairs={{0,1},{1,0},{2,3},{3,2},{4,5},{5,4},{6,7},{7,6},{8,9},{9,8},{10,11... | collective-permute-start | bytes 49160 | tf_op jit(solution)/shard_map/ppermute | solution.py:414
  15.5 0.8 %collective-permute-done.6 = bf16[64,128]{1,0:T(8,128)(2,1)S(1)} collective-permute-done((bf16[64,128]{1,0:T(8,128)(2,1)S(1)}, bf16[64,128]{1,0:T(8,128)(2,1)S(1)}, u32[]{:S(2)}, u32[]{:S(2)}) %collective-permute-start.6) | collective-permute-done | bytes 16416 | tf_op jit(solution)/shard_map/ppermute | solution.py:414
  16.4 0.6 %broadcast_select_fusion = bf16[64,128]{1,0:T(8,128)(2,1)} fusion(bf16[64,128]{1,0:T(8,128)(2,1)S(1)} %shard_map.98, bf16[64,128]{1,0:T(8,128)(2,1)S(1)} %collective-permute-done.6, pred[]{:T(512)S(6)} %eq.5), kind=kLoop, calls=%fused_computation.1 | loop fusion | flops 8192 | bytes 49153 | tf_op jit(solution)/shard_map/jit(_where)/select_n | solution.py:452
  (9 shorter events, 0.0 us)
Async XLA Ops:
  0.0 0.7 %copy-start = (s32[2,32]{1,0:T(2,128)S(1)}, s32[2,32]{1,0:T(2,128)}, u32[]{:S(2)}) copy-start(s32[2,32]{1,0:T(2,128)} %refs_1_.2) | copy-start | bytes 772
  0.0 2.0 %collective-permute-start = (bf16[64,128]{1,0:T(8,128)(2,1)}, bf16[64,128]{1,0:T(8,128)(2,1)S(1)}, u32[]{:S(2)}, u32[]{:S(2)}) collective-permute-start(bf16[64,128]{1,0:T(8,128)(2,1)} %bitcast.2), channel_id=1, source_target_pairs={{0,1},{1,0},{2,3},{3,2},{4,5},{5,4},{6,7},{7,6},{8,9},{9,8},{10,11... | collective-permute-start | bytes 49160 | tf_op jit(solution)/shard_map/ppermute | solution.py:414
  0.7 1.3 %collective-permute-start.1 = (s32[2,32]{1,0:T(2,128)S(1)}, s32[2,32]{1,0:T(2,128)S(1)}, u32[]{:S(2)}, u32[]{:S(2)}) collective-permute-start(s32[2,32]{1,0:T(2,128)S(1)} %copy-done), channel_id=1, source_target_pairs={{0,1},{1,0},{2,3},{3,2},{4,5},{5,4},{6,7},{7,6},{8,9},{9,8},{10,11... | collective-permute-start | bytes 776 | tf_op jit(solution)/shard_map/ppermute | solution.py:414
  2.0 4.8 %collective-permute-start.2 = (bf16[144,128]{1,0:T(8,128)(2,1)S(1)}, bf16[144,128]{1,0:T(8,128)(2,1)S(1)}, u32[]{:S(2)}, u32[]{:S(2)}) collective-permute-start(bf16[144,128]{1,0:T(8,128)(2,1)S(1)} %shard_map.92), channel_id=1, source_target_pairs={{0,2},{1,9},{2,0},{3,11},{4,6},{5,13},{6,4},{7,15},{8,10},{9,1},{1... | collective-permute-start | bytes 110600 | tf_op jit(solution)/shard_map/ppermute | solution.py:423
  6.8 4.4 %collective-permute-start.4 = (bf16[272,128]{1,0:T(8,128)(2,1)S(1)}, bf16[272,128]{1,0:T(8,128)(2,1)S(1)}, u32[]{:S(2)}, u32[]{:S(2)}) collective-permute-start(bf16[272,128]{1,0:T(8,128)(2,1)S(1)} %pad_maximum_fusion.block), channel_id=1, source_target_pairs={{0,16},{1,3},{2,18},{3,1},{4,20},{5,7},{6,22},{7,5},{8,24},{9,11},... | collective-permute-start | bytes 208904 | tf_op jit(solution)/shard_map/ppermute | solution.py:423
  8.9 4.3 %collective-permute-start.5 = (bf16[272,128]{1,0:T(8,128)(2,1)S(1)}, bf16[272,128]{1,0:T(8,128)(2,1)S(1)}, u32[]{:S(2)}, u32[]{:S(2)}) collective-permute-start(bf16[272,128]{1,0:T(8,128)(2,1)S(1)} %pad_maximum_fusion.block), channel_id=1, source_target_pairs={{0,16},{1,7},{2,18},{3,5},{4,20},{5,3},{6,22},{7,1},{8,24},{9,15},... | collective-permute-start | bytes 208904 | tf_op jit(solution)/shard_map/ppermute | solution.py:423
  9.0 5.0 %collective-permute-start.3 = (bf16[272,128]{1,0:T(8,128)(2,1)S(1)}, bf16[272,128]{1,0:T(8,128)(2,1)S(1)}, u32[]{:S(2)}, u32[]{:S(2)}) collective-permute-start(bf16[272,128]{1,0:T(8,128)(2,1)S(1)} %pad_maximum_fusion.block), channel_id=1, source_target_pairs={{0,16},{1,5},{2,18},{3,7},{4,20},{5,1},{6,22},{7,3},{8,24},{9,13},... | collective-permute-start | bytes 208904 | tf_op jit(solution)/shard_map/ppermute | solution.py:423
  14.0 2.4 %collective-permute-start.6 = (bf16[64,128]{1,0:T(8,128)(2,1)S(1)}, bf16[64,128]{1,0:T(8,128)(2,1)S(1)}, u32[]{:S(2)}, u32[]{:S(2)}) collective-permute-start(bf16[64,128]{1,0:T(8,128)(2,1)S(1)} %get-tuple-element.94), channel_id=1, source_target_pairs={{0,1},{1,0},{2,3},{3,2},{4,5},{5,4},{6,7},{7,6},{8,9},{9,8},{10,11... | collective-permute-start | bytes 49160 | tf_op jit(solution)/shard_map/ppermute | solution.py:414
